TPU v7x, 32 devices: a whole 2x2x4 slice. The times are simulated.
32 devices in a mesh: img: 4 (over y, x), sp: 8 (over z, core).
Axes of the slice: x: 2, y: 2, z: 4, core: 2. Of those that a mesh axis runs over, the one named last changes fastest.
Arguments:
- tokens: bfloat16 [4, 7168, 2240], P('img', 'sp'), may hold values from -12 to 12
- queries: bfloat16 [4, 7168, 1120], P('img', 'sp'), may hold values from -6 to 6
- w_key: bfloat16 [2240, 1120], P('img'), may hold values from -0.125 to 0.125
- w_value: bfloat16 [2240, 1120], P('img'), may hold values from -0.125 to 0.125
- cotangent: bfloat16 [4, 7168, 1120], P('img', 'sp'), may hold values from -6 to 6
Outputs:
- attended: bfloat16 [4, 7168, 1120], P('img', 'sp')
- d_tokens: bfloat16 [4, 7168, 2240], P('img', 'sp')
- d_queries: bfloat16 [4, 7168, 1120], P('img', 'sp')
- d_w_key: float32 [2240, 1120], P('img')
- d_w_value: float32 [2240, 1120], P('img')
All inputs are finite; a program needn't handle non-finite values.
Results may differ from a plain program's by a relative error of at most 0.006.
Values may be sent and summed in bfloat16 or wider, within the bound.
No kernel may reach another device: no remote copies, remote signals or barrier semaphores. Data moves between devices by JAX's collectives and lax.ppermute only.
A program may use at most 128 MiB of HBM per device.

v0:
```python
import jax
import jax.numpy as jnp
from jax import lax
from jax.sharding import PartitionSpec as P

HD = 32


EPS_DEN = 1e-06


def body(tokens, queries, w_key, w_value, cotangent):
    high = lax.Precision.HIGHEST
    tok_rows = tokens[0]
    count = tok_rows.shape[0]
    width = w_key.shape[1]
    heads = width // HD
    tok_img = count * lax.axis_size("sp")
    images = lax.axis_size("img")
    gathered = (
        lax.all_gather(w_key, "img", axis=0, tiled=True),
        lax.all_gather(w_value, "img", axis=0, tiled=True),
    )
    key_pre = jnp.dot(tok_rows, gathered[0], preferred_element_type=jnp.float32)
    val_pre = jnp.dot(tok_rows, gathered[1], preferred_element_type=jnp.float32)
    key_feat = jnp.maximum(key_pre, 0.0).astype(jnp.bfloat16).reshape(count, heads, HD)
    val_feat = val_pre.astype(jnp.bfloat16).reshape(count, heads, HD)
    state_part = jnp.einsum("thi,thj->hij", key_feat, val_feat, preferred_element_type=jnp.float32)
    norm_part = jnp.sum(key_feat, axis=0, dtype=jnp.float32)
    kv_state, key_norm = lax.psum((state_part, norm_part), "sp")
    q_feat = jnp.maximum(queries[0].astype(jnp.float32), 0.0).reshape(count, heads, HD)
    numerator = jnp.einsum("thi,hij->thj", q_feat, kv_state, precision=high)
    denominator = jnp.einsum("thi,hi->th", q_feat, key_norm, precision=high) + EPS_DEN
    attn_f32 = numerator / denominator[..., None]
    attended = attn_f32.astype(jnp.bfloat16).reshape(1, count, width)
    cot_f32 = cotangent[0].astype(jnp.float32).reshape(count, heads, HD)
    d_num = cot_f32 / denominator[..., None]
    d_den = -jnp.sum(cot_f32 * attn_f32, axis=-1) / denominator
    d_feat = (
        jnp.einsum("thj,hij->thi", d_num, kv_state, precision=high)
        + d_den[..., None] * key_norm[None]
    )
    d_queries = jnp.where(q_feat > 0, d_feat, 0.0).astype(jnp.bfloat16).reshape(1, count, width)
    grad_part = jnp.einsum("thi,thj->hij", q_feat, d_num, precision=high)
    gnorm_part = jnp.einsum("th,thi->hi", d_den, q_feat, precision=high)
    grad_state, grad_norm = lax.psum((grad_part, gnorm_part), "sp")
    grad_state = grad_state * tok_img
    grad_norm = grad_norm * tok_img
    key_f32 = key_feat.astype(jnp.float32)
    d_key_f = (
        jnp.einsum("thj,hij->thi", val_feat.astype(jnp.float32), grad_state, precision=high)
        + grad_norm[None]
    )
    d_key = jnp.where(key_f32 > 0, d_key_f, 0.0).astype(jnp.bfloat16).reshape(count, width)
    d_value = (
        jnp.einsum("thi,hij->thj", key_f32, grad_state, precision=high)
        .astype(jnp.bfloat16)
        .reshape(count, width)
    )
    back_dims = (((1,), (1,)), ((), ()))
    d_flat = lax.dot_general(
        d_key, gathered[0], back_dims, preferred_element_type=jnp.float32
    ) + lax.dot_general(d_value, gathered[1], back_dims, preferred_element_type=jnp.float32)
    d_tokens = d_flat.astype(jnp.bfloat16).reshape(1, count, tok_rows.shape[1])
    d_both = jnp.concatenate([d_key, d_value], axis=1)
    tok_dims = (((0,), (0,)), ((), ()))
    grad_shard = lax.psum_scatter(
        lax.dot_general(tok_rows, d_both, tok_dims, preferred_element_type=jnp.float32),
        "img",
        scatter_dimension=0,
        tiled=True,
    )
    grad_whole = lax.psum(grad_shard, "sp")
    scale = 1.0 / jnp.sqrt(jnp.float32(images * tok_img))
    grad_whole = grad_whole * scale
    return (attended, d_tokens, d_queries, grad_whole[:, :width], grad_whole[:, width:])


def solution(mesh):
    in_specs = (
        P("img", "sp", None),
        P("img", "sp", None),
        P("img", None),
        P("img", None),
        P("img", "sp", None),
    )
    out_specs = (
        P("img", "sp", None),
        P("img", "sp", None),
        P("img", "sp", None),
        P("img", None),
        P("img", None),
    )
    return jax.shard_map(body, mesh=mesh, in_specs=in_specs, out_specs=out_specs, check_vma=False)
```

profile of v0, /device:TPU:0, one launch (start us, length us, event | category | flops | bytes accessed | tf_op | source)
XLA Modules:
  0.0 630.9 jit_solution(10363640057393242581)
XLA Ops:
  8.7 3.8 convert_maximum_fusion
  12.5 60.9 %all-gather.3.cloned.1.call-done = bf16[2240,1120]{1,0:T(8,128)(2,1)} async-done(((bf16[560,1120]{1,0:T(8,128)(2,1)}), bf16[2240,1120]{1,0:T(8,128)(2,1)}) %all-gather.3.cloned.1.call-update) | async-done | bytes 5017616 | tf_op jit(solution)/shard_map/all_gather | solution.py:21
  73.3 9.3 %convert_reduce_fusion = (f32[1120]{0:T(1024)S(1)}, bf16[896,1120]{0,1:T(8,128)(2,1)S(1)}) fusion(bf16[2240,1120]{1,0:T(8,128)(2,1)} %all-gather.3.cloned.1.call-done, bf16[1,896,2240]{1,2,0:T(8,128)(2,1)} %param.5), kind=kOutput, calls=%fused_computation.23 | convolution fusion | flops 4499782656 | bytes 11043200 | tf_op jit(solution)/shard_map/dot_general | solution.py:24
  82.7 28.7 %psum.36 = f32[35,32]{1,0:T(8,128)S(1)} all-reduce(f32[35,32]{1,0:T(8,128)S(1)} %reduce_sum.21), channel_id=1, replica_groups=mesh['img'=4,'sp'=8] {'sp'}, use_global_device_ids=true, to_apply=%region_2.0 | all-reduce | flops 1120 | bytes 8960 | tf_op jit(solution)/shard_map/psum | solution.py:30
  111.5 4.3 fusion.29
  115.8 20.2 %all-gather.5.cloned.1.call-done = bf16[2240,1120]{1,0:T(8,128)(2,1)} async-done(((bf16[560,1120]{1,0:T(8,128)(2,1)}), bf16[2240,1120]{1,0:T(8,128)(2,1)}) %all-gather.5.cloned.1.call-update) | async-done | bytes 5017616 | tf_op jit(solution)/shard_map/all_gather | solution.py:22
  136.0 9.4 %fusion.12 = bf16[896,1120]{0,1:T(8,128)(2,1)S(1)} fusion(bf16[2240,1120]{1,0:T(8,128)(2,1)} %all-gather.5.cloned.1.call-done, bf16[1,896,2240]{1,2,0:T(8,128)(2,1)} %param.5), kind=kOutput, calls=%fused_computation.24 | convolution fusion | flops 4496773120 | bytes 11038720 | tf_op jit(solution)/shard_map/dot_general | solution.py:25
  148.2 5.7 fusion.19
  154.0 59.3 %all-reduce.6.cloned.1.call-done = (f32[35,32,32]{2,1,0:T(8,128)}, f32[35,32,32]{2,1,0:T(8,128)}) async-done(((f32[35,32,32]{2,1,0:T(8,128)}, f32[35,32,32]{2,1,0:T(8,128)}), (f32[35,32,32]{2,1,0:T(8,128)}, f32[35,32,32]{2,1,0:T(8,128)})) %all-reduce.6.cloned.1.call-update) | async-done | bytes 286736 | tf_op jit(solution)/shard_map/psum | solution.py:30
  213.3 4.4 convolution_convert_fusion
  217.7 7.6 %fusion.1 = (f32[896,35]{0,1:T(8,128)S(1)}, bf16[896,35,32]{0,2,1:T(8,128)(2,1)}) fusion(bf16[896,35,32]{0,2,1:T(8,128)(2,1)} %bitcast.94, f32[896,35]{0,1:T(8,128)S(1)} %fusion.26, f32[35,32,32]{2,1,0:T(8,128)S(1)} %copy-done.11, f32[896,35,32]{0,2,1:T(8,128)S(1)} %bitcast.75), kind=kOutput, calls=%fused_computation.8 | convolution fusion | flops 390337920 | bytes 8422400 | tf_op jit(solution)/shard_map/thi,hij->thj/dot_general | solution.py:32
  225.3 3.9 fusion.27
  229.2 26.2 %psum.38 = f32[35,32]{1,0:T(8,128)S(1)} all-reduce(f32[35,32]{1,0:T(8,128)S(1)} %bitcast.88), channel_id=1, replica_groups=mesh['img'=4,'sp'=8] {'sp'}, use_global_device_ids=true, to_apply=%region_5.6 | all-reduce | flops 1120 | bytes 8960 | tf_op jit(solution)/shard_map/psum | solution.py:46
  255.4 3.8 fusion.7
  260.5 14.5 %convolution_bitcast_fusion = f32[2240,2240]{0,1:T(8,128)} fusion(bf16[896,1120]{0,1:T(8,128)(2,1)S(1)} %bitcast.84, bf16[896,1120]{0,1:T(8,128)(2,1)S(1)} %bitcast.82, bf16[1,896,2240]{1,2,0:T(8,128)(2,1)S(1)} %copy-done.9), kind=kOutput, calls=%fused_computation | convolution fusion | flops 8999567360 | bytes 28098560 | tf_op jit(solution)/shard_map/dot_general | solution.py:68
  275.0 21.8 %copy.28 = f32[2240,2240]{1,0:T(8,128)} copy(f32[2240,2240]{0,1:T(8,128)} %convolution_bitcast_fusion) | data formatting | bytes 40140800
  299.0 181.8 %reduce-scatter.4.cloned.1.call-done = f32[560,2240]{1,0:T(8,128)} async-done(((f32[2240,2240]{1,0:T(8,128)}), f32[560,2240]{1,0:T(8,128)}) %reduce-scatter.4.cloned.1.call-update) | async-done | bytes 5017616
  480.8 6.4 %copy.29 = f32[560,2240]{0,1:T(8,128)} copy(f32[560,2240]{1,0:T(8,128)} %reduce-scatter.4.cloned.1.call-done) | data formatting | bytes 10035200
  488.3 7.3 %fusion.6 = bf16[896,35,32]{0,2,1:T(8,128)(2,1)} fusion(pred[896,35,32]{0,2,1:T(32,128)(4,1)S(1)} %bitcast.86, f32[35,32]{1,0:T(8,128)S(1)} %psum.36, f32[896,35]{0,1:T(8,128)S(1)} %negate_divide_fusion, f32[35,32,32]{2,1,0:T(8,128)S(1)} %copy-done.12, bf16[896,35,32]{0,2,1:T(8,128)(2,1)} %bitcast.95, f32[896,35]{0,1:T(8,128)S(1)} %fusion.26), kind=kOutput, calls=%fused_computation.14 | convolution fusion | flops 391372800 | bytes 5416320 | tf_op jit(solution)/shard_map/thj,hij->thi/dot_general | solution.py:40
  495.7 6.0 fusion.36
  501.7 7.7 %fusion = bf16[1,896,2240]{1,2,0:T(8,128)(2,1)} fusion(f32[896,2240]{0,1:T(8,128)S(1)} %fusion.36, bf16[2240,1120]{1,0:T(8,128)(2,1)S(1)} %bitcast.93, bf16[896,1120]{0,1:T(8,128)(2,1)S(1)} %bitcast.85), kind=kOutput, calls=%fused_computation.6 | convolution fusion | flops 4499783680 | bytes 19066880 | tf_op jit(solution)/shard_map/dot_general | solution.py:63
  509.4 104.0 %all-reduce.4.cloned.1.call-done = f32[560,2240]{0,1:T(8,128)} async-done(((f32[560,2240]{0,1:T(8,128)}), f32[560,2240]{0,1:T(8,128)}) %all-reduce.4.cloned.1.call-update) | async-done | bytes 5017616 | tf_op jit(solution)/shard_map/psum | solution.py:73
  613.4 3.1 broadcast_multiply_fusion
  618.5 3.4 copy.21
  (55 shorter events, 13.3 us)
Async XLA Ops:
  7.2 66.2 %all-gather.3.cloned.1.call-start = ((), (), s32[]{:S(2)}) async-start(), calls=%async_computation.1 | async-start | bytes 6451200 | tf_op jit(solution)/shard_map/all_gather | solution.py:21
  7.9 128.1 %all-gather.5.cloned.1.call-start = ((), (), s32[]{:S(2)}) async-start(), calls=%async_computation.2 | async-start | bytes 6451200 | tf_op jit(solution)/shard_map/all_gather | solution.py:22
  8.6 204.6 %all-reduce.6.cloned.1.call-start = ((), (), s32[]{:S(2)}) async-start(), calls=%async_computation.5 | async-start | bytes 2293760 | tf_op jit(solution)/shard_map/psum | solution.py:30
  136.0 12.3 %copy-start.10 = (bf16[1,896,1120]{1,2,0:T(8,128)(2,1)S(1)}, bf16[1,896,1120]{1,2,0:T(8,128)(2,1)}, u32[]{:S(2)}) copy-start(bf16[1,896,1120]{1,2,0:T(8,128)(2,1)} %param.9) | copy-start | bytes 6021124
  145.3 1.3 copy-start.3
  145.3 2.9 copy-start
  154.0 326.9 %reduce-scatter.4.cloned.1.call-start = ((), (), s32[]{:S(2)}) async-start(), calls=%async_computation.4 | async-start | bytes 25804800
  213.3 4.4 copy-start.1
  213.3 4.4 copy-start.11
  225.3 30.1 %copy-start.4 = (f32[35,32,32]{2,1,0:T(8,128)S(1)}, f32[35,32,32]{2,1,0:T(8,128)}, u32[]{:S(2)}) copy-start(f32[35,32,32]{2,1,0:T(8,128)} %get-tuple-element.21) | copy-start | bytes 430084
  255.4 5.1 copy-start.7
  255.4 5.1 copy-start.9
  259.2 1.3 copy-start.5
  296.8 1.6 copy-start.2
  296.8 316.6 %all-reduce.4.cloned.1.call-start = ((), (), s32[]{:S(2)}) async-start(), calls=%async_computation.3 | async-start | bytes 11468800 | tf_op jit(solution)/shard_map/psum | solution.py:73
  487.3 1.1 copy-start.12
  487.3 8.4 %slice-start = ((s8[5160960]{0:T(1024)(128)(4,1)}), s8[966656]{0:T(1024)(128)(4,1)S(1)}, s32[]{:S(2)}) async-start(s8[5160960]{0:T(1024)(128)(4,1)} %bitcast.90), calls=%async_computation.6 | async-start | bytes 1933312
  488.3 7.4 %copy-start.6 = (bf16[896,35,32]{0,2,1:T(8,128)(2,1)S(1)}, bf16[896,35,32]{0,2,1:T(8,128)(2,1)}, u32[]{:S(2)}) copy-start(bf16[896,35,32]{0,2,1:T(8,128)(2,1)} %copy-done.5) | copy-start | bytes 6021124
  488.3 7.4 %slice-start.1 = ((s8[5160960]{0:T(1024)(128)(4,1)}), s8[4194304]{0:T(1024)(128)(4,1)S(1)}, s32[]{:S(2)}) async-start(s8[5160960]{0:T(1024)(128)(4,1)} %bitcast.90), calls=%async_computation.7 | async-start | bytes 8388608
  488.3 13.4 %slice-start.2 = ((s8[5160960]{0:T(1024)(128)(4,1)}), s8[4194304]{0:T(1024)(128)(4,1)S(1)}, s32[]{:S(2)}) async-start(s8[5160960]{0:T(1024)(128)(4,1)} %bitcast.92), calls=%async_computation.8 | async-start | bytes 8388608
  495.7 6.0 copy-start.8
  495.7 6.0 slice-start.3
Sparse Core Ops, SparseCore 0:
  9.8 63.4 all-gather.2
  75.2 60.7 all-gather.4
  154.1 59.1 all-reduce.5
  296.9 183.8 reduce-scatter.3
  487.4 125.9 all-reduce.3
where the time goes:
time: 637 us; the launch traced here: 631 us
  waiting for transfers between devices  428 us (67%)
  matrix products  85.5 us (13%)
  blocking collectives  54.9 us (9%)
  local copies, waits for them, and re-layouts  41 us (6%)
  between operations  14.2 us (2%)
  other arithmetic  7.59 us (1%)
    unnamed x6, waiting for transfers between devices  183 us
    psum x1, waiting for transfers between devices, body(): grad_whole = lax.psum(grad_shard, 'sp')  104 us
    all_gather x1, waiting for transfers between devices, body(): lax.all_gather(w_key, 'img', axis=0, tiled=True)  60.9 us
    psum x1, waiting for transfers between devices, body(): kv_state, key_norm = lax.psum((state_part, norm_part), 'sp')  59.3 us
    unnamed x38, local copies, waits for them, and re-layouts  39 us
    psum x1, blocking collectives, body(): kv_state, key_norm = lax.psum((state_part, norm_part), 'sp')  28.7 us
    psum x1, blocking collectives, body(): grad_state, grad_norm = lax.psum((grad_part, gnorm_part), 'sp')  26.2 us
    all_gather x1, waiting for transfers between devices, body(): lax.all_gather(w_value, 'img', axis=0, tiled=True)  20.2 us
  transfers between devices with their start and end apart: 5, of which 5 were waited for; matrix products, arithmetic and copies ran while one was open for 6% of the time, Pallas kernels for 0%

commit v1 on v0

v1 whole, which is shorter than its diff:
```python
import functools

import jax
import jax.numpy as jnp
from jax import lax
from jax.experimental import pallas as pl
from jax.experimental.pallas import tpu as pltpu
from jax.sharding import PartitionSpec as P

HD = 32
EPS_DEN = 1e-06
LANES = 256
STATE_ROWS = 40
BF, F32 = jnp.bfloat16, jnp.float32
VMEM_LIMIT = 48 * 1024 * 1024


def dot(a, b, ca, cb):
    return lax.dot_general(a, b, (((ca,), (cb,)), ((), ())), preferred_element_type=F32)


def tiles_of(width):
    return [(s, min(LANES, width - s)) for s in range(0, width, LANES)]


def same_head(w):
    row = lax.broadcasted_iota(jnp.int32, (w, w), 0) // HD
    col = lax.broadcasted_iota(jnp.int32, (w, w), 1) // HD
    return row == col


def fold(full, w):
    kept = jnp.where(same_head(w), full, 0.0)
    total = kept[0:HD]
    for at in range(HD, w, HD):
        total = total + kept[at : at + HD]
    return total


def unfold(rows, w):
    return jnp.where(same_head(w), jnp.concatenate([rows] * (w // HD), axis=0), 0.0)


def split(x):
    high = x.astype(BF)
    return high, (x - high.astype(F32)).astype(BF)


def params(**kw):
    return pltpu.CompilerParams(vmem_limit_bytes=VMEM_LIMIT, **kw)


def place_copies(scal, refs, places, bufs, sems):
    copies = []
    for n, (ref, (which, rel, off, shard)) in enumerate(zip(refs, places)):
        if rel is None:
            start = off
        else:
            start = pl.multiple_of((scal[0] ^ rel) * shard + off, 16)
        copies.append(
            pltpu.make_async_copy(ref, bufs[which].at[pl.ds(start, ref.shape[0]), :], sems.at[n])
        )
    return copies


def proj_kernel(places, width, scal, tok, *refs):
    pieces = refs[: len(places)]
    k_out, v_out, st_out, w_a, w_b, sems = refs[len(places) :]
    step = pl.program_id(0)

    @pl.when(step == 0)
    def _():
        copies = place_copies(scal, pieces, places, (w_a, w_b), sems)
        for c in copies:
            c.start()
        for c in copies:
            c.wait()
        st_out[...] = jnp.zeros_like(st_out)

    first = scal[1] == 0
    rows = tok[...]
    a = dot(rows, w_a[...], 1, 0)
    b = dot(rows, w_b[...], 1, 0)
    key = jnp.maximum(jnp.where(first, a, b), 0.0)
    val = jnp.where(first, b, a)
    k_out[...] = key.astype(BF)
    v_out[...] = val.astype(BF)
    for s, w in tiles_of(width):
        cols = slice(s, s + w)
        k, v = k_out[:, cols], v_out[:, cols]
        st_out[0:HD, cols] += fold(dot(v, k, 0, 0), w)
        st_out[HD : HD + 1, cols] += jnp.sum(k.astype(F32), axis=0, keepdims=True)


def project(scal, tok, pieces, places, width, tile):
    count, depth = tok.shape
    grid = count // tile
    return pl.pallas_call(
        functools.partial(proj_kernel, places, width),
        grid_spec=pltpu.PrefetchScalarGridSpec(
            num_scalar_prefetch=1,
            grid=(grid,),
            in_specs=[pl.BlockSpec((tile, depth), lambda i, s: (i, 0))]
            + [pl.BlockSpec(memory_space=pl.ANY)] * len(pieces),
            out_specs=[
                pl.BlockSpec((tile, width), lambda i, s: (i, 0)),
                pl.BlockSpec((tile, width), lambda i, s: (i, 0)),
                pl.BlockSpec((STATE_ROWS, width), lambda i, s: (0, 0)),
            ],
            scratch_shapes=[
                pltpu.VMEM((depth, width), BF),
                pltpu.VMEM((depth, width), BF),
                pltpu.SemaphoreType.DMA((len(pieces),)),
            ],
        ),
        out_shape=[
            jax.ShapeDtypeStruct((count, width), BF),
            jax.ShapeDtypeStruct((count, width), BF),
            jax.ShapeDtypeStruct((STATE_ROWS, width), F32),
        ],
        compiler_params=params(dimension_semantics=("arbitrary",)),
        cost_estimate=pl.CostEstimate(
            flops=4 * count * depth * width, bytes_accessed=2 * count * depth + 4 * depth * width, transcendentals=0
        ),
        name="project",
    )(scal, tok, *pieces)


def attend_kernel(off, width, n_prev, q_ref, g_ref, st, *refs):
    prev = refs[: 2 * n_prev]
    att_out, dq_out, gs_out, kv_hi, kv_lo, kn_hi, kn_lo = refs[2 * n_prev :]
    step = pl.program_id(0)
    tiles = tiles_of(width)

    @pl.when(step == 0)
    def _():
        gs_out[...] = jnp.zeros_like(gs_out)
        for n, (s, w) in enumerate(tiles):
            kv = unfold(st[0:HD, s : s + w], w)
            kn = unfold(jnp.broadcast_to(st[HD : HD + 1, s : s + w], (HD, w)), w)
            kv_hi[n, 0:w, 0:w], kv_lo[n, 0:w, 0:w] = split(kv)
            kn_hi[n, 0:w, 0:w], kn_lo[n, 0:w, 0:w] = split(kn)

    at = 0
    for n in range(n_prev):
        w = prev[2 * n].shape[1]
        att_out[:, at : at + w] = prev[2 * n][...]
        dq_out[:, at : at + w] = prev[2 * n + 1][...]
        at += w
    for n, (s, w) in enumerate(tiles):
        q = jnp.maximum(q_ref[:, off + s : off + s + w], 0)
        g = g_ref[:, off + s : off + s + w].astype(F32)
        h, l = kv_hi[n, 0:w, 0:w], kv_lo[n, 0:w, 0:w]
        num = dot(q, h, 1, 1) + dot(q, l, 1, 1)
        den = dot(q, kn_hi[n, 0:w, 0:w], 1, 1) + dot(q, kn_lo[n, 0:w, 0:w], 1, 1) + EPS_DEN
        inv = 1.0 / den
        attn = num * inv
        dn = g * inv
        ones = jnp.where(same_head(w), 1.0, 0.0).astype(BF)
        ga_hi, ga_lo = split(g * attn)
        dden = -(dot(ga_hi, ones, 1, 0) + dot(ga_lo, ones, 1, 0)) * inv
        dn_hi, dn_lo = split(dn)
        df = dot(dn_hi, h, 1, 0) + dot(dn_hi, l, 1, 0) + dot(dn_lo, h, 1, 0)
        df = df + dden * st[HD : HD + 1, s : s + w]
        q32 = q.astype(F32)
        att_out[:, at + s : at + s + w] = attn.astype(BF)
        dq_out[:, at + s : at + s + w] = jnp.where(q32 > 0, df, 0.0).astype(BF)
        gs_out[0:HD, s : s + w] += fold(dot(dn_hi, q, 0, 0) + dot(dn_lo, q, 0, 0), w)
        gs_out[HD : HD + 1, s : s + w] += jnp.sum(dden * q32, axis=0, keepdims=True)


def attend(queries, cotangent, state, off, width, prev, tile):
    count, full = queries.shape
    n_prev = len(prev) // 2
    tiles = len(tiles_of(width))
    wide = width + sum(p.shape[1] for p in prev[::2])
    row = lambda w: pl.BlockSpec((tile, w), lambda i: (i, 0))
    return pl.pallas_call(
        functools.partial(attend_kernel, off, width, n_prev),
        grid=(count // tile,),
        in_specs=[row(full), row(full), pl.BlockSpec((STATE_ROWS, width), lambda i: (0, 0))]
        + [row(p.shape[1]) for p in prev],
        out_specs=[row(wide), row(wide), pl.BlockSpec((STATE_ROWS, width), lambda i: (0, 0))],
        out_shape=[
            jax.ShapeDtypeStruct((count, wide), BF),
            jax.ShapeDtypeStruct((count, wide), BF),
            jax.ShapeDtypeStruct((STATE_ROWS, width), F32),
        ],
        scratch_shapes=[pltpu.VMEM((tiles, LANES, LANES), BF)] * 4,
        compiler_params=params(dimension_semantics=("arbitrary",)),
        cost_estimate=pl.CostEstimate(
            flops=24 * count * width * LANES, bytes_accessed=8 * count * full, transcendentals=0
        ),
        name="attend",
    )(queries, cotangent, state, *prev)


def feat_kernel(width, scale, scal, k_ref, v_ref, st, keep, send, gs_hi, gs_lo):
    tiles = tiles_of(width)

    @pl.when(pl.program_id(0) == 0)
    def _():
        for n, (s, w) in enumerate(tiles):
            gs = unfold(st[0:HD, s : s + w] * scale, w)
            gs_hi[n, 0:w, 0:w], gs_lo[n, 0:w, 0:w] = split(gs)

    first = scal[1] == 0
    for n, (s, w) in enumerate(tiles):
        cols = slice(s, s + w)
        k, v = k_ref[:, cols], v_ref[:, cols]
        h, l = gs_hi[n, 0:w, 0:w], gs_lo[n, 0:w, 0:w]
        dv = dot(k, h, 1, 1) + dot(k, l, 1, 1)
        dk = dot(v, h, 1, 0) + dot(v, l, 1, 0) + st[HD : HD + 1, cols] * scale
        dk = jnp.where(k.astype(F32) > 0, dk, 0.0)
        keep[:, cols] = jnp.where(first, dk, dv).astype(BF)
        send[:, cols] = jnp.where(first, dv, dk).astype(BF)


def feature_grads(scal, key, val, state, scale, tile):
    count, width = key.shape
    tiles = len(tiles_of(width))
    row = pl.BlockSpec((tile, width), lambda i, s: (i, 0))
    return pl.pallas_call(
        functools.partial(feat_kernel, width, scale),
        grid_spec=pltpu.PrefetchScalarGridSpec(
            num_scalar_prefetch=1,
            grid=(count // tile,),
            in_specs=[row, row, pl.BlockSpec((STATE_ROWS, width), lambda i, s: (0, 0))],
            out_specs=[row, row],
            scratch_shapes=[pltpu.VMEM((tiles, LANES, LANES), BF)] * 2,
        ),
        out_shape=[jax.ShapeDtypeStruct((count, width), BF)] * 2,
        compiler_params=params(dimension_semantics=("arbitrary",)),
        cost_estimate=pl.CostEstimate(
            flops=8 * count * width * LANES, bytes_accessed=8 * count * width, transcendentals=0
        ),
        name="feature_grads",
    )(scal, key, val, state)


def weight_kernel(cut, scal, t_own, t_other, d_own, d_other, send_a, send_b, keep_a, keep_b):
    step = pl.program_id(0)
    part = dot(t_own[...], d_own[...], 1, 0) + dot(t_other[...], d_other[...], 1, 0)
    a, b = part[:cut], part[cut:]

    @pl.when(step == 0)
    def _():
        send_a[1] = a.astype(BF)
        send_b[1] = b.astype(BF)

    @pl.when(step == 1)
    def _():
        send_b[0] = b.astype(BF)
        keep_a[1] = a

    @pl.when(step == 2)
    def _():
        send_a[0] = a.astype(BF)
        keep_b[1] = b

    @pl.when(step == 3)
    def _():
        keep_a[0] = a
        keep_b[0] = b


def weight_grads(scal, t_own, t_other, d_own, d_other, shard, cut):
    depth, count = t_own.shape
    width = d_own.shape[1]
    at = lambda i, s: ((3 - i) ^ s[0], 0)
    rows = pl.BlockSpec((shard, count), at)
    whole = pl.BlockSpec((count, width), lambda i, s: (0, 0))
    full = lambda r: pl.BlockSpec((2, r, width), lambda i, s: (0, 0, 0))
    rest = shard - cut
    return pl.pallas_call(
        functools.partial(weight_kernel, cut),
        grid_spec=pltpu.PrefetchScalarGridSpec(
            num_scalar_prefetch=1,
            grid=(4,),
            in_specs=[rows, rows, whole, whole],
            out_specs=[full(cut), full(rest), full(cut), full(rest)],
        ),
        out_shape=[
            jax.ShapeDtypeStruct((2, cut, width), BF),
            jax.ShapeDtypeStruct((2, rest, width), BF),
            jax.ShapeDtypeStruct((2, cut, width), F32),
            jax.ShapeDtypeStruct((2, rest, width), F32),
        ],
        compiler_params=params(dimension_semantics=("arbitrary",)),
        cost_estimate=pl.CostEstimate(
            flops=4 * count * depth * width, bytes_accessed=4 * count * depth + 6 * depth * width, transcendentals=0
        ),
        name="weight_grads",
    )(scal, t_own, t_other, d_own, d_other)


def input_kernel(plan, scal, *refs):
    n_d = 2 * len(plan)
    n_w = sum(len(places) for places, _ in plan)
    grads, pieces = refs[:n_d], refs[n_d : n_d + n_w]
    out = refs[n_d + n_w]
    bufs = refs[n_d + n_w + 1 : n_d + n_w + 1 + n_d]
    sems = refs[-1]

    @pl.when(pl.program_id(0) == 0)
    def _():
        copies, at = [], 0
        for n, (places, _) in enumerate(plan):
            here = pieces[at : at + len(places)]
            copies += place_copies(scal, here, places, bufs[2 * n : 2 * n + 2], sems.at[pl.ds(at, len(places))])
            at += len(places)
        for c in copies:
            c.start()
        for c in copies:
            c.wait()

    total = dot(grads[0][...], bufs[0][...], 1, 1)
    for n in range(1, n_d):
        total = total + dot(grads[n][...], bufs[n][...], 1, 1)
    out[...] = total.astype(BF)


def input_grads(scal, grads, pieces, plan, depth, tile):
    count = grads[0].shape[0]
    widths = [g.shape[1] for g in grads]
    return pl.pallas_call(
        functools.partial(input_kernel, plan),
        grid_spec=pltpu.PrefetchScalarGridSpec(
            num_scalar_prefetch=1,
            grid=(count // tile,),
            in_specs=[pl.BlockSpec((tile, w), lambda i, s: (i, 0)) for w in widths]
            + [pl.BlockSpec(memory_space=pl.ANY)] * len(pieces),
            out_specs=pl.BlockSpec((tile, depth), lambda i, s: (i, 0)),
            scratch_shapes=[pltpu.VMEM((depth, w), BF) for w in widths]
            + [pltpu.SemaphoreType.DMA((len(pieces),))],
        ),
        out_shape=jax.ShapeDtypeStruct((count, depth), BF),
        compiler_params=params(dimension_semantics=("arbitrary",)),
        cost_estimate=pl.CostEstimate(
            flops=2 * count * depth * sum(widths), bytes_accessed=2 * count * depth + 2 * depth * sum(widths), transcendentals=0
        ),
        name="input_grads",
    )(scal, *grads, *pieces)


def swap(x, axis, bit):
    n = lax.axis_size(axis)
    return lax.ppermute(x, axis, [(i, i ^ bit) for i in range(n)])


def cuts_of(width):
    first = min(512, width)
    return [(0, first), (first, width - first)] if first < width else [(0, width)]


def tile_of(count):
    return next(t for t in (224, 128, 64, 32, 16) if count % t == 0)


def body_exchange(tokens, queries, w_key, w_value, cotangent):
    tok, qs, cot = tokens[0], queries[0], cotangent[0]
    count, depth = tok.shape
    shard, full = w_key.shape
    tile = tile_of(count)
    img, spx = lax.axis_index("img"), lax.axis_index("sp")
    core = spx % 2
    first = core == 0
    scal = jnp.stack([img, core]).astype(jnp.int32)
    tok_img = count * lax.axis_size("sp")
    scale = 1.0 / (lax.axis_size("img") * tok_img) ** 0.5
    cut = shard // 2 // 16 * 16

    def sum_tiles(x):
        x = x + swap(x, "sp", 1)
        x = x + swap(x, "sp", 2)
        return x + swap(x, "sp", 4)

    tok_t = tok.T
    tok_t_other = swap(tok_t, "sp", 1)

    after = None
    gathered = []
    for off, width in cuts_of(full):
        wk, wv = w_key[:, off : off + width], w_value[:, off : off + width]
        mine, theirs = jnp.where(first, wk, wv), jnp.where(first, wv, wk)
        if after is not None:
            mine, _ = lax.optimization_barrier((mine, after))
        by_x, by_y = swap(mine, "img", 1), swap(mine, "img", 2)
        far_a = swap(by_y[:cut], "img", 1)
        far_b = swap(by_x[cut:], "img", 2)
        after = (by_x, by_y)
        got = [(mine, 0, 0), (by_x, 1, 0), (by_y, 2, 0), (far_a, 3, 0), (far_b, 3, cut)]
        places = [(0, rel, at, shard) for _, rel, at in got] + [(1, rel, at, shard) for _, rel, at in got]
        pieces = [p for p, _, _ in got] + [theirs] + [swap(p, "sp", 1) for p, _, _ in got[1:]]
        gathered.append((pieces, places))

    feats = []
    for (off, width), (pieces, places) in zip(cuts_of(full), gathered):
        key, val, state = project(scal, tok, pieces, places, width, tile)
        feats.append((key, val, sum_tiles(state)))

    prev, grads = [], []
    chunks = cuts_of(full)
    for n, ((off, width), (key, val, state)) in enumerate(zip(chunks, feats)):
        merge = prev if n == len(chunks) - 1 else []
        att, dq, gs = attend(qs, cot, state, off, width, merge, tile)
        prev += [att, dq]
        keep, send = feature_grads(scal, key, val, sum_tiles(gs), float(tok_img), tile)
        grads.append((keep, send))
    attended, d_queries = prev[-2:]

    shards = []
    for keep, send in grads:
        other = swap(send, "sp", 1)
        send_a, send_b, keep_a, keep_b = weight_grads(scal, tok_t, tok_t_other, keep, other, shard, cut)
        a = keep_a + swap(send_a, "img", 1).astype(F32)
        b = keep_b + swap(send_b, "img", 2).astype(F32)
        a0 = a[0] + swap(a[1].astype(BF), "img", 2).astype(F32)
        b0 = b[0] + swap(b[1].astype(BF), "img", 1).astype(F32)
        own = jnp.concatenate([a0, b0], axis=0)
        width = own.shape[1]
        z0, z1 = (spx // 2) % 2, (spx // 4) % 2
        halves = own.reshape(2, shard // 2, width)
        half = lax.dynamic_index_in_dim(halves, z0, 0, False)
        give = lax.dynamic_index_in_dim(halves, 1 - z0, 0, False)
        half = half + swap(give.astype(BF), "sp", 2).astype(F32)
        quarters = half.reshape(2, shard // 4, width)
        quarter = lax.dynamic_index_in_dim(quarters, z1, 0, False)
        give = lax.dynamic_index_in_dim(quarters, 1 - z1, 0, False)
        quarter = (quarter + swap(give.astype(BF), "sp", 4).astype(F32)) * scale
        quarter = quarter.astype(BF)
        back = swap(quarter, "sp", 4)
        low = z1 == 0
        half = jnp.concatenate([jnp.where(low, quarter, back), jnp.where(low, back, quarter)], axis=0)
        back = swap(half, "sp", 2)
        low = z0 == 0
        whole = jnp.concatenate([jnp.where(low, half, back), jnp.where(low, back, half)], axis=0)
        shards.append((whole, swap(whole, "sp", 1)))
    d_tokens = input_grads(
        scal,
        [g for pair in grads for g in pair],
        [p for pieces, _ in gathered for p in pieces],
        [(places, None) for _, places in gathered],
        depth,
        tile,
    )
    mine = jnp.concatenate([m for m, _ in shards], axis=1).astype(F32)
    theirs = jnp.concatenate([t for _, t in shards], axis=1).astype(F32)
    d_w_key = jnp.where(first, mine, theirs)
    d_w_value = jnp.where(first, theirs, mine)
    return attended[None], d_tokens[None], d_queries[None], d_w_key, d_w_value


def body_general(tokens, queries, w_key, w_value, cotangent):
    tok, qs, cot = tokens[0], queries[0], cotangent[0]
    count, depth = tok.shape
    full = w_key.shape[1]
    tile = tile_of(count)
    scal = jnp.zeros((2,), jnp.int32)
    tok_img = count * lax.axis_size("sp")
    scale = 1.0 / (lax.axis_size("img") * tok_img) ** 0.5
    pieces = [lax.all_gather(w, "img", axis=0, tiled=True) for w in (w_key, w_value)]
    places = [(0, None, 0, depth), (1, None, 0, depth)]
    key, val, state = project(scal, tok, pieces, places, full, tile)
    attended, d_queries, gs = attend(qs, cot, lax.psum(state, "sp"), 0, full, [], tile)
    d_key, d_value = feature_grads(scal, key, val, lax.psum(gs, "sp"), float(tok_img), tile)
    d_tokens = input_grads(scal, [d_key, d_value], pieces, [(places, None)], depth, tile)
    out = []
    for d in (d_key, d_value):
        part = lax.psum_scatter(dot(tok, d, 0, 0), "img", scatter_dimension=0, tiled=True)
        out.append(lax.psum(part, "sp") * scale)
    return attended[None], d_tokens[None], d_queries[None], *out


def solution(mesh):
    in_specs = (
        P("img", "sp", None),
        P("img", "sp", None),
        P("img", None),
        P("img", None),
        P("img", "sp", None),
    )
    out_specs = (
        P("img", "sp", None),
        P("img", "sp", None),
        P("img", "sp", None),
        P("img", None),
        P("img", None),
    )
    cubes = mesh.shape["img"] == 4 and mesh.shape["sp"] == 8
    body = body_exchange if cubes else body_general
    return jax.shard_map(body, mesh=mesh, in_specs=in_specs, out_specs=out_specs, check_vma=False)
```

time: 637 us -> 289 us (0.45)
  waiting for transfers between devices: 428 us -> 110 us
  matrix products: 85.5 us -> 0 us
  Pallas kernels: 0 us -> 82.4 us
  blocking collectives: 54.9 us -> 0 us
  starting transfers between devices: 0.2 us -> 41 us
  between operations: 14.2 us -> 1.41 us
    unnamed x6 -> x0, waiting for transfers between devices: 183 us -> none
    psum x2 -> x0, waiting for transfers between devices: 163 us -> none  [the longest x1 104 us: body(): grad_whole = lax.psum(grad_shard, 'sp')]
    ppermute x0 -> x49, waiting for transfers between devices: none -> 110 us  [swap(): return lax.ppermute(x, axis, [(i, i ^ bit) for i in range(n)])]
    dot_general x13 -> x0, matrix products: 85.5 us -> none  [the longest x1 14.5 us: body(): lax.dot_general(tok_rows, d_both, tok_dims, preferred_element_type=jnp.fl...]
    pallas_call x0 -> x9, Pallas kernels: none -> 82.4 us  [the longest x2 23.8 us: project(): pl.pallas_call(functools.partial(proj_kernel, places, width), grid_spec=p...]
    all_gather x2 -> x0, waiting for transfers between devices: 81 us -> none  [the longest x1 60.9 us: body(): lax.all_gather(w_key, 'img', axis=0, tiled=True)]
    psum x2 -> x0, blocking collectives: 54.9 us -> none  [the longest x1 28.7 us: body(): kv_state, key_norm = lax.psum((state_part, norm_part), 'sp')]
    ppermute x0 -> x49, starting transfers between devices: none -> 41 us  [swap(): return lax.ppermute(x, axis, [(i, i ^ bit) for i in range(n)])]
  transfers between devices with their start and end apart: 5 -> 49, of which waited for: 5 -> 23; matrix products, arithmetic and copies ran while one was open for 6% -> 15% of each run, Pallas kernels for 0% -> 29%
where the time goes in v1:
time: 289 us; the launch traced here: 288 us
  waiting for transfers between devices  110 us (38%)
  Pallas kernels  82.4 us (29%)
  local copies, waits for them, and re-layouts  41.8 us (14%)
  starting transfers between devices  41 us (14%)
  other arithmetic  11.5 us (4%)
    ppermute x49, waiting for transfers between devices, swap(): return lax.ppermute(x, axis, [(i, i ^ bit) for i in range(n)])  110 us
    ppermute x49, starting transfers between devices, swap(): return lax.ppermute(x, axis, [(i, i ^ bit) for i in range(n)])  41 us
    unnamed x73, local copies, waits for them, and re-layouts  27.4 us
    pallas_call x2, Pallas kernels, project(): pl.pallas_call(functools.partial(proj_kernel, places, width), grid_spec=p...  23.8 us
    pallas_call x2, Pallas kernels, weight_grads(): pl.pallas_call(functools.partial(weight_kernel, cut), grid_spec=pltpu.Pre...  20.3 us
    pallas_call x1, Pallas kernels, input_grads(): pl.pallas_call(functools.partial(input_kernel, plan), grid_spec=pltpu.Pre...  19.5 us
    pallas_call x2, Pallas kernels, attend(): pl.pallas_call(functools.partial(attend_kernel, off, width, n_prev), grid...  12.7 us
    squeeze x1, local copies, waits for them, and re-layouts, body_exchange(): tok, qs, cot = (tokens[0], queries[0], cotangent[0])  6.41 us
  transfers between devices with their start and end apart: 49, of which 23 were waited for; matrix products, arithmetic and copies ran while one was open for 15% of the time, Pallas kernels for 29%

profile of v1, /device:TPU:0, one launch (start us, length us, event | category | flops | bytes accessed | tf_op | source)
XLA Modules:
  0.0 287.8 jit_solution(2071595149638191348)
XLA Ops:
  6.5 11.5 %collective-permute-done.refs_1_.refs_5_ = bf16[560,512]{1,0:T(8,128)(2,1)S(1)} collective-permute-done((bf16[560,512]{1,0:T(8,128)(2,1)S(1)}, bf16[560,512]{1,0:T(8,128)(2,1)S(1)}, u32[]{:S(2)}, u32[]{:S(2)}) %collective-permute-start) | collective-permute-done | bytes 573472 | tf_op jit(solution)/shard_map/ppermute | solution.py:348
  22.9 6.4 %copy.26.tok = bf16[896,2240]{1,0:T(8,128)(2,1)} copy(bf16[896,2240]{0,1:T(8,128)(2,1)} %bitcast.70) | data formatting | bytes 8028160 | tf_op jit(solution)/shard_map/squeeze | solution.py:361
  33.4 10.3 %project.3 = (bf16[896,512]{1,0:T(8,128)(2,1)S(1)}, bf16[896,512]{1,0:T(8,128)(2,1)}, f32[40,512]{1,0:T(8,128)S(1)}) custom-call(s32[2]{0:T(128)S(1)} %pad_add_fusion.scal, bf16[896,2240]{1,0:T(8,128)(2,1)} %copy.26.tok, bf16[560,512]{1,0:T(8,128)(2,1)S(1)} %get-tuple-element.73.refs_0_.refs_4_, bf16[560,512]{1,0:T(8,128)(2,1)S(1)} %collective-permute-done.refs_1_.refs_5_, ...), custom_call_target="tpu_custom_call" | custom-call | flops 4110417920 | bytes 8601600 | tf_op jit(solution)/shard_map/project/pallas_call | solution.py:98
  57.4 5.8 %collective-permute-done.5.refs_4_.refs_18_ = bf16[288,608]{1,0:T(8,128)(2,1)} collective-permute-done((bf16[288,608]{1,0:T(8,128)(2,1)S(1)}, bf16[288,608]{1,0:T(8,128)(2,1)}, u32[]{:S(2)}, u32[]{:S(2)}) %collective-permute-start.5) | collective-permute-done | bytes 350240 | tf_op jit(solution)/shard_map/ppermute | solution.py:348
  69.0 4.4 %copy.25 = bf16[1,896,1120]{2,1,0:T(8,128)(2,1)} copy(bf16[1,896,1120]{1,2,0:T(8,128)(2,1)} %param.9) | data formatting | bytes 4014080 | tf_op args[4]
  74.5 13.5 %project.2 = (bf16[896,608]{1,0:T(8,128)(2,1)}, bf16[896,608]{1,0:T(8,128)(2,1)}, f32[40,608]{1,0:T(8,128)S(1)}) custom-call(s32[2]{0:T(128)S(1)} %pad_add_fusion.scal, bf16[896,2240]{1,0:T(8,128)(2,1)} %copy.26.tok, bf16[560,608]{1,0:T(8,128)(2,1)S(1)} %get-tuple-element.30.refs_0_.refs_14_, bf16[560,608]{1,0:T(8,128)(2,1)} %collective-permute-done.2.refs_1_.refs_15_, ...), custom_call_target="tpu_custom_call" | custom-call | flops 4881121280 | bytes 9461760 | tf_op jit(solution)/shard_map/project/pallas_call | solution.py:98
  88.5 5.0 %attend.2 = (bf16[896,512]{1,0:T(8,128)(2,1)S(1)}, bf16[896,512]{1,0:T(8,128)(2,1)S(1)}, f32[40,512]{1,0:T(8,128)S(1)}) custom-call(bf16[896,1120]{1,0:T(8,128)(2,1)S(1)} %bitcast.62, bf16[896,1120]{1,0:T(8,128)(2,1)S(1)} %bitcast.65, f32[40,512]{1,0:T(8,128)S(1)} %add.114.st), custom_call_target="tpu_custom_call" | custom-call | flops 2818572288 | bytes 8028160 | tf_op jit(solution)/shard_map/attend/pallas_call | solution.py:178
  102.8 7.4 %collective-permute-done.24 = f32[40,512]{1,0:T(8,128)S(1)} collective-permute-done((f32[40,512]{1,0:T(8,128)S(1)}, f32[40,512]{1,0:T(8,128)S(1)}, u32[]{:S(2)}, u32[]{:S(2)}) %collective-permute-start.24) | collective-permute-done | bytes 81952 | tf_op jit(solution)/shard_map/ppermute | solution.py:348
  110.2 7.7 %attend.3 = (bf16[896,1120]{1,0:T(8,128)(2,1)S(1)}, bf16[896,1120]{1,0:T(8,128)(2,1)S(1)}, f32[40,608]{1,0:T(8,128)S(1)}) custom-call(bf16[896,1120]{1,0:T(8,128)(2,1)} %bitcast.63, bf16[896,1120]{1,0:T(8,128)(2,1)} %bitcast.64, f32[40,608]{1,0:T(8,128)S(1)} %add.111.st, bf16[896,512]{1,0:T(8,128)(2,1)S(1)} %get-tuple-element.33.refs_0_, ...), custom_call_target="tpu_custom_call" | custom-call | flops 3347054592 | bytes 8028160 | tf_op jit(solution)/shard_map/attend/pallas_call | solution.py:178
  119.3 3.4 %feature_grads.2 = (bf16[896,512]{1,0:T(8,128)(2,1)S(1)}, bf16[896,512]{1,0:T(8,128)(2,1)}) custom-call(s32[2]{0:T(128)S(1)} %pad_add_fusion.scal, bf16[896,512]{1,0:T(8,128)(2,1)S(1)} %copy-done.29, bf16[896,512]{1,0:T(8,128)(2,1)S(1)} %copy-done.30, f32[40,512]{1,0:T(8,128)S(1)} %add.117.st), custom_call_target="tpu_custom_call" | custom-call | flops 939524096 | bytes 3670016 | tf_op jit(solution)/shard_map/feature_grads/pallas_call | solution.py:223
  123.4 4.6 %collective-permute-done.26 = f32[40,608]{1,0:T(8,128)S(1)} collective-permute-done((f32[40,608]{1,0:T(8,128)S(1)}, f32[40,608]{1,0:T(8,128)S(1)}, u32[]{:S(2)}, u32[]{:S(2)}) %collective-permute-start.26) | collective-permute-done | bytes 97312 | tf_op jit(solution)/shard_map/ppermute | solution.py:348
  130.0 5.2 %collective-permute-done.27 = f32[40,608]{1,0:T(8,128)S(1)} collective-permute-done((f32[40,608]{1,0:T(8,128)S(1)}, f32[40,608]{1,0:T(8,128)S(1)}, u32[]{:S(2)}, u32[]{:S(2)}) %collective-permute-start.27) | collective-permute-done | bytes 97312 | tf_op jit(solution)/shard_map/ppermute | solution.py:348
  141.9 9.0 %weight_grads.2 = (bf16[2,272,512]{2,1,0:T(8,128)(2,1)}, bf16[2,288,512]{2,1,0:T(8,128)(2,1)S(1)}, f32[2,272,512]{2,1,0:T(8,128)S(1)}, f32[2,288,512]{2,1,0:T(8,128)S(1)}) custom-call(s32[2]{0:T(128)S(1)} %pad_add_fusion.scal, bf16[2240,896]{1,0:T(8,128)(2,1)} %bitcast.71, bf16[2240,896]{1,0:T(8,128)(2,1)} %collective-permute-done.28.t_other, ...), custom_call_target="tpu_custom_call" | custom-call | flops 4110417920 | bytes 14909440 | tf_op jit(solution)/shard_map/weight_grads/pallas_call | solution.py:275
  154.2 4.1 %copy.30 = bf16[1,896,1120]{1,2,0:T(8,128)(2,1)} copy(bf16[1,896,1120]{2,1,0:T(8,128)(2,1)} %bitcast.61) | data formatting | bytes 4014080
  164.6 11.4 %weight_grads.3 = (bf16[2,272,608]{2,1,0:T(8,128)(2,1)S(1)}, bf16[2,288,608]{2,1,0:T(8,128)(2,1)S(1)}, f32[2,272,608]{2,1,0:T(8,128)S(1)}, f32[2,288,608]{2,1,0:T(8,128)}) custom-call(s32[2]{0:T(128)S(1)} %pad_add_fusion.scal, bf16[2240,896]{1,0:T(8,128)(2,1)} %bitcast.72, bf16[2240,896]{1,0:T(8,128)(2,1)} %collective-permute-done.28.t_other, ...), custom_call_target="tpu_custom_call" | custom-call | flops 4881121280 | bytes 16199680 | tf_op jit(solution)/shard_map/weight_grads/pallas_call | solution.py:275
  181.7 14.3 %collective-permute-done.39 = bf16[2,272,608]{2,1,0:T(8,128)(2,1)S(1)} collective-permute-done((bf16[2,272,608]{2,1,0:T(8,128)(2,1)S(1)}, bf16[2,272,608]{2,1,0:T(8,128)(2,1)S(1)}, u32[]{:S(2)}, u32[]{:S(2)}) %collective-permute-start.39) | collective-permute-done | bytes 661536 | tf_op jit(solution)/shard_map/ppermute | solution.py:348
  202.6 5.1 %collective-permute-done.40 = bf16[272,608]{1,0:T(8,128)(2,1)S(1)} collective-permute-done((bf16[272,608]{1,0:T(8,128)(2,1)S(1)}, bf16[272,608]{1,0:T(8,128)(2,1)S(1)}, u32[]{:S(2)}, u32[]{:S(2)}) %collective-permute-start.40) | collective-permute-done | bytes 330784 | tf_op jit(solution)/shard_map/ppermute | solution.py:348
  212.9 8.5 %collective-permute-done.43 = bf16[280,608]{1,0:T(8,128)(2,1)S(1)} collective-permute-done((bf16[280,608]{1,0:T(8,128)(2,1)S(1)}, bf16[280,608]{1,0:T(8,128)(2,1)S(1)}, u32[]{:S(2)}, u32[]{:S(2)}) %collective-permute-start.43) | collective-permute-done | bytes 340512 | tf_op jit(solution)/shard_map/ppermute | solution.py:348
  225.6 9.4 %collective-permute-done.44 = bf16[140,608]{1,0:T(8,128)(2,1)S(1)} collective-permute-done((bf16[140,608]{1,0:T(8,128)(2,1)S(1)}, bf16[140,608]{1,0:T(8,128)(2,1)S(1)}, u32[]{:S(2)}, u32[]{:S(2)}) %collective-permute-start.44) | collective-permute-done | bytes 170272 | tf_op jit(solution)/shard_map/ppermute | solution.py:348
  235.2 7.1 %collective-permute-done.36 = bf16[140,512]{1,0:T(8,128)(2,1)S(1)} collective-permute-done((bf16[140,512]{1,0:T(8,128)(2,1)S(1)}, bf16[140,512]{1,0:T(8,128)(2,1)S(1)}, u32[]{:S(2)}, u32[]{:S(2)}) %collective-permute-start.36) | collective-permute-done | bytes 143392 | tf_op jit(solution)/shard_map/ppermute | solution.py:348
  245.4 6.7 %collective-permute-done.37 = bf16[280,512]{1,0:T(8,128)(2,1)S(1)} collective-permute-done((bf16[280,512]{1,0:T(8,128)(2,1)S(1)}, bf16[280,512]{1,0:T(8,128)(2,1)S(1)}, u32[]{:S(2)}, u32[]{:S(2)}) %collective-permute-start.37) | collective-permute-done | bytes 286752 | tf_op jit(solution)/shard_map/ppermute | solution.py:348
  253.2 5.7 %collective-permute-done.46 = bf16[280,608]{1,0:T(8,128)(2,1)S(1)} collective-permute-done((bf16[280,608]{1,0:T(8,128)(2,1)S(1)}, bf16[280,608]{1,0:T(8,128)(2,1)S(1)}, u32[]{:S(2)}, u32[]{:S(2)}) %collective-permute-start.46) | collective-permute-done | bytes 340512 | tf_op jit(solution)/shard_map/ppermute | solution.py:348
  259.3 19.5 %input_grads.1 = bf16[896,2240]{1,0:T(8,128)(2,1)} custom-call(s32[2]{0:T(128)S(1)} %pad_add_fusion.scal, bf16[896,512]{1,0:T(8,128)(2,1)} %copy-done.26, bf16[896,512]{1,0:T(8,128)(2,1)} %get-tuple-element.40.refs_1_, bf16[896,608]{1,0:T(8,128)(2,1)} %copy-done.22, bf16[896,608]{1,0:T(8,128)(2,1)} %copy-done.3, bf16[560,512]{1,0:T(8,128)(2,1)S(1)} %copy-done.11, ...), custom_call_target="tpu_custom_call" | custom-call | flops 8991539200 | bytes 14049280 | tf_op jit(solution)/shard_map/input_grads/pallas_call | solution.py:326
  278.8 6.3 %copy.31 = bf16[1,896,2240]{1,2,0:T(8,128)(2,1)} copy(bf16[1,896,2240]{2,1,0:T(8,128)(2,1)} %bitcast.68) | data formatting | bytes 8028160
  (211 shorter events, 94.3 us)
Async XLA Ops:
  2.0 16.0 %collective-permute-start = (bf16[560,512]{1,0:T(8,128)(2,1)S(1)}, bf16[560,512]{1,0:T(8,128)(2,1)S(1)}, u32[]{:S(2)}, u32[]{:S(2)}) collective-permute-start(bf16[560,512]{1,0:T(8,128)(2,1)S(1)} %get-tuple-element.73.refs_0_.refs_4_), channel_id=1, source_target_pairs={{0,8},{8,0},{16,24},{24,16},{1,9},{9,1},{17,25},{25,17},{2,10},{10... | collective-permute-start | bytes 1720328 | tf_op jit(solution)/shard_map/ppermute | solution.py:348
  5.0 14.8 %collective-permute-start.1 = (bf16[560,512]{1,0:T(8,128)(2,1)S(1)}, bf16[560,512]{1,0:T(8,128)(2,1)}, u32[]{:S(2)}, u32[]{:S(2)}) collective-permute-start(bf16[560,512]{1,0:T(8,128)(2,1)S(1)} %get-tuple-element.73.refs_0_.refs_4_), channel_id=1, source_target_pairs={{0,16},{8,24},{16,0},{24,8},{1,17},{9,25},{17,1},{25,9},{2,18},{10... | collective-permute-start | bytes 1720328 | tf_op jit(solution)/shard_map/ppermute | solution.py:348
  18.0 11.8 %collective-permute-start.14 = (bf16[288,512]{1,0:T(8,128)(2,1)S(1)}, bf16[288,512]{1,0:T(8,128)(2,1)S(1)}, u32[]{:S(2)}, u32[]{:S(2)}) collective-permute-start(bf16[288,512]{1,0:T(8,128)(2,1)S(1)} %slice.71), channel_id=1, source_target_pairs={{0,16},{8,24},{16,0},{24,8},{1,17},{9,25},{17,1},{25,9},{2,18},{10... | collective-permute-start | bytes 884744 | tf_op jit(solution)/shard_map/ppermute | solution.py:348
  22.9 117.8 %collective-permute-start.28 = (bf16[2240,896]{1,0:T(8,128)(2,1)}, bf16[2240,896]{1,0:T(8,128)(2,1)}, u32[]{:S(2)}, u32[]{:S(2)}) collective-permute-start(bf16[2240,896]{1,0:T(8,128)(2,1)} %bitcast.69), channel_id=1, source_target_pairs={{0,1},{1,0},{2,3},{3,2},{4,5},{5,4},{6,7},{7,6},{8,9},{9,8},{10,11... | collective-permute-start | bytes 12042248 | tf_op jit(solution)/shard_map/ppermute | solution.py:348
  31.5 20.8 %collective-permute-start.2 = (bf16[560,608]{1,0:T(8,128)(2,1)S(1)}, bf16[560,608]{1,0:T(8,128)(2,1)}, u32[]{:S(2)}, u32[]{:S(2)}) collective-permute-start(bf16[560,608]{1,0:T(8,128)(2,1)S(1)} %get-tuple-element.30.refs_0_.refs_14_), channel_id=1, source_target_pairs={{0,8},{8,0},{16,24},{24,16},{1,9},{9,1},{17,25},{25,17},{2,10},{10... | collective-permute-start | bytes 2042888 | tf_op jit(solution)/shard_map/ppermute | solution.py:348
  32.1 22.2 %collective-permute-start.3 = (bf16[560,608]{1,0:T(8,128)(2,1)S(1)}, bf16[560,608]{1,0:T(8,128)(2,1)}, u32[]{:S(2)}, u32[]{:S(2)}) collective-permute-start(bf16[560,608]{1,0:T(8,128)(2,1)S(1)} %get-tuple-element.30.refs_0_.refs_14_), channel_id=1, source_target_pairs={{0,16},{8,24},{16,0},{24,8},{1,17},{9,25},{17,1},{25,9},{2,18},{10... | collective-permute-start | bytes 2042888 | tf_op jit(solution)/shard_map/ppermute | solution.py:348
  54.2 20.2 %collective-permute-start.6 = (bf16[560,608]{1,0:T(8,128)(2,1)}, bf16[560,608]{1,0:T(8,128)(2,1)}, u32[]{:S(2)}, u32[]{:S(2)}) collective-permute-start(bf16[560,608]{1,0:T(8,128)(2,1)} %collective-permute-done.2.refs_1_.refs_15_), channel_id=1, source_target_pairs={{0,1},{1,0},{2,3},{3,2},{4,5},{5,4},{6,7},{7,6},{8,9},{9,8},{10,11... | collective-permute-start | bytes 2042888 | tf_op jit(solution)/shard_map/ppermute | solution.py:348
  54.3 20.2 %collective-permute-start.7 = (bf16[560,608]{1,0:T(8,128)(2,1)}, bf16[560,608]{1,0:T(8,128)(2,1)}, u32[]{:S(2)}, u32[]{:S(2)}) collective-permute-start(bf16[560,608]{1,0:T(8,128)(2,1)} %collective-permute-done.3.refs_2_.refs_16_), channel_id=1, source_target_pairs={{0,1},{1,0},{2,3},{3,2},{4,5},{5,4},{6,7},{7,6},{8,9},{9,8},{10,11... | collective-permute-start | bytes 2042888 | tf_op jit(solution)/shard_map/ppermute | solution.py:348
  122.7 18.0 %collective-permute-start.29 = (bf16[896,512]{1,0:T(8,128)(2,1)}, bf16[896,512]{1,0:T(8,128)(2,1)}, u32[]{:S(2)}, u32[]{:S(2)}) collective-permute-start(bf16[896,512]{1,0:T(8,128)(2,1)} %get-tuple-element.40.refs_1_), channel_id=1, source_target_pairs={{0,1},{1,0},{2,3},{3,2},{4,5},{5,4},{6,7},{7,6},{8,9},{9,8},{10,11... | collective-permute-start | bytes 2752520 | tf_op jit(solution)/shard_map/ppermute | solution.py:348
  140.7 20.0 %collective-permute-start.38 = (bf16[896,608]{0,1:T(8,128)(2,1)}, bf16[896,608]{0,1:T(8,128)(2,1)}, u32[]{:S(2)}, u32[]{:S(2)}) collective-permute-start(bf16[896,608]{0,1:T(8,128)(2,1)} %copy.28), channel_id=1, source_target_pairs={{0,1},{1,0},{2,3},{3,2},{4,5},{5,4},{6,7},{7,6},{8,9},{9,8},{10,11... | collective-permute-start | bytes 3268616 | tf_op jit(solution)/shard_map/ppermute | solution.py:348
  152.7 25.3 %collective-permute-start.30 = (bf16[2,272,512]{2,1,0:T(8,128)(2,1)}, bf16[2,272,512]{2,1,0:T(8,128)(2,1)}, u32[]{:S(2)}, u32[]{:S(2)}) collective-permute-start(bf16[2,272,512]{2,1,0:T(8,128)(2,1)} %get-tuple-element.48), channel_id=1, source_target_pairs={{0,8},{8,0},{16,24},{24,16},{1,9},{9,1},{17,25},{25,17},{2,10},{10... | collective-permute-start | bytes 1671176 | tf_op jit(solution)/shard_map/ppermute | solution.py:348
  162.8 17.8 %collective-permute-start.32 = (bf16[2,288,512]{2,1,0:T(8,128)(2,1)S(1)}, bf16[2,288,512]{2,1,0:T(8,128)(2,1)S(1)}, u32[]{:S(2)}, u32[]{:S(2)}) collective-permute-start(bf16[2,288,512]{2,1,0:T(8,128)(2,1)S(1)} %copy-done.15), channel_id=1, source_target_pairs={{0,16},{8,24},{16,0},{24,8},{1,17},{9,25},{17,1},{25,9},{2,18},{10... | collective-permute-start | bytes 1769480 | tf_op jit(solution)/shard_map/ppermute | solution.py:348
  176.0 20.8 %collective-permute-start.41 = (bf16[2,288,608]{2,1,0:T(8,128)(2,1)S(1)}, bf16[2,288,608]{2,1,0:T(8,128)(2,1)S(1)}, u32[]{:S(2)}, u32[]{:S(2)}) collective-permute-start(bf16[2,288,608]{2,1,0:T(8,128)(2,1)S(1)} %get-tuple-element.54), channel_id=1, source_target_pairs={{0,16},{8,24},{16,0},{24,8},{1,17},{9,25},{17,1},{25,9},{2,18},{10... | collective-permute-start | bytes 2101256 | tf_op jit(solution)/shard_map/ppermute | solution.py:348
  177.5 18.5 %collective-permute-start.39 = (bf16[2,272,608]{2,1,0:T(8,128)(2,1)S(1)}, bf16[2,272,608]{2,1,0:T(8,128)(2,1)S(1)}, u32[]{:S(2)}, u32[]{:S(2)}) collective-permute-start(bf16[2,272,608]{2,1,0:T(8,128)(2,1)S(1)} %get-tuple-element.52), channel_id=1, source_target_pairs={{0,8},{8,0},{16,24},{24,16},{1,9},{9,1},{17,25},{25,17},{2,10},{10... | collective-permute-start | bytes 1984520 | tf_op jit(solution)/shard_map/ppermute | solution.py:348
  179.3 22.0 %collective-permute-start.31 = (bf16[272,512]{1,0:T(8,128)(2,1)S(1)}, bf16[272,512]{1,0:T(8,128)(2,1)S(1)}, u32[]{:S(2)}, u32[]{:S(2)}) collective-permute-start(bf16[272,512]{1,0:T(8,128)(2,1)S(1)} %fusion.13), channel_id=1, source_target_pairs={{0,16},{8,24},{16,0},{24,8},{1,17},{9,25},{17,1},{25,9},{2,18},{10... | collective-permute-start | bytes 835592 | tf_op jit(solution)/shard_map/ppermute | solution.py:348
  180.9 21.5 %collective-permute-start.33 = (bf16[288,512]{1,0:T(8,128)(2,1)S(1)}, bf16[288,512]{1,0:T(8,128)(2,1)S(1)}, u32[]{:S(2)}, u32[]{:S(2)}) collective-permute-start(bf16[288,512]{1,0:T(8,128)(2,1)S(1)} %fusion.9), channel_id=1, source_target_pairs={{0,8},{8,0},{16,24},{24,16},{1,9},{9,1},{17,25},{25,17},{2,10},{10... | collective-permute-start | bytes 884744 | tf_op jit(solution)/shard_map/ppermute | solution.py:348
  196.2 11.6 %collective-permute-start.40 = (bf16[272,608]{1,0:T(8,128)(2,1)S(1)}, bf16[272,608]{1,0:T(8,128)(2,1)S(1)}, u32[]{:S(2)}, u32[]{:S(2)}) collective-permute-start(bf16[272,608]{1,0:T(8,128)(2,1)S(1)} %fusion.8), channel_id=1, source_target_pairs={{0,16},{8,24},{16,0},{24,8},{1,17},{9,25},{17,1},{25,9},{2,18},{10... | collective-permute-start | bytes 992264 | tf_op jit(solution)/shard_map/ppermute | solution.py:348
  209.1 12.3 %collective-permute-start.43 = (bf16[280,608]{1,0:T(8,128)(2,1)S(1)}, bf16[280,608]{1,0:T(8,128)(2,1)S(1)}, u32[]{:S(2)}, u32[]{:S(2)}) collective-permute-start(bf16[280,608]{1,0:T(8,128)(2,1)S(1)} %fusion.7), channel_id=1, source_target_pairs={{0,2},{1,3},{2,0},{3,1},{4,6},{5,7},{6,4},{7,5},{8,10},{9,11},{10,... | collective-permute-start | bytes 1021448 | tf_op jit(solution)/shard_map/ppermute | solution.py:348
  210.1 12.2 %collective-permute-start.35 = (bf16[140,512]{1,0:T(8,128)(2,1)}, bf16[140,512]{1,0:T(8,128)(2,1)}, u32[]{:S(2)}, u32[]{:S(2)}) collective-permute-start(bf16[140,512]{1,0:T(8,128)(2,1)} %fusion.15), channel_id=1, source_target_pairs={{0,4},{1,5},{2,6},{3,7},{4,0},{5,1},{6,2},{7,3},{8,12},{9,13},{10,... | collective-permute-start | bytes 430088 | tf_op jit(solution)/shard_map/ppermute | solution.py:348
  221.6 13.4 %collective-permute-start.44 = (bf16[140,608]{1,0:T(8,128)(2,1)S(1)}, bf16[140,608]{1,0:T(8,128)(2,1)S(1)}, u32[]{:S(2)}, u32[]{:S(2)}) collective-permute-start(bf16[140,608]{1,0:T(8,128)(2,1)S(1)} %fusion.14), channel_id=1, source_target_pairs={{0,4},{1,5},{2,6},{3,7},{4,0},{5,1},{6,2},{7,3},{8,12},{9,13},{10,... | collective-permute-start | bytes 510728 | tf_op jit(solution)/shard_map/ppermute | solution.py:348
  223.3 19.0 %collective-permute-start.36 = (bf16[140,512]{1,0:T(8,128)(2,1)S(1)}, bf16[140,512]{1,0:T(8,128)(2,1)S(1)}, u32[]{:S(2)}, u32[]{:S(2)}) collective-permute-start(bf16[140,512]{1,0:T(8,128)(2,1)S(1)} %fusion.11), channel_id=1, source_target_pairs={{0,4},{1,5},{2,6},{3,7},{4,0},{5,1},{6,2},{7,3},{8,12},{9,13},{10,... | collective-permute-start | bytes 430088 | tf_op jit(solution)/shard_map/ppermute | solution.py:348
  245.3 13.6 %collective-permute-start.46 = (bf16[280,608]{1,0:T(8,128)(2,1)S(1)}, bf16[280,608]{1,0:T(8,128)(2,1)S(1)}, u32[]{:S(2)}, u32[]{:S(2)}) collective-permute-start(bf16[280,608]{1,0:T(8,128)(2,1)S(1)} %pad_maximum_fusion.5), channel_id=1, source_target_pairs={{0,2},{1,3},{2,0},{3,1},{4,6},{5,7},{6,4},{7,5},{8,10},{9,11},{10,... | collective-permute-start | bytes 1021448 | tf_op jit(solution)/shard_map/ppermute | solution.py:348
  253.2 32.0 %collective-permute-start.47 = (bf16[560,512]{1,0:T(8,128)(2,1)}, bf16[560,512]{1,0:T(8,128)(2,1)S(1)}, u32[]{:S(2)}, u32[]{:S(2)}) collective-permute-start(bf16[560,512]{1,0:T(8,128)(2,1)} %pad_maximum_fusion.4), channel_id=1, source_target_pairs={{0,1},{1,0},{2,3},{3,2},{4,5},{5,4},{6,7},{7,6},{8,9},{9,8},{10,11... | collective-permute-start | bytes 1720328 | tf_op jit(solution)/shard_map/ppermute | solution.py:348
  259.2 25.9 %collective-permute-start.48 = (bf16[560,608]{1,0:T(8,128)(2,1)S(1)}, bf16[560,608]{1,0:T(8,128)(2,1)S(1)}, u32[]{:S(2)}, u32[]{:S(2)}) collective-permute-start(bf16[560,608]{1,0:T(8,128)(2,1)S(1)} %pad_maximum_fusion.3), channel_id=1, source_target_pairs={{0,1},{1,0},{2,3},{3,2},{4,5},{5,4},{6,7},{7,6},{8,9},{9,8},{10,11... | collective-permute-start | bytes 2042888 | tf_op jit(solution)/shard_map/ppermute | solution.py:348
  (59 other events, 576.4 us)

commit v2 on v0

v2 whole, which is shorter than its diff:
```python
import functools

import jax
import jax.numpy as jnp
from jax import lax
from jax.experimental import pallas as pl
from jax.experimental.pallas import tpu as pltpu
from jax.sharding import PartitionSpec as P

HD = 32
EPS_DEN = 1e-06
LANES = 256
BF, F32 = jnp.bfloat16, jnp.float32
MIB = 1024 * 1024


def dot(a, b, ca, cb):
    return lax.dot_general(a, b, (((ca,), (cb,)), ((), ())), preferred_element_type=F32)


def tiles_of(width):
    return [(s, min(LANES, width - s)) for s in range(0, width, LANES)]


def same_head(w):
    row = lax.broadcasted_iota(jnp.int32, (w, w), 0) // HD
    col = lax.broadcasted_iota(jnp.int32, (w, w), 1) // HD
    return row == col


def diagonal(w):
    return lax.broadcasted_iota(jnp.int32, (w, w), 0) == lax.broadcasted_iota(jnp.int32, (w, w), 1)


def fold(full, w):
    kept = jnp.where(same_head(w), full, 0.0)
    total = kept[0:HD]
    for at in range(HD, w, HD):
        total = total + kept[at : at + HD]
    return total


def unfold(rows, w):
    return jnp.where(same_head(w), jnp.concatenate([rows] * (w // HD), axis=0), 0.0)


def padded(width):
    return -(-width // 128) * 128


def split(x):
    high = x.astype(BF)
    return high, (x - high.astype(F32)).astype(BF)


def call(
    kernel, name, flops, nbytes, args, *, grid, in_specs, out_specs, out_shape, scalars=0, scratch=(), wait=(), vmem=40
):
    at, skip = scalars + len(in_specs), len(wait)

    def run(*refs):
        kernel(*refs[:at], *refs[at + skip :])

    return pl.pallas_call(
        run,
        grid_spec=pltpu.PrefetchScalarGridSpec(
            num_scalar_prefetch=scalars,
            grid=grid,
            in_specs=list(in_specs) + [pl.BlockSpec(memory_space=pltpu.HBM)] * skip,
            out_specs=out_specs,
            scratch_shapes=list(scratch),
        ),
        out_shape=out_shape,
        compiler_params=pltpu.CompilerParams(
            vmem_limit_bytes=vmem * MIB, dimension_semantics=("arbitrary",)
        ),
        cost_estimate=pl.CostEstimate(flops=flops, bytes_accessed=nbytes, transcendentals=0),
        name=name,
    )(*args, *wait)


def place(core, refs, spots, shard, buf, sems):
    span = span_of(shard)
    copies = []
    for n, (ref, (owner, whose, at)) in enumerate(zip(refs, spots)):
        size, skip, off = ref.shape[0], 0, at
        if whose is not None and whose != core:
            skip = 2 * span - shard if at == 0 else 0
            off = shard - span + at + skip
        copies.append(
            pltpu.make_async_copy(
                ref.at[pl.ds(skip, size - skip), :],
                buf.at[pl.ds(owner * shard + off, size - skip), :],
                sems.at[n],
            )
        )
    return copies


def span_of(shard):
    return (shard // 2 + 15) // 16 * 16


def fetch(scal, refs, spots, shard, buf, sems):
    for core in (0, 1):

        @pl.when(scal[0] == core)
        def _():
            copies = place(core, refs, spots, shard, buf, sems)
            for c in copies:
                c.start()
            for c in copies:
                c.wait()


def layout_kernel(scal, block, near, far, give):
    step = pl.program_id(0)
    shard = far.shape[1]
    half = shard // 2
    give[0] = jnp.where(scal[0] == 0, block[0, half:], block[0, :half])
    for r in range(near.shape[1] // shard):

        @pl.when(step == r)
        def _():
            near[:, r * shard : (r + 1) * shard] = block[0].T

    @pl.when(step == pl.num_programs(0) - 1)
    def _():
        far[...] = block[0].T


def token_rows(scal, blocks):
    owners, shard, count = blocks.shape
    wide = (owners - 1) * shard
    return call(
        layout_kernel,
        "token_rows",
        0,
        6 * owners * shard * count,
        (scal, blocks),
        scalars=1,
        grid=(owners,),
        in_specs=[pl.BlockSpec((1, shard, count), lambda i, s: (s[1] ^ i, 0, 0))],
        out_specs=[
            pl.BlockSpec((count, wide), lambda i, s: (0, 0)),
            pl.BlockSpec((count, shard), lambda i, s: (0, 0)),
            pl.BlockSpec((1, shard // 2, count), lambda i, s: (i, 0, 0)),
        ],
        out_shape=[
            jax.ShapeDtypeStruct((count, wide), BF),
            jax.ShapeDtypeStruct((count, shard), BF),
            jax.ShapeDtypeStruct((owners, shard // 2, count), BF),
        ],
    )


def first_kernel(spots, shard, scal, tok, *refs):
    pieces = refs[: len(spots)]
    out, buf, sems = refs[len(spots) :]

    @pl.when(pl.program_id(0) == 0)
    def _():
        fetch(scal, pieces, spots, shard, buf, sems)

    out[...] = dot(tok[...], buf[...], 1, 0)


def key_kernel(spots, shard, scal, tok, part, *refs):
    pieces = refs[: len(spots)]
    k_out, kn_out, buf, sems = refs[len(spots) :]

    @pl.when(pl.program_id(0) == 0)
    def _():
        fetch(scal, pieces, spots, shard, buf, sems)
        kn_out[...] = jnp.zeros_like(kn_out)

    key = jnp.maximum(dot(tok[...], buf[...], 1, 0) + part[...], 0.0).astype(BF)
    k_out[:, : key.shape[1]] = key
    kn_out[...] += jnp.sum(key.astype(F32), axis=0, keepdims=True)


def val_kernel(spots, shard, scal, tok, part, k_ref, *refs):
    pieces = refs[: len(spots)]
    v_out, kv_out, buf, sems = refs[len(spots) :]

    @pl.when(pl.program_id(0) == 0)
    def _():
        fetch(scal, pieces, spots, shard, buf, sems)
        kv_out[...] = jnp.zeros_like(kv_out)

    width = buf.shape[1]
    v_out[:, :width] = (dot(tok[...], buf[...], 1, 0) + part[...]).astype(BF)
    for s, w in tiles_of(width):
        cols = slice(s, s + w)
        kv_out[:, cols] += fold(dot(v_out[:, cols], k_ref[:, cols], 0, 0), w)


def project(kernel, name, scal, tok, feats, pieces, spots, shard, state_rows, tile, wait=()):
    count, depth = tok.shape
    width = pieces[0].shape[1]
    rows = lambda w: pl.BlockSpec((tile, w), lambda i, s: (i, 0))
    kind, wide = (BF, padded(width)) if state_rows else (F32, width)
    return call(
        functools.partial(kernel, spots, shard),
        name,
        2 * count * depth * width,
        2 * (count * depth + depth * width + 3 * count * width),
        (scal, tok, *feats, *pieces),
        scalars=1,
        grid=(count // tile,),
        in_specs=[pl.BlockSpec((tile, depth), lambda i, s: (i, 0))]
        + [rows(x.shape[1]) for x in feats]
        + [pl.BlockSpec(memory_space=pltpu.HBM)] * len(pieces),
        out_specs=[rows(wide)] + [pl.BlockSpec((state_rows, width), lambda i, s: (0, 0))] * bool(state_rows),
        out_shape=[jax.ShapeDtypeStruct((count, wide), kind)]
        + [jax.ShapeDtypeStruct((state_rows, width), F32)] * bool(state_rows),
        scratch=[pltpu.VMEM((depth, width), BF), pltpu.SemaphoreType.DMA((len(pieces),))],
        wait=wait,
    )


def valid_rows(x, width):
    w = x.shape[0]
    return jnp.where(lax.broadcasted_iota(jnp.int32, (w, 1), 0) < width - pl.program_id(0) * w, x, 0)


def valid_lanes(x, width):
    w = x.shape[1]
    return jnp.where(lax.broadcasted_iota(jnp.int32, (1, w), 1) < width - pl.program_id(0) * w, x, 0)


def denominators(q, kn_row, w):
    high, low = split(jnp.where(same_head(w), jnp.broadcast_to(kn_row, (w, w)), 0.0))
    return 1.0 / (dot(high, q, 1, 0) + dot(low, q, 1, 0) + EPS_DEN)


def grad_kernel(width, q_ref, g_ref, kn, gs_out):
    w = q_ref.shape[0]
    q = valid_rows(jnp.maximum(q_ref[...], 0), width)
    g = valid_rows(g_ref[...], width).astype(F32)
    kn_row = valid_lanes(kn[...], width)
    dn = (g * denominators(q, kn_row, w)).astype(BF)
    gs_out[...] = fold(dot(dn, q, 1, 1), w)


def norm_kernel(width, q_ref, g_ref, kn, st, gn_out):
    w = q_ref.shape[0]
    q = valid_rows(jnp.maximum(q_ref[...], 0), width)
    g = valid_rows(g_ref[...], width).astype(F32)
    kn_row = valid_lanes(kn[...], width)
    kv_hi, kv_lo = split(unfold(valid_lanes(st[...], width), w))
    ones = jnp.where(same_head(w), 1.0, 0.0).astype(BF)
    inv = denominators(q, kn_row, w)
    attn = (dot(kv_hi, q, 1, 0) + dot(kv_lo, q, 1, 0)) * inv
    dden = -dot(ones, (g * attn).astype(BF), 1, 0) * inv
    gn = jnp.sum(dden * q.astype(F32), axis=1, keepdims=True)
    gn_out[...] = jnp.sum(jnp.where(diagonal(w), gn, 0.0), axis=0, keepdims=True)


def attend_kernel(width, q_ref, g_ref, kn, st, att_out, dq_out):
    w = q_ref.shape[0]
    q = valid_rows(jnp.maximum(q_ref[...], 0), width)
    g = valid_rows(g_ref[...], width).astype(F32)
    kn_row = valid_lanes(kn[...], width)
    kv = unfold(valid_lanes(st[...], width), w)
    kv_hi, kv_lo = split(kv)
    back_hi, back_lo = split(kv.T)
    kn_col = jnp.sum(jnp.where(diagonal(w), kn_row, 0.0), axis=1, keepdims=True)
    ones = jnp.where(same_head(w), 1.0, 0.0).astype(BF)

    inv = denominators(q, kn_row, w)
    attn = (dot(kv_hi, q, 1, 0) + dot(kv_lo, q, 1, 0)) * inv
    att_out[...] = attn.astype(BF)
    ga_hi, ga_lo = split(g * attn)
    dden = -(dot(ones, ga_hi, 1, 0) + dot(ones, ga_lo, 1, 0)) * inv
    dn_hi, dn_lo = split(g * inv)
    df = dot(back_hi, dn_hi, 1, 0) + dot(back_lo, dn_hi, 1, 0) + dot(back_hi, dn_lo, 1, 0)
    df = df + dden * kn_col
    dq_out[...] = jnp.where(q.astype(F32) > 0, df, 0.0).astype(BF)


def attention(kernel, name, queries, cotangent, states, n_big, state_rows, passes, wait=()):
    full, count = queries.shape
    row = pl.BlockSpec((LANES, count), lambda i: (i, 0))
    state = lambda r: pl.BlockSpec((r, LANES), lambda i: (0, i))
    return call(
        functools.partial(kernel, full),
        name,
        2 * passes * count * full * LANES,
        2 * (2 + n_big) * count * full,
        (queries, cotangent, *states),
        grid=(-(-full // LANES),),
        in_specs=[row, row] + [state(x.shape[0]) for x in states],
        out_specs=[row] * n_big + [state(state_rows)] * bool(state_rows),
        out_shape=[jax.ShapeDtypeStruct((full, count), BF)] * n_big
        + [jax.ShapeDtypeStruct((state_rows, full), F32)] * bool(state_rows),
        wait=wait,
    )


def dval_of(feats, states, scale, high, low, cols):
    (key,) = feats
    return dot(key[:, cols], high, 1, 1) + dot(key[:, cols], low, 1, 1)


def dkey_of(feats, states, scale, high, low, cols):
    key, val = feats
    d = dot(val[:, cols], high, 1, 0) + dot(val[:, cols], low, 1, 0) + states[1][:, cols] * scale
    return jnp.where(key[:, cols].astype(F32) > 0, d, 0.0)


def feature_grad(make, scale, feats, states, out):
    for s, w in tiles_of(states[0].shape[1]):
        cols = slice(s, s + w)
        high, low = split(unfold(states[0][:, cols] * scale, w))
        out[:, cols] = make(feats, states, scale, high, low, cols).astype(BF)


def feature_kernel(make, scale, n_feats, *refs):
    feature_grad(make, scale, refs[:n_feats], refs[n_feats:-1], refs[-1])


def feature_grads(make, name, feats, states, scale):
    count, wide = feats[0].shape
    return call(
        functools.partial(feature_kernel, make, scale, len(feats)),
        name,
        4 * count * wide * LANES,
        2 * count * wide * (1 + len(feats)),
        (*feats, *states),
        grid=(1,),
        in_specs=[pl.BlockSpec(x.shape, lambda i: (0, 0)) for x in (*feats, *states)],
        out_specs=[pl.BlockSpec((count, wide), lambda i: (0, 0))],
        out_shape=[jax.ShapeDtypeStruct((count, wide), BF)],
    )


def weight_kernel(make, scale, n_feats, n_states, scal, t_own, t_other, *refs):
    own, other = refs[:n_feats], refs[n_feats : 2 * n_feats]
    states = refs[2 * n_feats : 2 * n_feats + n_states]
    d_own, send_a, send_b, keep_a, keep_b, d_other = refs[2 * n_feats + n_states :]
    step = pl.program_id(0)

    @pl.when(step == 0)
    def _():
        feature_grad(make, scale, own, states, d_own)
        feature_grad(make, scale, other, states, d_other)

    cut, width = send_a.shape[1:]
    part = dot(t_own[0], d_own[:, :width], 1, 0) + dot(t_other[0], d_other[:, :width], 1, 0)
    a, b = part[:cut], part[cut:]

    @pl.when(step == 0)
    def _():
        send_a[1] = a.astype(BF)
        send_b[1] = b.astype(BF)

    @pl.when(step == 1)
    def _():
        send_b[0] = b.astype(BF)
        keep_a[1] = a

    @pl.when(step == 2)
    def _():
        send_a[0] = a.astype(BF)
        keep_b[1] = b

    @pl.when(step == 3)
    def _():
        keep_a[0] = a
        keep_b[0] = b


def weight_grads(make, name, scal, t_own, t_other, own, other, states, scale, wait=()):
    blocks, rows, count = t_other.shape
    wide, width = own[0].shape[1], states[0].shape[1]
    owned = pl.BlockSpec((1, rows, count), lambda i, s: (2 * (s[1] ^ (3 - i)) + s[0], 0, 0))
    others = pl.BlockSpec((1, rows, count), lambda i, s: (3 - i, 0, 0))
    whole = lambda x: pl.BlockSpec(x.shape, lambda i, s: (0, 0))
    full = lambda r: pl.BlockSpec((2, r, width), lambda i, s: (0, 0, 0))
    cut = (rows // 2 + 15) // 16 * 16
    rest = rows - cut
    return call(
        functools.partial(weight_kernel, make, scale, len(own), len(states)),
        name,
        4 * count * blocks * rows * width,
        4 * count * (blocks * rows + width * len(own)) + 3 * blocks * rows * width,
        (scal, t_own, t_other, *own, *other, *states),
        scalars=1,
        grid=(blocks,),
        in_specs=[owned, others] + [whole(x) for x in (*own, *other, *states)],
        out_specs=[whole(own[0]), full(cut), full(rest), full(cut), full(rest)],
        out_shape=[
            jax.ShapeDtypeStruct((count, wide), BF),
            jax.ShapeDtypeStruct((2, cut, width), BF),
            jax.ShapeDtypeStruct((2, rest, width), BF),
            jax.ShapeDtypeStruct((2, cut, width), F32),
            jax.ShapeDtypeStruct((2, rest, width), F32),
        ],
        scratch=[pltpu.VMEM((count, wide), BF)],
        wait=wait,
        vmem=48,
    )


def input_kernel(counts, spots, shard, scal, d_key, d_val, *refs):
    n = len(spots)
    keys, vals = refs[:n], refs[n : 2 * n]
    out, buf_k, buf_v, sems = refs[2 * n :]
    step = pl.program_id(0)

    def copies(core, k):
        at = sum(counts[:k])
        some = slice(at, at + counts[k])
        return [
            c
            for w, (pieces, buf) in enumerate(((keys, buf_k), (vals, buf_v)))
            for c in place(core, pieces[some], spots[some], shard, buf.at[k], sems.at[w, pl.ds(at, counts[k])])
        ]

    for core in (0, 1):

        @pl.when((scal[0] == core) & (step == 0))
        def _():
            for k in range(len(counts)):
                for c in copies(core, k):
                    c.start()

        for k in range(len(counts)):

            @pl.when((scal[0] == core) & (step == k))
            def _():
                for c in copies(core, k):
                    c.wait()

    width = buf_k.shape[2]
    total = dot(buf_k[step], d_key[:, :width], 1, 1) + dot(buf_v[step], d_val[:, :width], 1, 1)
    out[...] = total.astype(BF)


def input_grads(scal, d_key, d_val, keys, vals, spots, shard, depth, wait=()):
    count, width = d_key.shape[0], keys[0].shape[1]
    owners = depth // shard
    counts = tuple(sum(p[0] == k for p in spots) for k in range(owners))
    local = tuple((0,) + p[1:] for p in spots)
    whole = pl.BlockSpec(d_key.shape, lambda i, s: (0, 0))
    return call(
        functools.partial(input_kernel, counts, local, shard),
        "d_tokens",
        4 * count * depth * width,
        2 * depth * (count + 2 * width) + 4 * count * width,
        (scal, d_key, d_val, *keys, *vals),
        scalars=1,
        grid=(owners,),
        in_specs=[whole, whole] + [pl.BlockSpec(memory_space=pltpu.HBM)] * (len(keys) + len(vals)),
        out_specs=pl.BlockSpec((shard, count), lambda i, s: (s[1] ^ i, 0)),
        out_shape=jax.ShapeDtypeStruct((depth, count), BF),
        scratch=[
            pltpu.VMEM((owners, shard, width), BF),
            pltpu.VMEM((owners, shard, width), BF),
            pltpu.SemaphoreType.DMA((2, len(keys))),
        ],
        wait=wait,
        vmem=56,
    )


def swap(x, axis, bit):
    n = lax.axis_size(axis)
    return lax.ppermute(x, axis, [(i, i ^ bit) for i in range(n)])


def tile_of(count, sizes=(448, 128, 64, 32, 16)):
    return next(t for t in sizes if count % t == 0)


def together(*xs):
    return lax.optimization_barrier(xs)


def body_exchange(tokens, queries, w_key, w_value, cotangent):
    tok_t, qs, cot = tokens[0].T, queries[0].T, cotangent[0].T
    depth, count = tok_t.shape
    shard, full = w_key.shape
    tile = tile_of(count)
    img, spx = lax.axis_index("img"), lax.axis_index("sp")
    core, z = spx % 2, spx // 2
    scal = jnp.stack([core, img]).astype(jnp.int32)
    tok_img = count * lax.axis_size("sp")
    feat_scale = float(tok_img)
    scale = 1.0 / (lax.axis_size("img") * tok_img) ** 0.5

    span = span_of(shard)
    near = span // 32 * 16

    def near_rows(w):
        return jnp.where(core == 0, w[:span], w[shard - span :])

    def gather_near(own):
        return swap(own, "img", 1), swap(own, "img", 2)

    def gather_far(by_x, by_y):
        return swap(by_y[:near], "img", 1), swap(by_x[near:], "img", 2)

    def with_other(*pieces):
        return [p for piece in pieces for p in (piece, swap(piece, "sp", 1))]

    near_spots = ((0, None, 0), (1, 0, 0), (1, 1, 0), (2, 0, 0), (2, 1, 0))
    far_spots = ((0, 0, 0), (0, 1, 0), (0, 0, near), (0, 1, near))
    spots = near_spots + tuple((3,) + p[1:] for p in far_spots)

    def add(x, bit):
        return x + swap(x, "sp", bit)

    def add_beside(x, bit, *beside):
        got, *beside = together(swap(x.astype(BF), "sp", bit), *beside)
        return (x + got.astype(F32), *beside)

    kx, ky = gather_near(near_rows(w_key))
    t_own = tok_t.reshape(2 * lax.axis_size("img"), shard // 2, count)
    tok_near, tok_far, t_give = token_rows(scal, tok_t.reshape(lax.axis_size("img"), shard, count))
    kx, ky, tok_near, tok_far, t_give = together(kx, ky, tok_near, tok_far, t_give)
    kfa, kfb = gather_far(kx, ky)
    keys_near = [w_key] + with_other(kx, ky)
    t_other = swap(t_give, "sp", 1)
    (k_part,) = project(first_kernel, "key_near", scal, tok_near, [], keys_near, near_spots, shard, 0, tile)
    kfa, kfb, k_part, v_own, t_other = together(kfa, kfb, k_part, near_rows(w_value), t_other)
    keys_far = with_other(kfa, kfb)
    vx, vy = gather_near(v_own)
    key, kn = project(key_kernel, "key_feat", scal, tok_far, [k_part], keys_far, far_spots, shard, 1, tile)
    kn, key = together(add(kn, 1), key)
    key_other = swap(key, "sp", 1)
    kn, vx, vy = together(add(add(kn, 2), 4), vx, vy)
    (gs,) = attention(grad_kernel, "grad_state", qs, cot, [kn], 0, HD, 4)
    vx, vy, gs = together(vx, vy, gs)
    vfa, vfb = gather_far(vx, vy)
    gs = add(gs, 1)
    vals_near = [w_value] + with_other(vx, vy)
    (v_part,) = project(
        first_kernel, "val_near", scal, tok_near, [], vals_near, near_spots, shard, 0, tile, [gs]
    )
    gs, v_part, vfa, vfb, key_other = add_beside(gs, 2, v_part, vfa, vfb, key_other)
    vals_far = with_other(vfa, vfb)
    val, kv = project(val_kernel, "val_feat", scal, tok_far, [v_part, key], vals_far, far_spots, shard, HD, tile)
    gs, val, kv = add_beside(gs, 4, val, kv)
    kv, val = together(add(kv, 1), val)
    val_other = swap(val, "sp", 1)

    def reduce_near(parts):
        send_a, send_b, keep_a, keep_b = parts
        return swap(send_a, "img", 1), swap(send_b, "img", 2), keep_a, keep_b

    def add_near(got_a, got_b, keep_a, keep_b):
        a, b = keep_a + got_a.astype(F32), keep_b + got_b.astype(F32)
        return a[0], b[0], a[1].astype(BF), b[1].astype(BF)

    def reduce_far(a, b, send_a, send_b):
        return a, b, swap(send_a, "img", 2), swap(send_b, "img", 1)

    def merge(a, b, ra, rb):
        rows = [a + ra.astype(F32), b + rb.astype(F32)]
        spare = jnp.zeros((-(shard // 2) % 32, full), F32)
        return jnp.concatenate(rows + [spare], axis=0)

    def reduce_z(own):
        quarters = own.reshape(4, own.shape[0] // 4, full)
        pick = lambda k: lax.dynamic_index_in_dim(quarters, z ^ k, 0, False)
        sends = [pick(k).astype(BF) for k in (1, 2, 3)]
        return pick(0), sends, [swap(x, "sp", 2 * k) for k, x in zip((1, 2, 3), sends)]

    def spread_z(mine, gots):
        for got in gots:
            mine = mine + got.astype(F32)
        mine = (mine * scale).astype(BF)
        return [mine] + [swap(mine, "sp", 2 * k) for k in (1, 2, 3)]

    z0, z1 = z % 2, z // 2

    def part_of(x, at):
        return lax.dynamic_index_in_dim(x.reshape(2, x.shape[0] // 2, full), at, 0, False)

    def joined(mine, other, bit):
        low = bit == 0
        return jnp.concatenate([jnp.where(low, mine, other), jnp.where(low, other, mine)], axis=0)

    def ordered(quarters):
        stack = jnp.stack(quarters)
        return jnp.concatenate([lax.dynamic_index_in_dim(stack, z ^ k, 0, False) for k in range(4)], axis=0)

    def assemble(own):
        own = own[: shard // 2]
        other = swap(own, "sp", 1)
        out = jnp.concatenate(
            [jnp.where(core == 0, own, other), jnp.where(core == 0, other, own)], axis=0
        )
        return out.astype(F32)

    gots = [swap(kv.astype(BF), "sp", 2 * k) for k in (1, 2, 3)]
    d_val, *parts_v = weight_grads(
        dval_of, "d_w_value", scal, t_own, t_other, [key], [key_other], [gs], feat_scale, [kv]
    )
    *gots, val_other, d_val, p0, p1, p2, p3 = together(*gots, val_other, d_val, *parts_v)
    parts_v = [p0, p1, p2, p3]
    for got in gots:
        kv = kv + got.astype(F32)
    near_v = reduce_near(parts_v)
    (gn,) = attention(norm_kernel, "grad_norm", qs, cot, [kn, kv], 0, 1, 5)
    gn = add(add(add(gn, 1), 2), 4)
    n0, n1, n2, n3, gn = together(*near_v, gn)
    half_v = add_near(n0, n1, n2, n3)
    d_key, *parts_k = weight_grads(
        dkey_of, "d_w_key", scal, t_own, t_other, [key, val], [key_other, val_other], [gs, gn], feat_scale,
        half_v[2:],
    )
    near_k = reduce_near(parts_k)
    far_v = reduce_far(*half_v)
    own_v = merge(*far_v)
    attended, d_queries = attention(
        attend_kernel, "attend", qs, cot, [kn, kv], 2, 0, 11, [half_v[2], half_v[3]]
    )
    *near_k, attended = together(*near_k, attended)
    half_k = add_near(*near_k)
    far_k = reduce_far(*half_k)
    half_z = part_of(own_v, z0)
    got_v = swap(part_of(own_v, 1 - z0).astype(BF), "sp", 2)
    *far_k, got_v = together(*far_k, got_v)
    mine_k, sends_k, gots_k = reduce_z(merge(*far_k))
    got_v, *sends = together(got_v, *sends_k)
    half_z = half_z + got_v.astype(F32)
    give_v = part_of(half_z, 1 - z1).astype(BF)
    got_v = swap(give_v, "sp", 4)
    d_tokens = input_grads(
        scal, d_key, d_val, keys_near + keys_far, vals_near + vals_far, spots, shard, depth, sends + [give_v]
    )
    *gots_k, d_tokens, got_v = together(*gots_k, d_tokens, got_v)
    quart_k = spread_z(mine_k, gots_k)
    quart_v = ((part_of(half_z, z1) + got_v.astype(F32)) * scale).astype(BF)
    half_v = joined(quart_v, swap(quart_v, "sp", 4), z1)
    whole_v = joined(half_v, swap(half_v, "sp", 2), z0)
    d_w_value = assemble(whole_v)
    d_w_key = assemble(ordered(quart_k))
    return attended.T[None], d_tokens.T[None], d_queries.T[None], d_w_key, d_w_value


def body_general(tokens, queries, w_key, w_value, cotangent):
    tok, qs, cot = tokens[0], queries[0].T, cotangent[0].T
    count = tok.shape[0]
    full = w_key.shape[1]
    tile = tile_of(count)
    tok_img = count * lax.axis_size("sp")
    feat_scale = float(tok_img)
    scale = 1.0 / (lax.axis_size("img") * tok_img) ** 0.5
    keys, vals = (lax.all_gather(w, "img", axis=0, tiled=True) for w in (w_key, w_value))
    key = jnp.maximum(dot(tok, keys, 1, 0), 0.0).astype(BF)
    val = dot(tok, vals, 1, 0).astype(BF)
    by_head = (count, full // HD, HD)
    kv = jnp.einsum("thj,thi->jhi", val.reshape(by_head), key.reshape(by_head), preferred_element_type=F32)
    kv = lax.psum(kv.reshape(HD, full), "sp")
    kn = lax.psum(jnp.sum(key.astype(F32), axis=0, keepdims=True), "sp")
    (gs,) = attention(grad_kernel, "grad_state", qs, cot, [kn], 0, HD, 4)
    gs = lax.psum(gs, "sp")
    (d_val,) = feature_grads(dval_of, "d_value", [key], [gs], feat_scale)
    (gn,) = attention(norm_kernel, "grad_norm", qs, cot, [kn, kv], 0, 1, 5)
    attended, d_queries = attention(attend_kernel, "attend", qs, cot, [kn, kv], 2, 0, 11)
    gn = lax.psum(gn, "sp")
    (d_key,) = feature_grads(dkey_of, "d_key", [key, val], [gs, gn], feat_scale)
    back = [dot(w, d[:, :full], 1, 1) for w, d in ((keys, d_key), (vals, d_val))]
    d_tokens = (back[0] + back[1]).astype(BF)
    out = []
    for d in (d_key, d_val):
        part = lax.psum_scatter(dot(tok, d[:, :full], 0, 0), "img", scatter_dimension=0, tiled=True)
        out.append(lax.psum(part, "sp") * scale)
    return attended.T[None], d_tokens.T[None], d_queries.T[None], *out


def solution(mesh):
    in_specs = (
        P("img", "sp", None),
        P("img", "sp", None),
        P("img", None),
        P("img", None),
        P("img", "sp", None),
    )
    out_specs = (
        P("img", "sp", None),
        P("img", "sp", None),
        P("img", "sp", None),
        P("img", None),
        P("img", None),
    )
    cubes = mesh.shape["img"] == 4 and mesh.shape["sp"] == 8
    body = body_exchange if cubes else body_general
    return jax.shard_map(body, mesh=mesh, in_specs=in_specs, out_specs=out_specs, check_vma=False)
```

time: 637 us -> 219 us (0.34)
  waiting for transfers between devices: 428 us -> 61 us
  Pallas kernels: 0 us -> 91.6 us
  matrix products: 85.5 us -> 0 us
  blocking collectives: 54.9 us -> 0 us
  starting transfers between devices: 0.2 us -> 52.8 us
  local copies, waits for them, and re-layouts: 41 us -> 2.93 us
  between operations: 14.2 us -> 1.43 us
    unnamed x6 -> x0, waiting for transfers between devices: 183 us -> none
    psum x2 -> x0, waiting for transfers between devices: 163 us -> none  [the longest x1 104 us: body(): grad_whole = lax.psum(grad_shard, 'sp')]
    pallas_call x0 -> x11, Pallas kernels: none -> 91.6 us  [call(): pl.pallas_call(run, grid_spec=pltpu.PrefetchScalarGridSpec(num_scalar_pre...]
    dot_general x13 -> x0, matrix products: 85.5 us -> none  [the longest x1 14.5 us: body(): lax.dot_general(tok_rows, d_both, tok_dims, preferred_element_type=jnp.fl...]
    all_gather x2 -> x0, waiting for transfers between devices: 81 us -> none  [the longest x1 60.9 us: body(): lax.all_gather(w_key, 'img', axis=0, tiled=True)]
    ppermute x0 -> x52, waiting for transfers between devices: none -> 61 us  [swap(): return lax.ppermute(x, axis, [(i, i ^ bit) for i in range(n)])]
    psum x2 -> x0, blocking collectives: 54.9 us -> none  [the longest x1 28.7 us: body(): kv_state, key_norm = lax.psum((state_part, norm_part), 'sp')]
    ppermute x0 -> x52, starting transfers between devices: none -> 52.8 us  [swap(): return lax.ppermute(x, axis, [(i, i ^ bit) for i in range(n)])]
  transfers between devices with their start and end apart: 5 -> 52, of which waited for: 5 -> 27; matrix products, arithmetic and copies ran while one was open for 6% -> 2% of each run, Pallas kernels for 0% -> 40%
where the time goes in v2:
time: 219 us
  Pallas kernels  91.6 us (42%)
  waiting for transfers between devices  61 us (28%)
  starting transfers between devices  52.8 us (24%)
  other arithmetic  9.12 us (4%)
  local copies, waits for them, and re-layouts  2.93 us (1%)
    pallas_call x11, Pallas kernels, call(): pl.pallas_call(run, grid_spec=pltpu.PrefetchScalarGridSpec(num_scalar_pre...  91.6 us
    ppermute x52, waiting for transfers between devices, swap(): return lax.ppermute(x, axis, [(i, i ^ bit) for i in range(n)])  61 us
    ppermute x52, starting transfers between devices, swap(): return lax.ppermute(x, axis, [(i, i ^ bit) for i in range(n)])  52.8 us
  transfers between devices with their start and end apart: 52, of which 27 were waited for; matrix products, arithmetic and copies ran while one was open for 2% of the time, Pallas kernels for 40%

profile of v2, /device:TPU:0, one launch (start us, length us, event | category | flops | bytes accessed | tf_op | source)
XLA Modules:
  0.0 218.9 jit_solution(9469052697187351276)
XLA Ops:
  2.0 3.0 %collective-permute-start.1 = (bf16[288,1120]{1,0:T(8,128)(2,1)S(1)}, bf16[288,1120]{1,0:T(8,128)(2,1)S(1)}, u32[]{:S(2)}, u32[]{:S(2)}) collective-permute-start(bf16[288,1120]{1,0:T(8,128)(2,1)S(1)} %slice_select_fusion.1), channel_id=1, source_target_pairs={{0,16},{8,24},{16,0},{24,8},{1,17},{9,25},{17,1},{25,9},{2,18},{10... | collective-permute-start | bytes 1935368 | tf_op jit(solution)/shard_map/ppermute | solution.py:470
  8.8 3.8 %token_rows.1 = (bf16[896,1680]{1,0:T(8,128)(2,1)S(1)}, bf16[896,560]{1,0:T(8,128)(2,1)S(1)}, bf16[4,280,896]{2,1,0:T(8,128)(2,1)}) custom-call(s32[2]{0:T(128)S(1)} %pad_add_fusion.refs_0_, bf16[4,560,896]{2,1,0:T(8,128)(2,1)S(1)} %bitcast.89), custom_call_target="tpu_custom_call" | custom-call | bytes 12042240 | tf_op jit(solution)/shard_map/token_rows/pallas_call | solution.py:64
  12.6 7.4 %collective-permute-done.1.refs_5_.refs_6_ = bf16[288,1120]{1,0:T(8,128)(2,1)S(1)} collective-permute-done((bf16[288,1120]{1,0:T(8,128)(2,1)S(1)}, bf16[288,1120]{1,0:T(8,128)(2,1)S(1)}, u32[]{:S(2)}, u32[]{:S(2)}) %collective-permute-start.1) | collective-permute-done | bytes 645152 | tf_op jit(solution)/shard_map/ppermute | solution.py:470
  27.0 6.3 %key_near.1.refs_2_ = f32[896,1120]{1,0:T(8,128)S(1)} custom-call(s32[2]{0:T(128)S(1)} %pad_add_fusion.refs_0_, bf16[896,1680]{1,0:T(8,128)(2,1)S(1)} %get-tuple-element.90.refs_1_, bf16[560,1120]{1,0:T(8,128)(2,1)S(1)} %copy-done.2, bf16[288,1120]{1,0:T(8,128)(2,1)S(1)} %collective-permute-done.refs_3_.refs_4_, ...), custom_call_target="tpu_custom_call" | custom-call | flops 3371827200 | bytes 12794880 | tf_op jit(solution)/shard_map/key_near/pallas_call | solution.py:64
  35.5 3.1 %key_feat.1 = (bf16[896,1152]{1,0:T(8,128)(2,1)S(1)}, f32[1,1120]{1,0:T(1,128)S(1)}) custom-call(s32[2]{0:T(128)S(1)} %pad_add_fusion.refs_0_, bf16[896,560]{1,0:T(8,128)(2,1)S(1)} %get-tuple-element.93.refs_1_, f32[896,1120]{1,0:T(8,128)S(1)} %key_near.1.refs_2_, bf16[144,1120]{1,0:T(8,128)(2,1)S(1)} %collective-permute-done.2.refs_3_.refs_8_, ...), custom_call_target="tpu_custom_call" | custom-call | flops 1123942400 | bytes 8279040 | tf_op jit(solution)/shard_map/key_feat/pallas_call | solution.py:64
  45.9 2.6 %collective-permute-start.11 = (f32[1,1120]{1,0:T(1,128)S(1)}, f32[1,1120]{1,0:T(1,128)S(1)}, u32[]{:S(2)}, u32[]{:S(2)}) collective-permute-start(f32[1,1120]{1,0:T(1,128)S(1)} %add.123), channel_id=1, source_target_pairs={{0,4},{1,5},{2,6},{3,7},{4,0},{5,1},{6,2},{7,3},{8,12},{9,13},{10,... | collective-permute-start | bytes 13448 | tf_op jit(solution)/shard_map/ppermute | solution.py:470
  50.5 6.8 %collective-permute-done.13.refs_5_.refs_15_ = bf16[288,1120]{1,0:T(8,128)(2,1)S(1)} collective-permute-done((bf16[288,1120]{1,0:T(8,128)(2,1)S(1)}, bf16[288,1120]{1,0:T(8,128)(2,1)S(1)}, u32[]{:S(2)}, u32[]{:S(2)}) %collective-permute-start.13) | collective-permute-done | bytes 645152 | tf_op jit(solution)/shard_map/ppermute | solution.py:470
  57.6 4.2 %grad_state.1 = f32[32,1120]{1,0:T(8,128)S(1)} custom-call(bf16[1120,896]{1,0:T(8,128)(2,1)S(1)} %bitcast.90, bf16[1120,896]{1,0:T(8,128)(2,1)S(1)} %bitcast.93, f32[1,1120]{1,0:T(1,128)S(1)} %add.124.refs_2_), custom_call_target="tpu_custom_call" | custom-call | flops 2055208960 | bytes 4014080 | tf_op jit(solution)/shard_map/grad_state/pallas_call | solution.py:64
  68.3 6.3 %val_near.1.refs_2_ = f32[896,1120]{1,0:T(8,128)S(1)} custom-call(s32[2]{0:T(128)S(1)} %pad_add_fusion.refs_0_, bf16[896,1680]{1,0:T(8,128)(2,1)S(1)} %get-tuple-element.90.refs_1_, bf16[560,1120]{1,0:T(8,128)(2,1)S(1)} %copy-done.3, bf16[288,1120]{1,0:T(8,128)(2,1)S(1)} %collective-permute-done.12.refs_3_.refs_13_, ...), custom_call_target="tpu_custom_call" | custom-call | flops 3371827200 | bytes 12794880 | tf_op jit(solution)/shard_map/val_near/pallas_call | solution.py:64
  75.6 2.7 %collective-permute-start.21 = (bf16[32,1120]{1,0:T(8,128)(2,1)S(1)}, bf16[32,1120]{1,0:T(8,128)(2,1)S(1)}, u32[]{:S(2)}, u32[]{:S(2)}) collective-permute-start(bf16[32,1120]{1,0:T(8,128)(2,1)S(1)} %fusion.17), channel_id=1, source_target_pairs={{0,4},{1,5},{2,6},{3,7},{4,0},{5,1},{6,2},{7,3},{8,12},{9,13},{10,... | collective-permute-start | bytes 215048 | tf_op jit(solution)/shard_map/ppermute | solution.py:470
  78.3 3.8 %val_feat.1 = (bf16[896,1152]{1,0:T(8,128)(2,1)S(1)}, f32[32,1120]{1,0:T(8,128)S(1)}) custom-call(s32[2]{0:T(128)S(1)} %pad_add_fusion.refs_0_, bf16[896,560]{1,0:T(8,128)(2,1)S(1)} %get-tuple-element.93.refs_1_, f32[896,1120]{1,0:T(8,128)S(1)} %val_near.1.refs_2_, bf16[896,1152]{1,0:T(8,128)(2,1)S(1)} %get-tuple-element.99.refs_3_, ...), custom_call_target="tpu_custom_call" | custom-call | flops 1123942400 | bytes 8279040 | tf_op jit(solution)/shard_map/val_feat/pallas_call | solution.py:64
  84.1 3.5 %collective-permute-start.27 = (bf16[32,1120]{1,0:T(8,128)(2,1)S(1)}, bf16[32,1120]{1,0:T(8,128)(2,1)S(1)}, u32[]{:S(2)}, u32[]{:S(2)}) collective-permute-start(bf16[32,1120]{1,0:T(8,128)(2,1)S(1)} %convert_element_type.123), channel_id=1, source_target_pairs={{0,6},{1,7},{2,4},{3,5},{4,2},{5,3},{6,0},{7,1},{8,14},{9,15},{10,... | collective-permute-start | bytes 215048 | tf_op jit(solution)/shard_map/ppermute | solution.py:470
  88.6 14.8 %d_w_value.1 = (bf16[896,1152]{1,0:T(8,128)(2,1)}, bf16[2,144,1120]{2,1,0:T(8,128)(2,1)}, bf16[2,136,1120]{2,1,0:T(8,128)(2,1)}, f32[2,144,1120]{2,1,0:T(8,128)S(1)}, f32[2,136,1120]{2,1,0:T(8,128)S(1)}) custom-call(s32[2]{0:T(128)S(1)} %pad_add_fusion.refs_0_, bf16[8,280,896]{2,1,0:T(8,128)(2,1)} %bitcast.87, ...), custom_call_target="tpu_custom_call" | custom-call | flops 4495769600 | bytes 11791360 | tf_op jit(solution)/shard_map/d_w_value/pallas_call | solution.py:64
  106.5 5.8 %grad_norm.1 = f32[1,1120]{1,0:T(1,128)S(1)} custom-call(bf16[1120,896]{1,0:T(8,128)(2,1)S(1)} %bitcast.91, bf16[1120,896]{1,0:T(8,128)(2,1)S(1)} %bitcast.94, f32[1,1120]{1,0:T(1,128)S(1)} %add.124.refs_2_, f32[32,1120]{1,0:T(8,128)S(1)} %convert_add_fusion.6.refs_3_), custom_call_target="tpu_custom_call" | custom-call | flops 2569011200 | bytes 4014080 | tf_op jit(solution)/shard_map/grad_norm/pallas_call | solution.py:64
  114.5 2.6 %collective-permute-done.32 = f32[1,1120]{1,0:T(1,128)S(1)} collective-permute-done((f32[1,1120]{1,0:T(1,128)S(1)}, f32[1,1120]{1,0:T(1,128)S(1)}, u32[]{:S(2)}, u32[]{:S(2)}) %collective-permute-start.32) | collective-permute-done | bytes 4512 | tf_op jit(solution)/shard_map/ppermute | solution.py:470
  126.0 15.2 %d_w_key.1 = (bf16[896,1152]{1,0:T(8,128)(2,1)}, bf16[2,144,1120]{2,1,0:T(8,128)(2,1)S(1)}, bf16[2,136,1120]{2,1,0:T(8,128)(2,1)S(1)}, f32[2,144,1120]{2,1,0:T(8,128)S(1)}, f32[2,136,1120]{2,1,0:T(8,128)S(1)}) custom-call(s32[2]{0:T(128)S(1)} %pad_add_fusion.refs_0_, bf16[8,280,896]{2,1,0:T(8,128)(2,1)} %bitcast.88, ...), custom_call_target="tpu_custom_call" | custom-call | flops 4495769600 | bytes 15805440 | tf_op jit(solution)/shard_map/d_w_key/pallas_call | solution.py:64
  143.6 9.7 %attend.1 = (bf16[1120,896]{1,0:T(8,128)(2,1)}, bf16[1120,896]{1,0:T(8,128)(2,1)}) custom-call(bf16[1120,896]{1,0:T(8,128)(2,1)S(1)} %bitcast.92, bf16[1120,896]{1,0:T(8,128)(2,1)S(1)} %bitcast.95, f32[1,1120]{1,0:T(1,128)S(1)} %add.124.refs_2_, f32[32,1120]{1,0:T(8,128)S(1)} %convert_add_fusion.6.refs_3_, bf16[144,1120]{1,0:T(8,128)(2,1)S(1)} %fusion.3.refs_9_.refs_4_, ...), custom_call_target="tpu_custom_call" | custom-call | flops 5651824640 | bytes 8028160 | tf_op jit(solution)/shard_map/attend/pallas_call | solution.py:64
  160.8 3.8 %collective-permute-done.37 = bf16[136,1120]{1,0:T(8,128)(2,1)S(1)} collective-permute-done((bf16[136,1120]{1,0:T(8,128)(2,1)S(1)}, bf16[136,1120]{1,0:T(8,128)(2,1)S(1)}, u32[]{:S(2)}, u32[]{:S(2)}) %collective-permute-start.37) | collective-permute-done | bytes 304672 | tf_op jit(solution)/shard_map/ppermute | solution.py:470
  166.2 3.5 %collective-permute-start.43 = (bf16[72,1120]{1,0:T(8,128)(2,1)S(1)}, bf16[72,1120]{1,0:T(8,128)(2,1)S(1)}, u32[]{:S(2)}, u32[]{:S(2)}) collective-permute-start(bf16[72,1120]{1,0:T(8,128)(2,1)S(1)} %get-tuple-element.157.refs_23_), channel_id=1, source_target_pairs={{0,6},{1,7},{2,4},{3,5},{4,2},{5,3},{6,0},{7,1},{8,14},{9,15},{10,... | collective-permute-start | bytes 483848 | tf_op jit(solution)/shard_map/ppermute | solution.py:470
  172.8 18.8 %d_tokens.1 = bf16[2240,896]{1,0:T(8,128)(2,1)} custom-call(s32[2]{0:T(128)} %copy-done.16, bf16[896,1152]{1,0:T(8,128)(2,1)} %get-tuple-element.152.refs_1_, bf16[896,1152]{1,0:T(8,128)(2,1)} %get-tuple-element.153.refs_2_, bf16[560,1120]{1,0:T(8,128)(2,1)} %refs_3_.1, bf16[288,1120]{1,0:T(8,128)(2,1)} %copy-done.13, bf16[288,1120]{1,0:T(8,128)(2,1)} %copy-done.25, ...), custom_call_target="tpu_custom_call" | custom-call | flops 8991539200 | bytes 18063360 | tf_op jit(solution)/shard_map/d_tokens/pallas_call | solution.py:64
  192.8 3.5 %collective-permute-start.47 = (bf16[72,1120]{1,0:T(8,128)(2,1)S(1)}, bf16[72,1120]{1,0:T(8,128)(2,1)S(1)}, u32[]{:S(2)}, u32[]{:S(2)}) collective-permute-start(bf16[72,1120]{1,0:T(8,128)(2,1)S(1)} %fusion.10), channel_id=1, source_target_pairs={{0,6},{1,7},{2,4},{3,5},{4,2},{5,3},{6,0},{7,1},{8,14},{9,15},{10,... | collective-permute-start | bytes 483848 | tf_op jit(solution)/shard_map/ppermute | solution.py:470
  197.2 6.3 %collective-permute-done.49 = bf16[72,1120]{1,0:T(8,128)(2,1)S(1)} collective-permute-done((bf16[72,1120]{1,0:T(8,128)(2,1)S(1)}, bf16[72,1120]{1,0:T(8,128)(2,1)S(1)}, u32[]{:S(2)}, u32[]{:S(2)}) %collective-permute-start.49) | collective-permute-done | bytes 161312 | tf_op jit(solution)/shard_map/ppermute | solution.py:470
  203.8 7.1 %collective-permute-done.46 = bf16[72,1120]{1,0:T(8,128)(2,1)S(1)} collective-permute-done((bf16[72,1120]{1,0:T(8,128)(2,1)S(1)}, bf16[72,1120]{1,0:T(8,128)(2,1)S(1)}, u32[]{:S(2)}, u32[]{:S(2)}) %collective-permute-start.46) | collective-permute-done | bytes 161312 | tf_op jit(solution)/shard_map/ppermute | solution.py:470
  211.2 3.6 %collective-permute-done.50 = bf16[144,1120]{1,0:T(8,128)(2,1)S(1)} collective-permute-done((bf16[144,1120]{1,0:T(8,128)(2,1)S(1)}, bf16[144,1120]{1,0:T(8,128)(2,1)S(1)}, u32[]{:S(2)}, u32[]{:S(2)}) %collective-permute-start.50) | collective-permute-done | bytes 322592 | tf_op jit(solution)/shard_map/ppermute | solution.py:470
  (213 shorter events, 69.6 us)
Async XLA Ops:
  2.0 17.9 %collective-permute-start.1 = (bf16[288,1120]{1,0:T(8,128)(2,1)S(1)}, bf16[288,1120]{1,0:T(8,128)(2,1)S(1)}, u32[]{:S(2)}, u32[]{:S(2)}) collective-permute-start(bf16[288,1120]{1,0:T(8,128)(2,1)S(1)} %slice_select_fusion.1), channel_id=1, source_target_pairs={{0,16},{8,24},{16,0},{24,8},{1,17},{9,25},{17,1},{25,9},{2,18},{10... | collective-permute-start | bytes 1935368 | tf_op jit(solution)/shard_map/ppermute | solution.py:470
  5.1 16.4 %collective-permute-start = (bf16[288,1120]{1,0:T(8,128)(2,1)S(1)}, bf16[288,1120]{1,0:T(8,128)(2,1)S(1)}, u32[]{:S(2)}, u32[]{:S(2)}) collective-permute-start(bf16[288,1120]{1,0:T(8,128)(2,1)S(1)} %slice_select_fusion.1), channel_id=1, source_target_pairs={{0,8},{8,0},{16,24},{24,16},{1,9},{9,1},{17,25},{25,17},{2,10},{10... | collective-permute-start | bytes 1935368 | tf_op jit(solution)/shard_map/ppermute | solution.py:470
  21.4 11.9 %collective-permute-start.6 = (bf16[4,280,896]{2,1,0:T(8,128)(2,1)}, bf16[4,280,896]{2,1,0:T(8,128)(2,1)}, u32[]{:S(2)}, u32[]{:S(2)}) collective-permute-start(bf16[4,280,896]{2,1,0:T(8,128)(2,1)} %get-tuple-element.91), channel_id=1, source_target_pairs={{0,1},{1,0},{2,3},{3,2},{4,5},{5,4},{6,7},{7,6},{8,9},{9,8},{10,11... | collective-permute-start | bytes 6021128 | tf_op jit(solution)/shard_map/ppermute | solution.py:470
  40.0 35.0 %collective-permute-start.20 = (bf16[896,1152]{1,0:T(8,128)(2,1)S(1)}, bf16[896,1152]{1,0:T(8,128)(2,1)S(1)}, u32[]{:S(2)}, u32[]{:S(2)}) collective-permute-start(bf16[896,1152]{1,0:T(8,128)(2,1)S(1)} %get-tuple-element.99.refs_3_), channel_id=1, source_target_pairs={{0,1},{1,0},{2,3},{3,2},{4,5},{5,4},{6,7},{7,6},{8,9},{9,8},{10,11... | collective-permute-start | bytes 6193160 | tf_op jit(solution)/shard_map/ppermute | solution.py:470
  40.3 17.0 %collective-permute-start.13 = (bf16[288,1120]{1,0:T(8,128)(2,1)S(1)}, bf16[288,1120]{1,0:T(8,128)(2,1)S(1)}, u32[]{:S(2)}, u32[]{:S(2)}) collective-permute-start(bf16[288,1120]{1,0:T(8,128)(2,1)S(1)} %slice_select_fusion), channel_id=1, source_target_pairs={{0,16},{8,24},{16,0},{24,8},{1,17},{9,25},{17,1},{25,9},{2,18},{10... | collective-permute-start | bytes 1935368 | tf_op jit(solution)/shard_map/ppermute | solution.py:470
  40.7 16.9 %collective-permute-start.12 = (bf16[288,1120]{1,0:T(8,128)(2,1)S(1)}, bf16[288,1120]{1,0:T(8,128)(2,1)S(1)}, u32[]{:S(2)}, u32[]{:S(2)}) collective-permute-start(bf16[288,1120]{1,0:T(8,128)(2,1)S(1)} %slice_select_fusion), channel_id=1, source_target_pairs={{0,8},{8,0},{16,24},{24,16},{1,9},{9,1},{17,25},{25,17},{2,10},{10... | collective-permute-start | bytes 1935368 | tf_op jit(solution)/shard_map/ppermute | solution.py:470
  62.5 12.1 %collective-permute-start.18 = (bf16[144,1120]{1,0:T(8,128)(2,1)S(1)}, bf16[144,1120]{1,0:T(8,128)(2,1)S(1)}, u32[]{:S(2)}, u32[]{:S(2)}) collective-permute-start(bf16[144,1120]{1,0:T(8,128)(2,1)S(1)} %slice.64), channel_id=1, source_target_pairs={{0,8},{8,0},{16,24},{24,16},{1,9},{9,1},{17,25},{25,17},{2,10},{10... | collective-permute-start | bytes 967688 | tf_op jit(solution)/shard_map/ppermute | solution.py:470
  83.9 19.5 %collective-permute-start.28 = (bf16[896,1152]{1,0:T(8,128)(2,1)S(1)}, bf16[896,1152]{1,0:T(8,128)(2,1)S(1)}, u32[]{:S(2)}, u32[]{:S(2)}) collective-permute-start(bf16[896,1152]{1,0:T(8,128)(2,1)S(1)} %get-tuple-element.116.refs_4_), channel_id=1, source_target_pairs={{0,1},{1,0},{2,3},{3,2},{4,5},{5,4},{6,7},{7,6},{8,9},{9,8},{10,11... | collective-permute-start | bytes 6193160 | tf_op jit(solution)/shard_map/ppermute | solution.py:470
  84.1 19.3 %collective-permute-start.27 = (bf16[32,1120]{1,0:T(8,128)(2,1)S(1)}, bf16[32,1120]{1,0:T(8,128)(2,1)S(1)}, u32[]{:S(2)}, u32[]{:S(2)}) collective-permute-start(bf16[32,1120]{1,0:T(8,128)(2,1)S(1)} %convert_element_type.123), channel_id=1, source_target_pairs={{0,6},{1,7},{2,4},{3,5},{4,2},{5,3},{6,0},{7,1},{8,14},{9,15},{10,... | collective-permute-start | bytes 215048 | tf_op jit(solution)/shard_map/ppermute | solution.py:470
  87.6 15.8 %collective-permute-start.26 = (bf16[32,1120]{1,0:T(8,128)(2,1)S(1)}, bf16[32,1120]{1,0:T(8,128)(2,1)S(1)}, u32[]{:S(2)}, u32[]{:S(2)}) collective-permute-start(bf16[32,1120]{1,0:T(8,128)(2,1)S(1)} %convert_element_type.123), channel_id=1, source_target_pairs={{0,4},{1,5},{2,6},{3,7},{4,0},{5,1},{6,2},{7,3},{8,12},{9,13},{10,... | collective-permute-start | bytes 215048 | tf_op jit(solution)/shard_map/ppermute | solution.py:470
  87.6 15.8 %collective-permute-start.25 = (bf16[32,1120]{1,0:T(8,128)(2,1)S(1)}, bf16[32,1120]{1,0:T(8,128)(2,1)S(1)}, u32[]{:S(2)}, u32[]{:S(2)}) collective-permute-start(bf16[32,1120]{1,0:T(8,128)(2,1)S(1)} %convert_element_type.123), channel_id=1, source_target_pairs={{0,2},{1,3},{2,0},{3,1},{4,6},{5,7},{6,4},{7,5},{8,10},{9,11},{10,... | collective-permute-start | bytes 215048 | tf_op jit(solution)/shard_map/ppermute | solution.py:470
  103.4 18.2 %collective-permute-start.30 = (bf16[2,136,1120]{2,1,0:T(8,128)(2,1)}, bf16[2,136,1120]{2,1,0:T(8,128)(2,1)}, u32[]{:S(2)}, u32[]{:S(2)}) collective-permute-start(bf16[2,136,1120]{2,1,0:T(8,128)(2,1)} %get-tuple-element.127), channel_id=1, source_target_pairs={{0,16},{8,24},{16,0},{24,8},{1,17},{9,25},{17,1},{25,9},{2,18},{10... | collective-permute-start | bytes 1827848 | tf_op jit(solution)/shard_map/ppermute | solution.py:470
  104.9 16.7 %collective-permute-start.29 = (bf16[2,144,1120]{2,1,0:T(8,128)(2,1)}, bf16[2,144,1120]{2,1,0:T(8,128)(2,1)}, u32[]{:S(2)}, u32[]{:S(2)}) collective-permute-start(bf16[2,144,1120]{2,1,0:T(8,128)(2,1)} %get-tuple-element.126), channel_id=1, source_target_pairs={{0,8},{8,0},{16,24},{24,16},{1,9},{9,1},{17,25},{25,17},{2,10},{10... | collective-permute-start | bytes 1935368 | tf_op jit(solution)/shard_map/ppermute | solution.py:470
  122.9 30.3 %collective-permute-start.39 = (bf16[136,1120]{1,0:T(8,128)(2,1)S(1)}, bf16[136,1120]{1,0:T(8,128)(2,1)S(1)}, u32[]{:S(2)}, u32[]{:S(2)}) collective-permute-start(bf16[136,1120]{1,0:T(8,128)(2,1)S(1)} %fusion.11.refs_10_.refs_5_), channel_id=1, source_target_pairs={{0,8},{8,0},{16,24},{24,16},{1,9},{9,1},{17,25},{25,17},{2,10},{10... | collective-permute-start | bytes 913928 | tf_op jit(solution)/shard_map/ppermute | solution.py:470
  125.4 28.0 %collective-permute-start.38 = (bf16[144,1120]{1,0:T(8,128)(2,1)S(1)}, bf16[144,1120]{1,0:T(8,128)(2,1)S(1)}, u32[]{:S(2)}, u32[]{:S(2)}) collective-permute-start(bf16[144,1120]{1,0:T(8,128)(2,1)S(1)} %fusion.3.refs_9_.refs_4_), channel_id=1, source_target_pairs={{0,16},{8,24},{16,0},{24,8},{1,17},{9,25},{17,1},{25,9},{2,18},{10... | collective-permute-start | bytes 967688 | tf_op jit(solution)/shard_map/ppermute | solution.py:470
  141.2 14.0 %collective-permute-start.35 = (bf16[2,136,1120]{2,1,0:T(8,128)(2,1)S(1)}, bf16[2,136,1120]{2,1,0:T(8,128)(2,1)S(1)}, u32[]{:S(2)}, u32[]{:S(2)}) collective-permute-start(bf16[2,136,1120]{2,1,0:T(8,128)(2,1)S(1)} %get-tuple-element.139), channel_id=1, source_target_pairs={{0,16},{8,24},{16,0},{24,8},{1,17},{9,25},{17,1},{25,9},{2,18},{10... | collective-permute-start | bytes 1827848 | tf_op jit(solution)/shard_map/ppermute | solution.py:470
  142.6 14.6 %collective-permute-start.34 = (bf16[2,144,1120]{2,1,0:T(8,128)(2,1)S(1)}, bf16[2,144,1120]{2,1,0:T(8,128)(2,1)S(1)}, u32[]{:S(2)}, u32[]{:S(2)}) collective-permute-start(bf16[2,144,1120]{2,1,0:T(8,128)(2,1)S(1)} %get-tuple-element.138), channel_id=1, source_target_pairs={{0,8},{8,0},{16,24},{24,16},{1,9},{9,1},{17,25},{25,17},{2,10},{10... | collective-permute-start | bytes 1935368 | tf_op jit(solution)/shard_map/ppermute | solution.py:470
  166.2 25.4 %collective-permute-start.43 = (bf16[72,1120]{1,0:T(8,128)(2,1)S(1)}, bf16[72,1120]{1,0:T(8,128)(2,1)S(1)}, u32[]{:S(2)}, u32[]{:S(2)}) collective-permute-start(bf16[72,1120]{1,0:T(8,128)(2,1)S(1)} %get-tuple-element.157.refs_23_), channel_id=1, source_target_pairs={{0,6},{1,7},{2,4},{3,5},{4,2},{5,3},{6,0},{7,1},{8,14},{9,15},{10,... | collective-permute-start | bytes 483848 | tf_op jit(solution)/shard_map/ppermute | solution.py:470
  169.6 21.9 %collective-permute-start.42 = (bf16[72,1120]{1,0:T(8,128)(2,1)S(1)}, bf16[72,1120]{1,0:T(8,128)(2,1)S(1)}, u32[]{:S(2)}, u32[]{:S(2)}) collective-permute-start(bf16[72,1120]{1,0:T(8,128)(2,1)S(1)} %get-tuple-element.156.refs_22_), channel_id=1, source_target_pairs={{0,4},{1,5},{2,6},{3,7},{4,0},{5,1},{6,2},{7,3},{8,12},{9,13},{10,... | collective-permute-start | bytes 483848 | tf_op jit(solution)/shard_map/ppermute | solution.py:470
  169.6 21.9 %collective-permute-start.41 = (bf16[72,1120]{1,0:T(8,128)(2,1)S(1)}, bf16[72,1120]{1,0:T(8,128)(2,1)S(1)}, u32[]{:S(2)}, u32[]{:S(2)}) collective-permute-start(bf16[72,1120]{1,0:T(8,128)(2,1)S(1)} %get-tuple-element.155.refs_21_), channel_id=1, source_target_pairs={{0,2},{1,3},{2,0},{3,1},{4,6},{5,7},{6,4},{7,5},{8,10},{9,11},{10,... | collective-permute-start | bytes 483848 | tf_op jit(solution)/shard_map/ppermute | solution.py:470
  170.7 20.8 %collective-permute-start.44 = (bf16[72,1120]{1,0:T(8,128)(2,1)S(1)}, bf16[72,1120]{1,0:T(8,128)(2,1)S(1)}, u32[]{:S(2)}, u32[]{:S(2)}) collective-permute-start(bf16[72,1120]{1,0:T(8,128)(2,1)S(1)} %fusion.16.refs_24_), channel_id=1, source_target_pairs={{0,4},{1,5},{2,6},{3,7},{4,0},{5,1},{6,2},{7,3},{8,12},{9,13},{10,... | collective-permute-start | bytes 483848 | tf_op jit(solution)/shard_map/ppermute | solution.py:470
  191.6 11.9 %collective-permute-start.49 = (bf16[72,1120]{1,0:T(8,128)(2,1)S(1)}, bf16[72,1120]{1,0:T(8,128)(2,1)S(1)}, u32[]{:S(2)}, u32[]{:S(2)}) collective-permute-start(bf16[72,1120]{1,0:T(8,128)(2,1)S(1)} %fusion.6), channel_id=1, source_target_pairs={{0,4},{1,5},{2,6},{3,7},{4,0},{5,1},{6,2},{7,3},{8,12},{9,13},{10,... | collective-permute-start | bytes 483848 | tf_op jit(solution)/shard_map/ppermute | solution.py:470
  196.3 14.6 %collective-permute-start.46 = (bf16[72,1120]{1,0:T(8,128)(2,1)S(1)}, bf16[72,1120]{1,0:T(8,128)(2,1)S(1)}, u32[]{:S(2)}, u32[]{:S(2)}) collective-permute-start(bf16[72,1120]{1,0:T(8,128)(2,1)S(1)} %fusion.10), channel_id=1, source_target_pairs={{0,4},{1,5},{2,6},{3,7},{4,0},{5,1},{6,2},{7,3},{8,12},{9,13},{10,... | collective-permute-start | bytes 483848 | tf_op jit(solution)/shard_map/ppermute | solution.py:470
  196.3 14.6 %collective-permute-start.45 = (bf16[72,1120]{1,0:T(8,128)(2,1)S(1)}, bf16[72,1120]{1,0:T(8,128)(2,1)S(1)}, u32[]{:S(2)}, u32[]{:S(2)}) collective-permute-start(bf16[72,1120]{1,0:T(8,128)(2,1)S(1)} %fusion.10), channel_id=1, source_target_pairs={{0,2},{1,3},{2,0},{3,1},{4,6},{5,7},{6,4},{7,5},{8,10},{9,11},{10,... | collective-permute-start | bytes 483848 | tf_op jit(solution)/shard_map/ppermute | solution.py:470
  (62 other events, 609.0 us)

commit v3 on v2

--- a/solution.py
+++ b/solution.py
@@ -616,26 +616,25 @@
     far_v = reduce_far(*half_v)
     own_v = merge(*far_v)
     attended, d_queries = attention(
-        attend_kernel, "attend", qs, cot, [kn, kv], 2, 0, 11, [half_v[2], half_v[3]]
-    )
-    *near_k, attended = together(*near_k, attended)
+        attend_kernel, "attend", qs, cot, [kn, kv], 2, 0, 11, [parts_k[0], parts_k[1]]
+    )
+    half_z = part_of(own_v, z0)
+    got_v = swap(part_of(own_v, 1 - z0).astype(BF), "sp", 2)
+    *near_k, attended, got_v = together(*near_k, attended, got_v)
     half_k = add_near(*near_k)
     far_k = reduce_far(*half_k)
-    half_z = part_of(own_v, z0)
-    got_v = swap(part_of(own_v, 1 - z0).astype(BF), "sp", 2)
+    half_z = half_z + got_v.astype(F32)
+    got_v = swap(part_of(half_z, 1 - z1).astype(BF), "sp", 4)
     *far_k, got_v = together(*far_k, got_v)
     mine_k, sends_k, gots_k = reduce_z(merge(*far_k))
-    got_v, *sends = together(got_v, *sends_k)
-    half_z = half_z + got_v.astype(F32)
-    give_v = part_of(half_z, 1 - z1).astype(BF)
-    got_v = swap(give_v, "sp", 4)
+    quart_v = ((part_of(half_z, z1) + got_v.astype(F32)) * scale).astype(BF)
+    got_v = swap(quart_v, "sp", 4)
     d_tokens = input_grads(
-        scal, d_key, d_val, keys_near + keys_far, vals_near + vals_far, spots, shard, depth, sends + [give_v]
+        scal, d_key, d_val, keys_near + keys_far, vals_near + vals_far, spots, shard, depth, sends_k + [quart_v]
     )
     *gots_k, d_tokens, got_v = together(*gots_k, d_tokens, got_v)
     quart_k = spread_z(mine_k, gots_k)
-    quart_v = ((part_of(half_z, z1) + got_v.astype(F32)) * scale).astype(BF)
-    half_v = joined(quart_v, swap(quart_v, "sp", 4), z1)
+    half_v = joined(quart_v, got_v, z1)
     whole_v = joined(half_v, swap(half_v, "sp", 2), z0)
     d_w_value = assemble(whole_v)
     d_w_key = assemble(ordered(quart_k))

time: 219 us -> 212 us (0.968)
  waiting for transfers between devices: 61 us -> 51.3 us
    ppermute x52, waiting for transfers between devices: 61 us -> 51.3 us  [swap(): return lax.ppermute(x, axis, [(i, i ^ bit) for i in range(n)])]
  transfers between devices with their start and end apart: 52 -> 52, of which waited for: 27 -> 26; matrix products, arithmetic and copies ran while one was open for 2% -> 3% of each run, Pallas kernels for 40% -> 42%
where the time goes in v3:
time: 212 us; the launch traced here: 211 us
  Pallas kernels  91.5 us (43%)
  starting transfers between devices  53.4 us (25%)
  waiting for transfers between devices  51.3 us (24%)
  other arithmetic  9.99 us (5%)
  local copies, waits for them, and re-layouts  3.73 us (2%)
    pallas_call x11, Pallas kernels, call(): pl.pallas_call(run, grid_spec=pltpu.PrefetchScalarGridSpec(num_scalar_pre...  91.5 us
    ppermute x52, starting transfers between devices, swap(): return lax.ppermute(x, axis, [(i, i ^ bit) for i in range(n)])  53.4 us
    ppermute x52, waiting for transfers between devices, swap(): return lax.ppermute(x, axis, [(i, i ^ bit) for i in range(n)])  51.3 us
  transfers between devices with their start and end apart: 52, of which 26 were waited for; matrix products, arithmetic and copies ran while one was open for 3% of the time, Pallas kernels for 42%

profile of v3, /device:TPU:0, one launch (start us, length us, event | category | flops | bytes accessed | tf_op | source)
XLA Modules:
  0.0 211.4 jit_solution(478714496895234588)
XLA Ops:
  2.0 3.0 %collective-permute-start = (bf16[288,1120]{1,0:T(8,128)(2,1)S(1)}, bf16[288,1120]{1,0:T(8,128)(2,1)S(1)}, u32[]{:S(2)}, u32[]{:S(2)}) collective-permute-start(bf16[288,1120]{1,0:T(8,128)(2,1)S(1)} %slice_select_fusion.1), channel_id=1, source_target_pairs={{0,8},{8,0},{16,24},{24,16},{1,9},{9,1},{17,25},{25,17},{2,10},{10... | collective-permute-start | bytes 1935368 | tf_op jit(solution)/shard_map/ppermute | solution.py:470
  8.8 3.8 %token_rows.1 = (bf16[896,1680]{1,0:T(8,128)(2,1)S(1)}, bf16[896,560]{1,0:T(8,128)(2,1)S(1)}, bf16[4,280,896]{2,1,0:T(8,128)(2,1)}) custom-call(s32[2]{0:T(128)S(1)} %pad_add_fusion.refs_0_, bf16[4,560,896]{2,1,0:T(8,128)(2,1)S(1)} %bitcast.89), custom_call_target="tpu_custom_call" | custom-call | bytes 12042240 | tf_op jit(solution)/shard_map/token_rows/pallas_call | solution.py:64
  12.6 7.3 %collective-permute-done.refs_3_.refs_4_ = bf16[288,1120]{1,0:T(8,128)(2,1)S(1)} collective-permute-done((bf16[288,1120]{1,0:T(8,128)(2,1)S(1)}, bf16[288,1120]{1,0:T(8,128)(2,1)S(1)}, u32[]{:S(2)}, u32[]{:S(2)}) %collective-permute-start) | collective-permute-done | bytes 645152 | tf_op jit(solution)/shard_map/ppermute | solution.py:470
  27.0 6.3 %key_near.1.refs_2_ = f32[896,1120]{1,0:T(8,128)S(1)} custom-call(s32[2]{0:T(128)S(1)} %pad_add_fusion.refs_0_, bf16[896,1680]{1,0:T(8,128)(2,1)S(1)} %get-tuple-element.87.refs_1_, bf16[560,1120]{1,0:T(8,128)(2,1)S(1)} %copy-done.2, bf16[288,1120]{1,0:T(8,128)(2,1)S(1)} %collective-permute-done.refs_3_.refs_4_, ...), custom_call_target="tpu_custom_call" | custom-call | flops 3371827200 | bytes 12794880 | tf_op jit(solution)/shard_map/key_near/pallas_call | solution.py:64
  35.5 3.1 %key_feat.1 = (bf16[896,1152]{1,0:T(8,128)(2,1)S(1)}, f32[1,1120]{1,0:T(1,128)S(1)}) custom-call(s32[2]{0:T(128)S(1)} %pad_add_fusion.refs_0_, bf16[896,560]{1,0:T(8,128)(2,1)S(1)} %get-tuple-element.90.refs_1_, f32[896,1120]{1,0:T(8,128)S(1)} %key_near.1.refs_2_, bf16[144,1120]{1,0:T(8,128)(2,1)S(1)} %collective-permute-done.2.refs_3_.refs_8_, ...), custom_call_target="tpu_custom_call" | custom-call | flops 1123942400 | bytes 8279040 | tf_op jit(solution)/shard_map/key_feat/pallas_call | solution.py:64
  46.0 2.6 %collective-permute-start.11 = (f32[1,1120]{1,0:T(1,128)S(1)}, f32[1,1120]{1,0:T(1,128)S(1)}, u32[]{:S(2)}, u32[]{:S(2)}) collective-permute-start(f32[1,1120]{1,0:T(1,128)S(1)} %add.123), channel_id=1, source_target_pairs={{0,4},{1,5},{2,6},{3,7},{4,0},{5,1},{6,2},{7,3},{8,12},{9,13},{10,... | collective-permute-start | bytes 13448 | tf_op jit(solution)/shard_map/ppermute | solution.py:470
  50.5 6.8 %collective-permute-done.12.refs_3_.refs_13_ = bf16[288,1120]{1,0:T(8,128)(2,1)S(1)} collective-permute-done((bf16[288,1120]{1,0:T(8,128)(2,1)S(1)}, bf16[288,1120]{1,0:T(8,128)(2,1)S(1)}, u32[]{:S(2)}, u32[]{:S(2)}) %collective-permute-start.12) | collective-permute-done | bytes 645152 | tf_op jit(solution)/shard_map/ppermute | solution.py:470
  57.6 4.2 %grad_state.1 = f32[32,1120]{1,0:T(8,128)S(1)} custom-call(bf16[1120,896]{1,0:T(8,128)(2,1)S(1)} %bitcast.90, bf16[1120,896]{1,0:T(8,128)(2,1)S(1)} %bitcast.93, f32[1,1120]{1,0:T(1,128)S(1)} %add.124.refs_2_), custom_call_target="tpu_custom_call" | custom-call | flops 2055208960 | bytes 4014080 | tf_op jit(solution)/shard_map/grad_state/pallas_call | solution.py:64
  68.3 6.3 %val_near.1.refs_2_ = f32[896,1120]{1,0:T(8,128)S(1)} custom-call(s32[2]{0:T(128)S(1)} %pad_add_fusion.refs_0_, bf16[896,1680]{1,0:T(8,128)(2,1)S(1)} %get-tuple-element.87.refs_1_, bf16[560,1120]{1,0:T(8,128)(2,1)S(1)} %copy-done.3, bf16[288,1120]{1,0:T(8,128)(2,1)S(1)} %collective-permute-done.12.refs_3_.refs_13_, ...), custom_call_target="tpu_custom_call" | custom-call | flops 3371827200 | bytes 12794880 | tf_op jit(solution)/shard_map/val_near/pallas_call | solution.py:64
  75.5 2.7 %collective-permute-start.21 = (bf16[32,1120]{1,0:T(8,128)(2,1)S(1)}, bf16[32,1120]{1,0:T(8,128)(2,1)S(1)}, u32[]{:S(2)}, u32[]{:S(2)}) collective-permute-start(bf16[32,1120]{1,0:T(8,128)(2,1)S(1)} %fusion.17), channel_id=1, source_target_pairs={{0,4},{1,5},{2,6},{3,7},{4,0},{5,1},{6,2},{7,3},{8,12},{9,13},{10,... | collective-permute-start | bytes 215048 | tf_op jit(solution)/shard_map/ppermute | solution.py:470
  78.2 3.8 %val_feat.1 = (bf16[896,1152]{1,0:T(8,128)(2,1)S(1)}, f32[32,1120]{1,0:T(8,128)S(1)}) custom-call(s32[2]{0:T(128)S(1)} %pad_add_fusion.refs_0_, bf16[896,560]{1,0:T(8,128)(2,1)S(1)} %get-tuple-element.90.refs_1_, f32[896,1120]{1,0:T(8,128)S(1)} %val_near.1.refs_2_, bf16[896,1152]{1,0:T(8,128)(2,1)S(1)} %get-tuple-element.96.refs_3_, ...), custom_call_target="tpu_custom_call" | custom-call | flops 1123942400 | bytes 8279040 | tf_op jit(solution)/shard_map/val_feat/pallas_call | solution.py:64
  85.4 2.7 %collective-permute-start.26 = (bf16[32,1120]{1,0:T(8,128)(2,1)S(1)}, bf16[32,1120]{1,0:T(8,128)(2,1)S(1)}, u32[]{:S(2)}, u32[]{:S(2)}) collective-permute-start(bf16[32,1120]{1,0:T(8,128)(2,1)S(1)} %convert_element_type.121), channel_id=1, source_target_pairs={{0,4},{1,5},{2,6},{3,7},{4,0},{5,1},{6,2},{7,3},{8,12},{9,13},{10,... | collective-permute-start | bytes 215048 | tf_op jit(solution)/shard_map/ppermute | solution.py:470
  88.5 14.8 %d_w_value.1 = (bf16[896,1152]{1,0:T(8,128)(2,1)}, bf16[2,144,1120]{2,1,0:T(8,128)(2,1)}, bf16[2,136,1120]{2,1,0:T(8,128)(2,1)}, f32[2,144,1120]{2,1,0:T(8,128)S(1)}, f32[2,136,1120]{2,1,0:T(8,128)S(1)}) custom-call(s32[2]{0:T(128)S(1)} %pad_add_fusion.refs_0_, bf16[8,280,896]{2,1,0:T(8,128)(2,1)} %bitcast.87, ...), custom_call_target="tpu_custom_call" | custom-call | flops 4495769600 | bytes 11791360 | tf_op jit(solution)/shard_map/d_w_value/pallas_call | solution.py:64
  106.4 5.8 %grad_norm.1 = f32[1,1120]{1,0:T(1,128)S(1)} custom-call(bf16[1120,896]{1,0:T(8,128)(2,1)S(1)} %bitcast.91, bf16[1120,896]{1,0:T(8,128)(2,1)S(1)} %bitcast.94, f32[1,1120]{1,0:T(1,128)S(1)} %add.124.refs_2_, f32[32,1120]{1,0:T(8,128)S(1)} %convert_add_fusion.6.refs_3_), custom_call_target="tpu_custom_call" | custom-call | flops 2569011200 | bytes 4014080 | tf_op jit(solution)/shard_map/grad_norm/pallas_call | solution.py:64
  113.8 3.3 %collective-permute-done.32 = f32[1,1120]{1,0:T(1,128)S(1)} collective-permute-done((f32[1,1120]{1,0:T(1,128)S(1)}, f32[1,1120]{1,0:T(1,128)S(1)}, u32[]{:S(2)}, u32[]{:S(2)}) %collective-permute-start.32) | collective-permute-done | bytes 4512 | tf_op jit(solution)/shard_map/ppermute | solution.py:470
  125.6 15.2 %d_w_key.1 = (bf16[896,1152]{1,0:T(8,128)(2,1)}, bf16[2,144,1120]{2,1,0:T(8,128)(2,1)S(1)}, bf16[2,136,1120]{2,1,0:T(8,128)(2,1)S(1)}, f32[2,144,1120]{2,1,0:T(8,128)S(1)}, f32[2,136,1120]{2,1,0:T(8,128)S(1)}) custom-call(s32[2]{0:T(128)S(1)} %pad_add_fusion.refs_0_, bf16[8,280,896]{2,1,0:T(8,128)(2,1)} %bitcast.88, ...), custom_call_target="tpu_custom_call" | custom-call | flops 4495769600 | bytes 15805440 | tf_op jit(solution)/shard_map/d_w_key/pallas_call | solution.py:64
  145.8 9.6 %attend.1 = (bf16[1120,896]{1,0:T(8,128)(2,1)}, bf16[1120,896]{1,0:T(8,128)(2,1)}) custom-call(bf16[1120,896]{1,0:T(8,128)(2,1)S(1)} %bitcast.92, bf16[1120,896]{1,0:T(8,128)(2,1)S(1)} %bitcast.95, f32[1,1120]{1,0:T(1,128)S(1)} %add.124.refs_2_, f32[32,1120]{1,0:T(8,128)S(1)} %convert_add_fusion.6.refs_3_, ...), custom_call_target="tpu_custom_call" | custom-call | flops 5651824640 | bytes 8028160 | tf_op jit(solution)/shard_map/attend/pallas_call | solution.py:64
  160.9 3.2 %collective-permute-done.41 = bf16[72,1120]{1,0:T(8,128)(2,1)S(1)} collective-permute-done((bf16[72,1120]{1,0:T(8,128)(2,1)S(1)}, bf16[72,1120]{1,0:T(8,128)(2,1)S(1)}, u32[]{:S(2)}, u32[]{:S(2)}) %collective-permute-start.41) | collective-permute-done | bytes 161312 | tf_op jit(solution)/shard_map/ppermute | solution.py:470
  169.1 2.8 %collective-permute-start.43 = (bf16[72,1120]{1,0:T(8,128)(2,1)S(1)}, bf16[72,1120]{1,0:T(8,128)(2,1)S(1)}, u32[]{:S(2)}, u32[]{:S(2)}) collective-permute-start(bf16[72,1120]{1,0:T(8,128)(2,1)S(1)} %get-tuple-element.162.refs_22_), channel_id=1, source_target_pairs={{0,4},{1,5},{2,6},{3,7},{4,0},{5,1},{6,2},{7,3},{8,12},{9,13},{10,... | collective-permute-start | bytes 483848 | tf_op jit(solution)/shard_map/ppermute | solution.py:470
  172.3 18.8 %d_tokens.1 = bf16[2240,896]{1,0:T(8,128)(2,1)} custom-call(s32[2]{0:T(128)} %copy-done.16, bf16[896,1152]{1,0:T(8,128)(2,1)} %get-tuple-element.150.refs_1_, bf16[896,1152]{1,0:T(8,128)(2,1)} %get-tuple-element.151.refs_2_, bf16[560,1120]{1,0:T(8,128)(2,1)} %refs_3_.1, bf16[288,1120]{1,0:T(8,128)(2,1)} %copy-done.12, bf16[288,1120]{1,0:T(8,128)(2,1)} %copy-done.24, ...), custom_call_target="tpu_custom_call" | custom-call | flops 8991539200 | bytes 18063360 | tf_op jit(solution)/shard_map/d_tokens/pallas_call | solution.py:64
  191.6 3.7 %collective-permute-start.47 = (bf16[72,1120]{1,0:T(8,128)(2,1)S(1)}, bf16[72,1120]{1,0:T(8,128)(2,1)S(1)}, u32[]{:S(2)}, u32[]{:S(2)}) collective-permute-start(bf16[72,1120]{1,0:T(8,128)(2,1)S(1)} %fusion.8), channel_id=1, source_target_pairs={{0,4},{1,5},{2,6},{3,7},{4,0},{5,1},{6,2},{7,3},{8,12},{9,13},{10,... | collective-permute-start | bytes 483848 | tf_op jit(solution)/shard_map/ppermute | solution.py:470
  196.9 3.9 %collective-permute-done.46 = bf16[72,1120]{1,0:T(8,128)(2,1)S(1)} collective-permute-done((bf16[72,1120]{1,0:T(8,128)(2,1)S(1)}, bf16[72,1120]{1,0:T(8,128)(2,1)S(1)}, u32[]{:S(2)}, u32[]{:S(2)}) %collective-permute-start.46) | collective-permute-done | bytes 161312 | tf_op jit(solution)/shard_map/ppermute | solution.py:470
  200.8 3.3 %collective-permute-done.48 = bf16[72,1120]{1,0:T(8,128)(2,1)S(1)} collective-permute-done((bf16[72,1120]{1,0:T(8,128)(2,1)S(1)}, bf16[72,1120]{1,0:T(8,128)(2,1)S(1)}, u32[]{:S(2)}, u32[]{:S(2)}) %collective-permute-start.48) | collective-permute-done | bytes 161312 | tf_op jit(solution)/shard_map/ppermute | solution.py:470
  204.4 2.8 %collective-permute-done.50 = bf16[144,1120]{1,0:T(8,128)(2,1)S(1)} collective-permute-done((bf16[144,1120]{1,0:T(8,128)(2,1)S(1)}, bf16[144,1120]{1,0:T(8,128)(2,1)S(1)}, u32[]{:S(2)}, u32[]{:S(2)}) %collective-permute-start.50) | collective-permute-done | bytes 322592 | tf_op jit(solution)/shard_map/ppermute | solution.py:470
  (211 shorter events, 70.4 us)
Async XLA Ops:
  2.0 17.9 %collective-permute-start = (bf16[288,1120]{1,0:T(8,128)(2,1)S(1)}, bf16[288,1120]{1,0:T(8,128)(2,1)S(1)}, u32[]{:S(2)}, u32[]{:S(2)}) collective-permute-start(bf16[288,1120]{1,0:T(8,128)(2,1)S(1)} %slice_select_fusion.1), channel_id=1, source_target_pairs={{0,8},{8,0},{16,24},{24,16},{1,9},{9,1},{17,25},{25,17},{2,10},{10... | collective-permute-start | bytes 1935368 | tf_op jit(solution)/shard_map/ppermute | solution.py:470
  5.0 16.4 %collective-permute-start.1 = (bf16[288,1120]{1,0:T(8,128)(2,1)S(1)}, bf16[288,1120]{1,0:T(8,128)(2,1)S(1)}, u32[]{:S(2)}, u32[]{:S(2)}) collective-permute-start(bf16[288,1120]{1,0:T(8,128)(2,1)S(1)} %slice_select_fusion.1), channel_id=1, source_target_pairs={{0,16},{8,24},{16,0},{24,8},{1,17},{9,25},{17,1},{25,9},{2,18},{10... | collective-permute-start | bytes 1935368 | tf_op jit(solution)/shard_map/ppermute | solution.py:470
  21.4 11.9 %collective-permute-start.6 = (bf16[4,280,896]{2,1,0:T(8,128)(2,1)}, bf16[4,280,896]{2,1,0:T(8,128)(2,1)}, u32[]{:S(2)}, u32[]{:S(2)}) collective-permute-start(bf16[4,280,896]{2,1,0:T(8,128)(2,1)} %get-tuple-element.88), channel_id=1, source_target_pairs={{0,1},{1,0},{2,3},{3,2},{4,5},{5,4},{6,7},{7,6},{8,9},{9,8},{10,11... | collective-permute-start | bytes 6021128 | tf_op jit(solution)/shard_map/ppermute | solution.py:470
  22.0 11.3 %collective-permute-start.2 = (bf16[144,1120]{1,0:T(8,128)(2,1)S(1)}, bf16[144,1120]{1,0:T(8,128)(2,1)S(1)}, u32[]{:S(2)}, u32[]{:S(2)}) collective-permute-start(bf16[144,1120]{1,0:T(8,128)(2,1)S(1)} %slice.60), channel_id=1, source_target_pairs={{0,8},{8,0},{16,24},{24,16},{1,9},{9,1},{17,25},{25,17},{2,10},{10... | collective-permute-start | bytes 967688 | tf_op jit(solution)/shard_map/ppermute | solution.py:470
  22.5 10.8 %collective-permute-start.3 = (bf16[144,1120]{1,0:T(8,128)(2,1)S(1)}, bf16[144,1120]{1,0:T(8,128)(2,1)S(1)}, u32[]{:S(2)}, u32[]{:S(2)}) collective-permute-start(bf16[144,1120]{1,0:T(8,128)(2,1)S(1)} %slice.61), channel_id=1, source_target_pairs={{0,16},{8,24},{16,0},{24,8},{1,17},{9,25},{17,1},{25,9},{2,18},{10... | collective-permute-start | bytes 967688 | tf_op jit(solution)/shard_map/ppermute | solution.py:470
  39.9 35.0 %collective-permute-start.20 = (bf16[896,1152]{1,0:T(8,128)(2,1)S(1)}, bf16[896,1152]{1,0:T(8,128)(2,1)}, u32[]{:S(2)}, u32[]{:S(2)}) collective-permute-start(bf16[896,1152]{1,0:T(8,128)(2,1)S(1)} %get-tuple-element.96.refs_3_), channel_id=1, source_target_pairs={{0,1},{1,0},{2,3},{3,2},{4,5},{5,4},{6,7},{7,6},{8,9},{9,8},{10,11... | collective-permute-start | bytes 6193160 | tf_op jit(solution)/shard_map/ppermute | solution.py:470
  40.3 17.0 %collective-permute-start.12 = (bf16[288,1120]{1,0:T(8,128)(2,1)S(1)}, bf16[288,1120]{1,0:T(8,128)(2,1)S(1)}, u32[]{:S(2)}, u32[]{:S(2)}) collective-permute-start(bf16[288,1120]{1,0:T(8,128)(2,1)S(1)} %slice_select_fusion), channel_id=1, source_target_pairs={{0,8},{8,0},{16,24},{24,16},{1,9},{9,1},{17,25},{25,17},{2,10},{10... | collective-permute-start | bytes 1935368 | tf_op jit(solution)/shard_map/ppermute | solution.py:470
  40.7 16.9 %collective-permute-start.13 = (bf16[288,1120]{1,0:T(8,128)(2,1)S(1)}, bf16[288,1120]{1,0:T(8,128)(2,1)S(1)}, u32[]{:S(2)}, u32[]{:S(2)}) collective-permute-start(bf16[288,1120]{1,0:T(8,128)(2,1)S(1)} %slice_select_fusion), channel_id=1, source_target_pairs={{0,16},{8,24},{16,0},{24,8},{1,17},{9,25},{17,1},{25,9},{2,18},{10... | collective-permute-start | bytes 1935368 | tf_op jit(solution)/shard_map/ppermute | solution.py:470
  62.5 12.1 %collective-permute-start.18 = (bf16[144,1120]{1,0:T(8,128)(2,1)S(1)}, bf16[144,1120]{1,0:T(8,128)(2,1)S(1)}, u32[]{:S(2)}, u32[]{:S(2)}) collective-permute-start(bf16[144,1120]{1,0:T(8,128)(2,1)S(1)} %slice.64), channel_id=1, source_target_pairs={{0,8},{8,0},{16,24},{24,16},{1,9},{9,1},{17,25},{25,17},{2,10},{10... | collective-permute-start | bytes 967688 | tf_op jit(solution)/shard_map/ppermute | solution.py:470
  83.8 19.5 %collective-permute-start.28 = (bf16[896,1152]{1,0:T(8,128)(2,1)S(1)}, bf16[896,1152]{1,0:T(8,128)(2,1)S(1)}, u32[]{:S(2)}, u32[]{:S(2)}) collective-permute-start(bf16[896,1152]{1,0:T(8,128)(2,1)S(1)} %get-tuple-element.113.refs_4_), channel_id=1, source_target_pairs={{0,1},{1,0},{2,3},{3,2},{4,5},{5,4},{6,7},{7,6},{8,9},{9,8},{10,11... | collective-permute-start | bytes 6193160 | tf_op jit(solution)/shard_map/ppermute | solution.py:470
  84.0 19.3 %collective-permute-start.25 = (bf16[32,1120]{1,0:T(8,128)(2,1)S(1)}, bf16[32,1120]{1,0:T(8,128)(2,1)S(1)}, u32[]{:S(2)}, u32[]{:S(2)}) collective-permute-start(bf16[32,1120]{1,0:T(8,128)(2,1)S(1)} %convert_element_type.121), channel_id=1, source_target_pairs={{0,2},{1,3},{2,0},{3,1},{4,6},{5,7},{6,4},{7,5},{8,10},{9,11},{10,... | collective-permute-start | bytes 215048 | tf_op jit(solution)/shard_map/ppermute | solution.py:470
  85.4 17.9 %collective-permute-start.26 = (bf16[32,1120]{1,0:T(8,128)(2,1)S(1)}, bf16[32,1120]{1,0:T(8,128)(2,1)S(1)}, u32[]{:S(2)}, u32[]{:S(2)}) collective-permute-start(bf16[32,1120]{1,0:T(8,128)(2,1)S(1)} %convert_element_type.121), channel_id=1, source_target_pairs={{0,4},{1,5},{2,6},{3,7},{4,0},{5,1},{6,2},{7,3},{8,12},{9,13},{10,... | collective-permute-start | bytes 215048 | tf_op jit(solution)/shard_map/ppermute | solution.py:470
  88.1 15.2 %collective-permute-start.27 = (bf16[32,1120]{1,0:T(8,128)(2,1)S(1)}, bf16[32,1120]{1,0:T(8,128)(2,1)S(1)}, u32[]{:S(2)}, u32[]{:S(2)}) collective-permute-start(bf16[32,1120]{1,0:T(8,128)(2,1)S(1)} %convert_element_type.121), channel_id=1, source_target_pairs={{0,6},{1,7},{2,4},{3,5},{4,2},{5,3},{6,0},{7,1},{8,14},{9,15},{10,... | collective-permute-start | bytes 215048 | tf_op jit(solution)/shard_map/ppermute | solution.py:470
  103.3 18.3 %collective-permute-start.29 = (bf16[2,144,1120]{2,1,0:T(8,128)(2,1)}, bf16[2,144,1120]{2,1,0:T(8,128)(2,1)}, u32[]{:S(2)}, u32[]{:S(2)}) collective-permute-start(bf16[2,144,1120]{2,1,0:T(8,128)(2,1)} %get-tuple-element.123), channel_id=1, source_target_pairs={{0,8},{8,0},{16,24},{24,16},{1,9},{9,1},{17,25},{25,17},{2,10},{10... | collective-permute-start | bytes 1935368 | tf_op jit(solution)/shard_map/ppermute | solution.py:470
  104.8 16.7 %collective-permute-start.30 = (bf16[2,136,1120]{2,1,0:T(8,128)(2,1)}, bf16[2,136,1120]{2,1,0:T(8,128)(2,1)}, u32[]{:S(2)}, u32[]{:S(2)}) collective-permute-start(bf16[2,136,1120]{2,1,0:T(8,128)(2,1)} %get-tuple-element.124), channel_id=1, source_target_pairs={{0,16},{8,24},{16,0},{24,8},{1,17},{9,25},{17,1},{25,9},{2,18},{10... | collective-permute-start | bytes 1827848 | tf_op jit(solution)/shard_map/ppermute | solution.py:470
  122.9 20.7 %collective-permute-start.36 = (bf16[144,1120]{1,0:T(8,128)(2,1)S(1)}, bf16[144,1120]{1,0:T(8,128)(2,1)S(1)}, u32[]{:S(2)}, u32[]{:S(2)}) collective-permute-start(bf16[144,1120]{1,0:T(8,128)(2,1)S(1)} %fusion.3.refs_9_), channel_id=1, source_target_pairs={{0,16},{8,24},{16,0},{24,8},{1,17},{9,25},{17,1},{25,9},{2,18},{10... | collective-permute-start | bytes 967688 | tf_op jit(solution)/shard_map/ppermute | solution.py:470
  124.7 18.8 %collective-permute-start.37 = (bf16[136,1120]{1,0:T(8,128)(2,1)S(1)}, bf16[136,1120]{1,0:T(8,128)(2,1)S(1)}, u32[]{:S(2)}, u32[]{:S(2)}) collective-permute-start(bf16[136,1120]{1,0:T(8,128)(2,1)S(1)} %fusion.11.refs_10_), channel_id=1, source_target_pairs={{0,8},{8,0},{16,24},{24,16},{1,9},{9,1},{17,25},{25,17},{2,10},{10... | collective-permute-start | bytes 913928 | tf_op jit(solution)/shard_map/ppermute | solution.py:470
  140.8 14.8 %collective-permute-start.34 = (bf16[2,144,1120]{2,1,0:T(8,128)(2,1)S(1)}, bf16[2,144,1120]{2,1,0:T(8,128)(2,1)S(1)}, u32[]{:S(2)}, u32[]{:S(2)}) collective-permute-start(bf16[2,144,1120]{2,1,0:T(8,128)(2,1)S(1)} %get-tuple-element.135.refs_4_), channel_id=1, source_target_pairs={{0,8},{8,0},{16,24},{24,16},{1,9},{9,1},{17,25},{25,17},{2,10},{10... | collective-permute-start | bytes 1935368 | tf_op jit(solution)/shard_map/ppermute | solution.py:470
  142.0 13.5 %collective-permute-start.35 = (bf16[2,136,1120]{2,1,0:T(8,128)(2,1)S(1)}, bf16[2,136,1120]{2,1,0:T(8,128)(2,1)S(1)}, u32[]{:S(2)}, u32[]{:S(2)}) collective-permute-start(bf16[2,136,1120]{2,1,0:T(8,128)(2,1)S(1)} %get-tuple-element.136.refs_5_), channel_id=1, source_target_pairs={{0,16},{8,24},{16,0},{24,8},{1,17},{9,25},{17,1},{25,9},{2,18},{10... | collective-permute-start | bytes 1827848 | tf_op jit(solution)/shard_map/ppermute | solution.py:470
  143.9 11.8 %collective-permute-start.38 = (bf16[144,1120]{1,0:T(8,128)(2,1)S(1)}, bf16[144,1120]{1,0:T(8,128)(2,1)S(1)}, u32[]{:S(2)}, u32[]{:S(2)}) collective-permute-start(bf16[144,1120]{1,0:T(8,128)(2,1)S(1)} %fusion.2), channel_id=1, source_target_pairs={{0,2},{1,3},{2,0},{3,1},{4,6},{5,7},{6,4},{7,5},{8,10},{9,11},{10,... | collective-permute-start | bytes 967688 | tf_op jit(solution)/shard_map/ppermute | solution.py:470
  166.5 24.6 %collective-permute-start.45 = (bf16[72,1120]{1,0:T(8,128)(2,1)S(1)}, bf16[72,1120]{1,0:T(8,128)(2,1)S(1)}, u32[]{:S(2)}, u32[]{:S(2)}) collective-permute-start(bf16[72,1120]{1,0:T(8,128)(2,1)S(1)} %fusion.10.refs_24_), channel_id=1, source_target_pairs={{0,4},{1,5},{2,6},{3,7},{4,0},{5,1},{6,2},{7,3},{8,12},{9,13},{10,... | collective-permute-start | bytes 483848 | tf_op jit(solution)/shard_map/ppermute | solution.py:470
  167.9 23.3 %collective-permute-start.42 = (bf16[72,1120]{1,0:T(8,128)(2,1)S(1)}, bf16[72,1120]{1,0:T(8,128)(2,1)S(1)}, u32[]{:S(2)}, u32[]{:S(2)}) collective-permute-start(bf16[72,1120]{1,0:T(8,128)(2,1)S(1)} %get-tuple-element.163.refs_21_), channel_id=1, source_target_pairs={{0,2},{1,3},{2,0},{3,1},{4,6},{5,7},{6,4},{7,5},{8,10},{9,11},{10,... | collective-permute-start | bytes 483848 | tf_op jit(solution)/shard_map/ppermute | solution.py:470
  169.1 22.1 %collective-permute-start.43 = (bf16[72,1120]{1,0:T(8,128)(2,1)S(1)}, bf16[72,1120]{1,0:T(8,128)(2,1)S(1)}, u32[]{:S(2)}, u32[]{:S(2)}) collective-permute-start(bf16[72,1120]{1,0:T(8,128)(2,1)S(1)} %get-tuple-element.162.refs_22_), channel_id=1, source_target_pairs={{0,4},{1,5},{2,6},{3,7},{4,0},{5,1},{6,2},{7,3},{8,12},{9,13},{10,... | collective-permute-start | bytes 483848 | tf_op jit(solution)/shard_map/ppermute | solution.py:470
  171.9 19.3 %collective-permute-start.44 = (bf16[72,1120]{1,0:T(8,128)(2,1)S(1)}, bf16[72,1120]{1,0:T(8,128)(2,1)S(1)}, u32[]{:S(2)}, u32[]{:S(2)}) collective-permute-start(bf16[72,1120]{1,0:T(8,128)(2,1)S(1)} %get-tuple-element.161.refs_23_), channel_id=1, source_target_pairs={{0,6},{1,7},{2,4},{3,5},{4,2},{5,3},{6,0},{7,1},{8,14},{9,15},{10,... | collective-permute-start | bytes 483848 | tf_op jit(solution)/shard_map/ppermute | solution.py:470
  (61 other events, 560.2 us)

commit v4 on v3

--- a/solution.py
+++ b/solution.py
@@ -422,14 +422,15 @@
 
         @pl.when((scal[0] == core) & (step == 0))
         def _():
-            for k in range(len(counts)):
-                for c in copies(core, k):
-                    c.start()
+            for c in copies(core, 0):
+                c.start()
 
         for k in range(len(counts)):
 
             @pl.when((scal[0] == core) & (step == k))
             def _():
+                for c in copies(core, k + 1) if k + 1 < len(counts) else ():
+                    c.start()
                 for c in copies(core, k):
                     c.wait()
 

time: 212 us -> 212 us (level)
  no operation moved by 1% of the time
where the time goes in v4:
time: 212 us; the launch traced here: 211 us
  Pallas kernels  91.5 us (43%)
  starting transfers between devices  53.4 us (25%)
  waiting for transfers between devices  51.3 us (24%)
  other arithmetic  9.99 us (5%)
  local copies, waits for them, and re-layouts  3.73 us (2%)
    pallas_call x11, Pallas kernels, call(): pl.pallas_call(run, grid_spec=pltpu.PrefetchScalarGridSpec(num_scalar_pre...  91.5 us
    ppermute x52, starting transfers between devices, swap(): return lax.ppermute(x, axis, [(i, i ^ bit) for i in range(n)])  53.4 us
    ppermute x52, waiting for transfers between devices, swap(): return lax.ppermute(x, axis, [(i, i ^ bit) for i in range(n)])  51.3 us
  transfers between devices with their start and end apart: 52, of which 26 were waited for; matrix products, arithmetic and copies ran while one was open for 3% of the time, Pallas kernels for 42%

profile of v4, /device:TPU:0, one launch (start us, length us, event | category | flops | bytes accessed | tf_op | source)
XLA Modules:
  0.0 211.3 jit_solution(11016671928279860471)
XLA Ops:
  2.0 3.0 %collective-permute-start = (bf16[288,1120]{1,0:T(8,128)(2,1)S(1)}, bf16[288,1120]{1,0:T(8,128)(2,1)S(1)}, u32[]{:S(2)}, u32[]{:S(2)}) collective-permute-start(bf16[288,1120]{1,0:T(8,128)(2,1)S(1)} %slice_select_fusion.1), channel_id=1, source_target_pairs={{0,8},{8,0},{16,24},{24,16},{1,9},{9,1},{17,25},{25,17},{2,10},{10... | collective-permute-start | bytes 1935368 | tf_op jit(solution)/shard_map/ppermute | solution.py:471
  8.8 3.8 %token_rows.1 = (bf16[896,1680]{1,0:T(8,128)(2,1)S(1)}, bf16[896,560]{1,0:T(8,128)(2,1)S(1)}, bf16[4,280,896]{2,1,0:T(8,128)(2,1)}) custom-call(s32[2]{0:T(128)S(1)} %pad_add_fusion.refs_0_, bf16[4,560,896]{2,1,0:T(8,128)(2,1)S(1)} %bitcast.89), custom_call_target="tpu_custom_call" | custom-call | bytes 12042240 | tf_op jit(solution)/shard_map/token_rows/pallas_call | solution.py:64
  12.6 7.3 %collective-permute-done.refs_3_.refs_4_ = bf16[288,1120]{1,0:T(8,128)(2,1)S(1)} collective-permute-done((bf16[288,1120]{1,0:T(8,128)(2,1)S(1)}, bf16[288,1120]{1,0:T(8,128)(2,1)S(1)}, u32[]{:S(2)}, u32[]{:S(2)}) %collective-permute-start) | collective-permute-done | bytes 645152 | tf_op jit(solution)/shard_map/ppermute | solution.py:471
  27.0 6.3 %key_near.1.refs_2_ = f32[896,1120]{1,0:T(8,128)S(1)} custom-call(s32[2]{0:T(128)S(1)} %pad_add_fusion.refs_0_, bf16[896,1680]{1,0:T(8,128)(2,1)S(1)} %get-tuple-element.87.refs_1_, bf16[560,1120]{1,0:T(8,128)(2,1)S(1)} %copy-done.2, bf16[288,1120]{1,0:T(8,128)(2,1)S(1)} %collective-permute-done.refs_3_.refs_4_, ...), custom_call_target="tpu_custom_call" | custom-call | flops 3371827200 | bytes 12794880 | tf_op jit(solution)/shard_map/key_near/pallas_call | solution.py:64
  35.5 3.1 %key_feat.1 = (bf16[896,1152]{1,0:T(8,128)(2,1)S(1)}, f32[1,1120]{1,0:T(1,128)S(1)}) custom-call(s32[2]{0:T(128)S(1)} %pad_add_fusion.refs_0_, bf16[896,560]{1,0:T(8,128)(2,1)S(1)} %get-tuple-element.90.refs_1_, f32[896,1120]{1,0:T(8,128)S(1)} %key_near.1.refs_2_, bf16[144,1120]{1,0:T(8,128)(2,1)S(1)} %collective-permute-done.2.refs_3_.refs_8_, ...), custom_call_target="tpu_custom_call" | custom-call | flops 1123942400 | bytes 8279040 | tf_op jit(solution)/shard_map/key_feat/pallas_call | solution.py:64
  46.0 2.6 %collective-permute-start.11 = (f32[1,1120]{1,0:T(1,128)S(1)}, f32[1,1120]{1,0:T(1,128)S(1)}, u32[]{:S(2)}, u32[]{:S(2)}) collective-permute-start(f32[1,1120]{1,0:T(1,128)S(1)} %add.123), channel_id=1, source_target_pairs={{0,4},{1,5},{2,6},{3,7},{4,0},{5,1},{6,2},{7,3},{8,12},{9,13},{10,... | collective-permute-start | bytes 13448 | tf_op jit(solution)/shard_map/ppermute | solution.py:471
  50.5 6.8 %collective-permute-done.12.refs_3_.refs_13_ = bf16[288,1120]{1,0:T(8,128)(2,1)S(1)} collective-permute-done((bf16[288,1120]{1,0:T(8,128)(2,1)S(1)}, bf16[288,1120]{1,0:T(8,128)(2,1)S(1)}, u32[]{:S(2)}, u32[]{:S(2)}) %collective-permute-start.12) | collective-permute-done | bytes 645152 | tf_op jit(solution)/shard_map/ppermute | solution.py:471
  57.6 4.2 %grad_state.1 = f32[32,1120]{1,0:T(8,128)S(1)} custom-call(bf16[1120,896]{1,0:T(8,128)(2,1)S(1)} %bitcast.90, bf16[1120,896]{1,0:T(8,128)(2,1)S(1)} %bitcast.93, f32[1,1120]{1,0:T(1,128)S(1)} %add.124.refs_2_), custom_call_target="tpu_custom_call" | custom-call | flops 2055208960 | bytes 4014080 | tf_op jit(solution)/shard_map/grad_state/pallas_call | solution.py:64
  68.3 6.3 %val_near.1.refs_2_ = f32[896,1120]{1,0:T(8,128)S(1)} custom-call(s32[2]{0:T(128)S(1)} %pad_add_fusion.refs_0_, bf16[896,1680]{1,0:T(8,128)(2,1)S(1)} %get-tuple-element.87.refs_1_, bf16[560,1120]{1,0:T(8,128)(2,1)S(1)} %copy-done.3, bf16[288,1120]{1,0:T(8,128)(2,1)S(1)} %collective-permute-done.12.refs_3_.refs_13_, ...), custom_call_target="tpu_custom_call" | custom-call | flops 3371827200 | bytes 12794880 | tf_op jit(solution)/shard_map/val_near/pallas_call | solution.py:64
  75.5 2.7 %collective-permute-start.21 = (bf16[32,1120]{1,0:T(8,128)(2,1)S(1)}, bf16[32,1120]{1,0:T(8,128)(2,1)S(1)}, u32[]{:S(2)}, u32[]{:S(2)}) collective-permute-start(bf16[32,1120]{1,0:T(8,128)(2,1)S(1)} %fusion.17), channel_id=1, source_target_pairs={{0,4},{1,5},{2,6},{3,7},{4,0},{5,1},{6,2},{7,3},{8,12},{9,13},{10,... | collective-permute-start | bytes 215048 | tf_op jit(solution)/shard_map/ppermute | solution.py:471
  78.2 3.8 %val_feat.1 = (bf16[896,1152]{1,0:T(8,128)(2,1)S(1)}, f32[32,1120]{1,0:T(8,128)S(1)}) custom-call(s32[2]{0:T(128)S(1)} %pad_add_fusion.refs_0_, bf16[896,560]{1,0:T(8,128)(2,1)S(1)} %get-tuple-element.90.refs_1_, f32[896,1120]{1,0:T(8,128)S(1)} %val_near.1.refs_2_, bf16[896,1152]{1,0:T(8,128)(2,1)S(1)} %get-tuple-element.96.refs_3_, ...), custom_call_target="tpu_custom_call" | custom-call | flops 1123942400 | bytes 8279040 | tf_op jit(solution)/shard_map/val_feat/pallas_call | solution.py:64
  85.4 2.7 %collective-permute-start.26 = (bf16[32,1120]{1,0:T(8,128)(2,1)S(1)}, bf16[32,1120]{1,0:T(8,128)(2,1)S(1)}, u32[]{:S(2)}, u32[]{:S(2)}) collective-permute-start(bf16[32,1120]{1,0:T(8,128)(2,1)S(1)} %convert_element_type.121), channel_id=1, source_target_pairs={{0,4},{1,5},{2,6},{3,7},{4,0},{5,1},{6,2},{7,3},{8,12},{9,13},{10,... | collective-permute-start | bytes 215048 | tf_op jit(solution)/shard_map/ppermute | solution.py:471
  88.5 14.8 %d_w_value.1 = (bf16[896,1152]{1,0:T(8,128)(2,1)}, bf16[2,144,1120]{2,1,0:T(8,128)(2,1)}, bf16[2,136,1120]{2,1,0:T(8,128)(2,1)}, f32[2,144,1120]{2,1,0:T(8,128)S(1)}, f32[2,136,1120]{2,1,0:T(8,128)S(1)}) custom-call(s32[2]{0:T(128)S(1)} %pad_add_fusion.refs_0_, bf16[8,280,896]{2,1,0:T(8,128)(2,1)} %bitcast.87, ...), custom_call_target="tpu_custom_call" | custom-call | flops 4495769600 | bytes 11791360 | tf_op jit(solution)/shard_map/d_w_value/pallas_call | solution.py:64
  106.4 5.8 %grad_norm.1 = f32[1,1120]{1,0:T(1,128)S(1)} custom-call(bf16[1120,896]{1,0:T(8,128)(2,1)S(1)} %bitcast.91, bf16[1120,896]{1,0:T(8,128)(2,1)S(1)} %bitcast.94, f32[1,1120]{1,0:T(1,128)S(1)} %add.124.refs_2_, f32[32,1120]{1,0:T(8,128)S(1)} %convert_add_fusion.6.refs_3_), custom_call_target="tpu_custom_call" | custom-call | flops 2569011200 | bytes 4014080 | tf_op jit(solution)/shard_map/grad_norm/pallas_call | solution.py:64
  113.8 3.3 %collective-permute-done.32 = f32[1,1120]{1,0:T(1,128)S(1)} collective-permute-done((f32[1,1120]{1,0:T(1,128)S(1)}, f32[1,1120]{1,0:T(1,128)S(1)}, u32[]{:S(2)}, u32[]{:S(2)}) %collective-permute-start.32) | collective-permute-done | bytes 4512 | tf_op jit(solution)/shard_map/ppermute | solution.py:471
  125.6 15.2 %d_w_key.1 = (bf16[896,1152]{1,0:T(8,128)(2,1)}, bf16[2,144,1120]{2,1,0:T(8,128)(2,1)S(1)}, bf16[2,136,1120]{2,1,0:T(8,128)(2,1)S(1)}, f32[2,144,1120]{2,1,0:T(8,128)S(1)}, f32[2,136,1120]{2,1,0:T(8,128)S(1)}) custom-call(s32[2]{0:T(128)S(1)} %pad_add_fusion.refs_0_, bf16[8,280,896]{2,1,0:T(8,128)(2,1)} %bitcast.88, ...), custom_call_target="tpu_custom_call" | custom-call | flops 4495769600 | bytes 15805440 | tf_op jit(solution)/shard_map/d_w_key/pallas_call | solution.py:64
  145.8 9.6 %attend.1 = (bf16[1120,896]{1,0:T(8,128)(2,1)}, bf16[1120,896]{1,0:T(8,128)(2,1)}) custom-call(bf16[1120,896]{1,0:T(8,128)(2,1)S(1)} %bitcast.92, bf16[1120,896]{1,0:T(8,128)(2,1)S(1)} %bitcast.95, f32[1,1120]{1,0:T(1,128)S(1)} %add.124.refs_2_, f32[32,1120]{1,0:T(8,128)S(1)} %convert_add_fusion.6.refs_3_, ...), custom_call_target="tpu_custom_call" | custom-call | flops 5651824640 | bytes 8028160 | tf_op jit(solution)/shard_map/attend/pallas_call | solution.py:64
  160.9 3.2 %collective-permute-done.41 = bf16[72,1120]{1,0:T(8,128)(2,1)S(1)} collective-permute-done((bf16[72,1120]{1,0:T(8,128)(2,1)S(1)}, bf16[72,1120]{1,0:T(8,128)(2,1)S(1)}, u32[]{:S(2)}, u32[]{:S(2)}) %collective-permute-start.41) | collective-permute-done | bytes 161312 | tf_op jit(solution)/shard_map/ppermute | solution.py:471
  169.1 2.8 %collective-permute-start.43 = (bf16[72,1120]{1,0:T(8,128)(2,1)S(1)}, bf16[72,1120]{1,0:T(8,128)(2,1)S(1)}, u32[]{:S(2)}, u32[]{:S(2)}) collective-permute-start(bf16[72,1120]{1,0:T(8,128)(2,1)S(1)} %get-tuple-element.162.refs_22_), channel_id=1, source_target_pairs={{0,4},{1,5},{2,6},{3,7},{4,0},{5,1},{6,2},{7,3},{8,12},{9,13},{10,... | collective-permute-start | bytes 483848 | tf_op jit(solution)/shard_map/ppermute | solution.py:471
  172.3 18.8 %d_tokens.1 = bf16[2240,896]{1,0:T(8,128)(2,1)} custom-call(s32[2]{0:T(128)} %copy-done.16, bf16[896,1152]{1,0:T(8,128)(2,1)} %get-tuple-element.150.refs_1_, bf16[896,1152]{1,0:T(8,128)(2,1)} %get-tuple-element.151.refs_2_, bf16[560,1120]{1,0:T(8,128)(2,1)} %refs_3_.1, bf16[288,1120]{1,0:T(8,128)(2,1)} %copy-done.12, bf16[288,1120]{1,0:T(8,128)(2,1)} %copy-done.24, ...), custom_call_target="tpu_custom_call" | custom-call | flops 8991539200 | bytes 18063360 | tf_op jit(solution)/shard_map/d_tokens/pallas_call | solution.py:64
  191.6 3.7 %collective-permute-start.47 = (bf16[72,1120]{1,0:T(8,128)(2,1)S(1)}, bf16[72,1120]{1,0:T(8,128)(2,1)S(1)}, u32[]{:S(2)}, u32[]{:S(2)}) collective-permute-start(bf16[72,1120]{1,0:T(8,128)(2,1)S(1)} %fusion.8), channel_id=1, source_target_pairs={{0,4},{1,5},{2,6},{3,7},{4,0},{5,1},{6,2},{7,3},{8,12},{9,13},{10,... | collective-permute-start | bytes 483848 | tf_op jit(solution)/shard_map/ppermute | solution.py:471
  196.9 3.9 %collective-permute-done.46 = bf16[72,1120]{1,0:T(8,128)(2,1)S(1)} collective-permute-done((bf16[72,1120]{1,0:T(8,128)(2,1)S(1)}, bf16[72,1120]{1,0:T(8,128)(2,1)S(1)}, u32[]{:S(2)}, u32[]{:S(2)}) %collective-permute-start.46) | collective-permute-done | bytes 161312 | tf_op jit(solution)/shard_map/ppermute | solution.py:471
  200.8 3.3 %collective-permute-done.48 = bf16[72,1120]{1,0:T(8,128)(2,1)S(1)} collective-permute-done((bf16[72,1120]{1,0:T(8,128)(2,1)S(1)}, bf16[72,1120]{1,0:T(8,128)(2,1)S(1)}, u32[]{:S(2)}, u32[]{:S(2)}) %collective-permute-start.48) | collective-permute-done | bytes 161312 | tf_op jit(solution)/shard_map/ppermute | solution.py:471
  204.4 2.8 %collective-permute-done.50 = bf16[144,1120]{1,0:T(8,128)(2,1)S(1)} collective-permute-done((bf16[144,1120]{1,0:T(8,128)(2,1)S(1)}, bf16[144,1120]{1,0:T(8,128)(2,1)S(1)}, u32[]{:S(2)}, u32[]{:S(2)}) %collective-permute-start.50) | collective-permute-done | bytes 322592 | tf_op jit(solution)/shard_map/ppermute | solution.py:471
  (211 shorter events, 70.4 us)
Async XLA Ops:
  2.0 17.9 %collective-permute-start = (bf16[288,1120]{1,0:T(8,128)(2,1)S(1)}, bf16[288,1120]{1,0:T(8,128)(2,1)S(1)}, u32[]{:S(2)}, u32[]{:S(2)}) collective-permute-start(bf16[288,1120]{1,0:T(8,128)(2,1)S(1)} %slice_select_fusion.1), channel_id=1, source_target_pairs={{0,8},{8,0},{16,24},{24,16},{1,9},{9,1},{17,25},{25,17},{2,10},{10... | collective-permute-start | bytes 1935368 | tf_op jit(solution)/shard_map/ppermute | solution.py:471
  5.0 16.4 %collective-permute-start.1 = (bf16[288,1120]{1,0:T(8,128)(2,1)S(1)}, bf16[288,1120]{1,0:T(8,128)(2,1)S(1)}, u32[]{:S(2)}, u32[]{:S(2)}) collective-permute-start(bf16[288,1120]{1,0:T(8,128)(2,1)S(1)} %slice_select_fusion.1), channel_id=1, source_target_pairs={{0,16},{8,24},{16,0},{24,8},{1,17},{9,25},{17,1},{25,9},{2,18},{10... | collective-permute-start | bytes 1935368 | tf_op jit(solution)/shard_map/ppermute | solution.py:471
  21.4 11.9 %collective-permute-start.6 = (bf16[4,280,896]{2,1,0:T(8,128)(2,1)}, bf16[4,280,896]{2,1,0:T(8,128)(2,1)}, u32[]{:S(2)}, u32[]{:S(2)}) collective-permute-start(bf16[4,280,896]{2,1,0:T(8,128)(2,1)} %get-tuple-element.88), channel_id=1, source_target_pairs={{0,1},{1,0},{2,3},{3,2},{4,5},{5,4},{6,7},{7,6},{8,9},{9,8},{10,11... | collective-permute-start | bytes 6021128 | tf_op jit(solution)/shard_map/ppermute | solution.py:471
  22.0 11.3 %collective-permute-start.2 = (bf16[144,1120]{1,0:T(8,128)(2,1)S(1)}, bf16[144,1120]{1,0:T(8,128)(2,1)S(1)}, u32[]{:S(2)}, u32[]{:S(2)}) collective-permute-start(bf16[144,1120]{1,0:T(8,128)(2,1)S(1)} %slice.60), channel_id=1, source_target_pairs={{0,8},{8,0},{16,24},{24,16},{1,9},{9,1},{17,25},{25,17},{2,10},{10... | collective-permute-start | bytes 967688 | tf_op jit(solution)/shard_map/ppermute | solution.py:471
  22.5 10.8 %collective-permute-start.3 = (bf16[144,1120]{1,0:T(8,128)(2,1)S(1)}, bf16[144,1120]{1,0:T(8,128)(2,1)S(1)}, u32[]{:S(2)}, u32[]{:S(2)}) collective-permute-start(bf16[144,1120]{1,0:T(8,128)(2,1)S(1)} %slice.61), channel_id=1, source_target_pairs={{0,16},{8,24},{16,0},{24,8},{1,17},{9,25},{17,1},{25,9},{2,18},{10... | collective-permute-start | bytes 967688 | tf_op jit(solution)/shard_map/ppermute | solution.py:471
  39.9 35.0 %collective-permute-start.20 = (bf16[896,1152]{1,0:T(8,128)(2,1)S(1)}, bf16[896,1152]{1,0:T(8,128)(2,1)}, u32[]{:S(2)}, u32[]{:S(2)}) collective-permute-start(bf16[896,1152]{1,0:T(8,128)(2,1)S(1)} %get-tuple-element.96.refs_3_), channel_id=1, source_target_pairs={{0,1},{1,0},{2,3},{3,2},{4,5},{5,4},{6,7},{7,6},{8,9},{9,8},{10,11... | collective-permute-start | bytes 6193160 | tf_op jit(solution)/shard_map/ppermute | solution.py:471
  40.3 17.0 %collective-permute-start.12 = (bf16[288,1120]{1,0:T(8,128)(2,1)S(1)}, bf16[288,1120]{1,0:T(8,128)(2,1)S(1)}, u32[]{:S(2)}, u32[]{:S(2)}) collective-permute-start(bf16[288,1120]{1,0:T(8,128)(2,1)S(1)} %slice_select_fusion), channel_id=1, source_target_pairs={{0,8},{8,0},{16,24},{24,16},{1,9},{9,1},{17,25},{25,17},{2,10},{10... | collective-permute-start | bytes 1935368 | tf_op jit(solution)/shard_map/ppermute | solution.py:471
  40.7 16.9 %collective-permute-start.13 = (bf16[288,1120]{1,0:T(8,128)(2,1)S(1)}, bf16[288,1120]{1,0:T(8,128)(2,1)S(1)}, u32[]{:S(2)}, u32[]{:S(2)}) collective-permute-start(bf16[288,1120]{1,0:T(8,128)(2,1)S(1)} %slice_select_fusion), channel_id=1, source_target_pairs={{0,16},{8,24},{16,0},{24,8},{1,17},{9,25},{17,1},{25,9},{2,18},{10... | collective-permute-start | bytes 1935368 | tf_op jit(solution)/shard_map/ppermute | solution.py:471
  62.5 12.1 %collective-permute-start.18 = (bf16[144,1120]{1,0:T(8,128)(2,1)S(1)}, bf16[144,1120]{1,0:T(8,128)(2,1)S(1)}, u32[]{:S(2)}, u32[]{:S(2)}) collective-permute-start(bf16[144,1120]{1,0:T(8,128)(2,1)S(1)} %slice.64), channel_id=1, source_target_pairs={{0,8},{8,0},{16,24},{24,16},{1,9},{9,1},{17,25},{25,17},{2,10},{10... | collective-permute-start | bytes 967688 | tf_op jit(solution)/shard_map/ppermute | solution.py:471
  83.8 19.5 %collective-permute-start.28 = (bf16[896,1152]{1,0:T(8,128)(2,1)S(1)}, bf16[896,1152]{1,0:T(8,128)(2,1)S(1)}, u32[]{:S(2)}, u32[]{:S(2)}) collective-permute-start(bf16[896,1152]{1,0:T(8,128)(2,1)S(1)} %get-tuple-element.113.refs_4_), channel_id=1, source_target_pairs={{0,1},{1,0},{2,3},{3,2},{4,5},{5,4},{6,7},{7,6},{8,9},{9,8},{10,11... | collective-permute-start | bytes 6193160 | tf_op jit(solution)/shard_map/ppermute | solution.py:471
  84.0 19.3 %collective-permute-start.25 = (bf16[32,1120]{1,0:T(8,128)(2,1)S(1)}, bf16[32,1120]{1,0:T(8,128)(2,1)S(1)}, u32[]{:S(2)}, u32[]{:S(2)}) collective-permute-start(bf16[32,1120]{1,0:T(8,128)(2,1)S(1)} %convert_element_type.121), channel_id=1, source_target_pairs={{0,2},{1,3},{2,0},{3,1},{4,6},{5,7},{6,4},{7,5},{8,10},{9,11},{10,... | collective-permute-start | bytes 215048 | tf_op jit(solution)/shard_map/ppermute | solution.py:471
  85.4 17.9 %collective-permute-start.26 = (bf16[32,1120]{1,0:T(8,128)(2,1)S(1)}, bf16[32,1120]{1,0:T(8,128)(2,1)S(1)}, u32[]{:S(2)}, u32[]{:S(2)}) collective-permute-start(bf16[32,1120]{1,0:T(8,128)(2,1)S(1)} %convert_element_type.121), channel_id=1, source_target_pairs={{0,4},{1,5},{2,6},{3,7},{4,0},{5,1},{6,2},{7,3},{8,12},{9,13},{10,... | collective-permute-start | bytes 215048 | tf_op jit(solution)/shard_map/ppermute | solution.py:471
  88.1 15.2 %collective-permute-start.27 = (bf16[32,1120]{1,0:T(8,128)(2,1)S(1)}, bf16[32,1120]{1,0:T(8,128)(2,1)S(1)}, u32[]{:S(2)}, u32[]{:S(2)}) collective-permute-start(bf16[32,1120]{1,0:T(8,128)(2,1)S(1)} %convert_element_type.121), channel_id=1, source_target_pairs={{0,6},{1,7},{2,4},{3,5},{4,2},{5,3},{6,0},{7,1},{8,14},{9,15},{10,... | collective-permute-start | bytes 215048 | tf_op jit(solution)/shard_map/ppermute | solution.py:471
  103.3 18.3 %collective-permute-start.29 = (bf16[2,144,1120]{2,1,0:T(8,128)(2,1)}, bf16[2,144,1120]{2,1,0:T(8,128)(2,1)}, u32[]{:S(2)}, u32[]{:S(2)}) collective-permute-start(bf16[2,144,1120]{2,1,0:T(8,128)(2,1)} %get-tuple-element.123), channel_id=1, source_target_pairs={{0,8},{8,0},{16,24},{24,16},{1,9},{9,1},{17,25},{25,17},{2,10},{10... | collective-permute-start | bytes 1935368 | tf_op jit(solution)/shard_map/ppermute | solution.py:471
  104.8 16.7 %collective-permute-start.30 = (bf16[2,136,1120]{2,1,0:T(8,128)(2,1)}, bf16[2,136,1120]{2,1,0:T(8,128)(2,1)}, u32[]{:S(2)}, u32[]{:S(2)}) collective-permute-start(bf16[2,136,1120]{2,1,0:T(8,128)(2,1)} %get-tuple-element.124), channel_id=1, source_target_pairs={{0,16},{8,24},{16,0},{24,8},{1,17},{9,25},{17,1},{25,9},{2,18},{10... | collective-permute-start | bytes 1827848 | tf_op jit(solution)/shard_map/ppermute | solution.py:471
  122.9 20.7 %collective-permute-start.36 = (bf16[144,1120]{1,0:T(8,128)(2,1)S(1)}, bf16[144,1120]{1,0:T(8,128)(2,1)S(1)}, u32[]{:S(2)}, u32[]{:S(2)}) collective-permute-start(bf16[144,1120]{1,0:T(8,128)(2,1)S(1)} %fusion.3.refs_9_), channel_id=1, source_target_pairs={{0,16},{8,24},{16,0},{24,8},{1,17},{9,25},{17,1},{25,9},{2,18},{10... | collective-permute-start | bytes 967688 | tf_op jit(solution)/shard_map/ppermute | solution.py:471
  124.7 18.8 %collective-permute-start.37 = (bf16[136,1120]{1,0:T(8,128)(2,1)S(1)}, bf16[136,1120]{1,0:T(8,128)(2,1)S(1)}, u32[]{:S(2)}, u32[]{:S(2)}) collective-permute-start(bf16[136,1120]{1,0:T(8,128)(2,1)S(1)} %fusion.11.refs_10_), channel_id=1, source_target_pairs={{0,8},{8,0},{16,24},{24,16},{1,9},{9,1},{17,25},{25,17},{2,10},{10... | collective-permute-start | bytes 913928 | tf_op jit(solution)/shard_map/ppermute | solution.py:471
  140.8 14.8 %collective-permute-start.34 = (bf16[2,144,1120]{2,1,0:T(8,128)(2,1)S(1)}, bf16[2,144,1120]{2,1,0:T(8,128)(2,1)S(1)}, u32[]{:S(2)}, u32[]{:S(2)}) collective-permute-start(bf16[2,144,1120]{2,1,0:T(8,128)(2,1)S(1)} %get-tuple-element.135.refs_4_), channel_id=1, source_target_pairs={{0,8},{8,0},{16,24},{24,16},{1,9},{9,1},{17,25},{25,17},{2,10},{10... | collective-permute-start | bytes 1935368 | tf_op jit(solution)/shard_map/ppermute | solution.py:471
  142.0 13.5 %collective-permute-start.35 = (bf16[2,136,1120]{2,1,0:T(8,128)(2,1)S(1)}, bf16[2,136,1120]{2,1,0:T(8,128)(2,1)S(1)}, u32[]{:S(2)}, u32[]{:S(2)}) collective-permute-start(bf16[2,136,1120]{2,1,0:T(8,128)(2,1)S(1)} %get-tuple-element.136.refs_5_), channel_id=1, source_target_pairs={{0,16},{8,24},{16,0},{24,8},{1,17},{9,25},{17,1},{25,9},{2,18},{10... | collective-permute-start | bytes 1827848 | tf_op jit(solution)/shard_map/ppermute | solution.py:471
  143.9 11.8 %collective-permute-start.38 = (bf16[144,1120]{1,0:T(8,128)(2,1)S(1)}, bf16[144,1120]{1,0:T(8,128)(2,1)S(1)}, u32[]{:S(2)}, u32[]{:S(2)}) collective-permute-start(bf16[144,1120]{1,0:T(8,128)(2,1)S(1)} %fusion.2), channel_id=1, source_target_pairs={{0,2},{1,3},{2,0},{3,1},{4,6},{5,7},{6,4},{7,5},{8,10},{9,11},{10,... | collective-permute-start | bytes 967688 | tf_op jit(solution)/shard_map/ppermute | solution.py:471
  166.5 24.6 %collective-permute-start.45 = (bf16[72,1120]{1,0:T(8,128)(2,1)S(1)}, bf16[72,1120]{1,0:T(8,128)(2,1)S(1)}, u32[]{:S(2)}, u32[]{:S(2)}) collective-permute-start(bf16[72,1120]{1,0:T(8,128)(2,1)S(1)} %fusion.10.refs_24_), channel_id=1, source_target_pairs={{0,4},{1,5},{2,6},{3,7},{4,0},{5,1},{6,2},{7,3},{8,12},{9,13},{10,... | collective-permute-start | bytes 483848 | tf_op jit(solution)/shard_map/ppermute | solution.py:471
  167.9 23.2 %collective-permute-start.42 = (bf16[72,1120]{1,0:T(8,128)(2,1)S(1)}, bf16[72,1120]{1,0:T(8,128)(2,1)S(1)}, u32[]{:S(2)}, u32[]{:S(2)}) collective-permute-start(bf16[72,1120]{1,0:T(8,128)(2,1)S(1)} %get-tuple-element.163.refs_21_), channel_id=1, source_target_pairs={{0,2},{1,3},{2,0},{3,1},{4,6},{5,7},{6,4},{7,5},{8,10},{9,11},{10,... | collective-permute-start | bytes 483848 | tf_op jit(solution)/shard_map/ppermute | solution.py:471
  169.1 22.0 %collective-permute-start.43 = (bf16[72,1120]{1,0:T(8,128)(2,1)S(1)}, bf16[72,1120]{1,0:T(8,128)(2,1)S(1)}, u32[]{:S(2)}, u32[]{:S(2)}) collective-permute-start(bf16[72,1120]{1,0:T(8,128)(2,1)S(1)} %get-tuple-element.162.refs_22_), channel_id=1, source_target_pairs={{0,4},{1,5},{2,6},{3,7},{4,0},{5,1},{6,2},{7,3},{8,12},{9,13},{10,... | collective-permute-start | bytes 483848 | tf_op jit(solution)/shard_map/ppermute | solution.py:471
  171.9 19.2 %collective-permute-start.44 = (bf16[72,1120]{1,0:T(8,128)(2,1)S(1)}, bf16[72,1120]{1,0:T(8,128)(2,1)S(1)}, u32[]{:S(2)}, u32[]{:S(2)}) collective-permute-start(bf16[72,1120]{1,0:T(8,128)(2,1)S(1)} %get-tuple-element.161.refs_23_), channel_id=1, source_target_pairs={{0,6},{1,7},{2,4},{3,5},{4,2},{5,3},{6,0},{7,1},{8,14},{9,15},{10,... | collective-permute-start | bytes 483848 | tf_op jit(solution)/shard_map/ppermute | solution.py:471
  (61 other events, 560.3 us)
